TPU v7x, 32 devices: a whole 2x2x4 slice. The times are simulated.
32 devices in a mesh: dp: 16 (over z, x, core), tensor: 2 (over y).
Axes of the slice: x: 2, y: 2, z: 4, core: 2. Of those that a mesh axis runs over, the one named last changes fastest.
Arguments:
- hidden_in: bfloat16 [32768, 1024], P(('dp', 'tensor')), may hold values from -6 to 6
- lengths: int32 [16, 4], P('dp'), may hold values from 1 to 1536, 2048 in all within a row
- cotangent: bfloat16 [32768, 1024], P(('dp', 'tensor')), may hold values from -6 to 6
- query_weight: bfloat16 [1024, 512], P('dp', 'tensor'), may hold values from -0.1875 to 0.1875
- key_weight: bfloat16 [1024, 512], P('dp', 'tensor'), may hold values from -0.1875 to 0.1875
- value_weight: bfloat16 [1024, 1024], P('dp', 'tensor'), may hold values from -0.1875 to 0.1875
- outgate_weight: bfloat16 [1024, 1024], P('dp', 'tensor'), may hold values from -0.1875 to 0.1875
- output_weight: bfloat16 [1024, 1024], P('tensor', 'dp'), may hold values from -0.375 to 0.375
- gate_weight: bfloat16 [1024, 2816], P('dp', 'tensor'), may hold values from -0.1875 to 0.1875
- up_weight: bfloat16 [1024, 2816], P('dp', 'tensor'), may hold values from -0.1875 to 0.1875
- down_weight: bfloat16 [2816, 1024], P('tensor', 'dp'), may hold values from -0.109375 to 0.109375
- mixer_gain: float32 [1024], replicated, may hold values from 0.5 to 1.5
- feed_gain: float32 [1024], replicated, may hold values from 0.5 to 1.5
- low_first: float32 [1024, 16], replicated, may hold values from -0.1875 to 0.1875
- low_second: float32 [16, 512], replicated, may hold values from -1.5 to 1.5
- decay_bias: float32 [512], replicated, may hold values from 0 to 7
- head_gain: float32 [256], replicated, may hold values from 0.5 to 1.5
Outputs:
- block_out: bfloat16 [32768, 1024], P(('dp', 'tensor'))
- input_grad: bfloat16 [32768, 1024], P(('dp', 'tensor'))
- query_grad: float32 [1024, 512], P('dp', 'tensor')
- key_grad: float32 [1024, 512], P('dp', 'tensor')
- value_grad: float32 [1024, 1024], P('dp', 'tensor')
- outgate_grad: float32 [1024, 1024], P('dp', 'tensor')
- output_grad: float32 [1024, 1024], P('tensor', 'dp')
- gate_grad: float32 [1024, 2816], P('dp', 'tensor')
- up_grad: float32 [1024, 2816], P('dp', 'tensor')
- down_grad: float32 [2816, 1024], P('tensor', 'dp')
- mixer_gain_grad: float32 [1024], replicated
- feed_gain_grad: float32 [1024], replicated
- low_first_grad: float32 [1024, 16], replicated
- low_second_grad: float32 [16, 512], replicated
- decay_bias_grad: float32 [512], replicated
- head_gain_grad: float32 [256], replicated
Inputs may be any that keep to these rules, and one draw needn't show every extreme that they name: `lengths`: each row sums to 2048, and its largest entry is exactly 1536.
All inputs are finite; a program needn't handle non-finite values.
Results may differ from a plain program's by a relative error of at most 0.02.
Values may be sent and summed in bfloat16 or wider, within the bound.
No kernel may reach another device: no remote copies, remote signals or barrier semaphores. Data moves between devices by JAX's collectives and lax.ppermute only.
A program may use at most 320 MiB of HBM per device.

v0:
```python
import jax
import jax.numpy as jnp
from jax import lax
from jax.sharding import PartitionSpec as P

KEY = 128
VAL = 256
SPAN = 64


HIGH_ACCURACY = lax.Precision.HIGHEST


def product(left, right):
    return jnp.dot(left, right, preferred_element_type=jnp.float32)


def inner_rows(left, right):
    return lax.dot_general(
        left, right, (((0,), (0,)), ((), ())), preferred_element_type=jnp.float32
    )


def times_trans(left, right):
    return lax.dot_general(
        left, right, (((1,), (1,)), ((), ())), preferred_element_type=jnp.float32
    )


def rms_scale(values, gains, eps):
    return values * lax.rsqrt(jnp.mean(values * values, axis=-1, keepdims=True) + eps) * gains


def segment_ids(lengths_row, total):
    starts = jnp.cumsum(lengths_row) - lengths_row
    places = jnp.arange(total, dtype=jnp.int32)
    return jnp.sum((places[:, None] >= starts[None, 1:]).astype(jnp.int32), axis=1)


def linear_core(queries, keys, values, decays, segment):
    total = queries.shape[0]
    heads = queries.shape[1] // KEY
    blocks = total // SPAN

    def split(array, width):
        return array.reshape(blocks, SPAN, heads, width).transpose(0, 2, 1, 3)

    lower = jnp.arange(SPAN)[:, None] >= jnp.arange(SPAN)[None, :]

    def advance(carry, item):
        state_matrix, before = carry
        query_block, key_block, block_values, decay_block, seg_block = item
        cumul = jnp.cumsum(decay_block, axis=1)
        final_state = cumul[:, -1:, :]
        query_decayed = query_block * jnp.exp(cumul)
        key_dec = key_block * jnp.exp(-cumul)
        mask = (lower & (seg_block[:, None] == seg_block[None, :])).astype(jnp.float32)
        scores = (
            jnp.einsum("hik,hjk->hij", query_decayed, key_dec, precision=HIGH_ACCURACY) * mask[None]
        )
        running_state = (seg_block == before).astype(jnp.float32)[None, :, None]
        cross_block_term = (
            jnp.einsum("wcb,wba->wca", query_decayed, state_matrix, precision=HIGH_ACCURACY)
            * running_state
        )
        outputs = cross_block_term + jnp.einsum(
            "hij,hjv->hiv", scores, block_values, precision=HIGH_ACCURACY
        )
        tail = (seg_block == seg_block[-1]).astype(jnp.float32)[None, :, None]
        key_tail_decay = key_block * jnp.exp(final_state - cumul) * tail
        retain_factor = (seg_block[-1] == before).astype(jnp.float32)
        state_matrix = state_matrix * (
            jnp.exp(final_state)[:, 0, :, None] * retain_factor
        ) + jnp.einsum("zco,zcr->zor", key_tail_decay, block_values, precision=HIGH_ACCURACY)
        return ((state_matrix, seg_block[-1]), outputs)

    start = (jnp.zeros((heads, KEY, VAL), jnp.float32), jnp.array(-1, dtype=jnp.int32))
    items = (
        split(queries, KEY),
        split(keys, KEY),
        split(values, VAL),
        split(decays, KEY),
        segment.reshape(blocks, SPAN),
    )
    unused, outs = lax.scan(advance, start, items)
    return outs.transpose(0, 2, 1, 3).reshape(total, heads * VAL)


def post_gate(core, gains, outgate):
    shaped = core.reshape(core.shape[0], -1, VAL)
    normed = rms_scale(shaped, gains, 1.0).reshape(core.shape)
    return normed * jax.nn.silu(outgate)


def gate_logits(lowrank, columns, bias_part):
    return jax.nn.log_sigmoid(jnp.dot(lowrank, columns, precision=HIGH_ACCURACY) + bias_part) / 16.0


def swiglu(gate_pre, up_pre):
    return jax.nn.silu(gate_pre) * up_pre


def norm_small(values, gains):
    return rms_scale(values, gains, 1e-06)


def local(
    hidden_in,
    lengths,
    cotangent,
    query_weight,
    key_weight,
    value_weight,
    outgate_weight,
    output_weight,
    gate_weight,
    up_weight,
    down_weight,
    mixer_gain,
    feed_gain,
    low_first,
    low_second,
    decay_bias,
    head_gain,
):
    parts = lax.axis_size("tensor")
    place = lax.axis_index("tensor")
    total = hidden_in.shape[0] * parts
    segment = segment_ids(lengths[0], total)
    scale = KEY ** (-0.5)
    full_query, full_key, full_value, full_outgate, full_gate, full_up = (
        lax.all_gather(query_weight, "dp", axis=0, tiled=True),
        lax.all_gather(key_weight, "dp", axis=0, tiled=True),
        lax.all_gather(value_weight, "dp", axis=0, tiled=True),
        lax.all_gather(outgate_weight, "dp", axis=0, tiled=True),
        lax.all_gather(gate_weight, "dp", axis=0, tiled=True),
        lax.all_gather(up_weight, "dp", axis=0, tiled=True),
    )
    full_output, full_down = (
        lax.all_gather(output_weight, "dp", axis=1, tiled=True),
        lax.all_gather(down_weight, "dp", axis=1, tiled=True),
    )
    resid = hidden_in.astype(jnp.float32)
    normed_a, pull_first = jax.vjp(norm_small, resid, mixer_gain)
    rows_a = lax.all_gather(normed_a.astype(jnp.bfloat16), "tensor", axis=0, tiled=True)
    queries = (product(rows_a, full_query) * scale).astype(jnp.bfloat16)
    keys_low = product(rows_a, full_key).astype(jnp.bfloat16)
    values_low = product(rows_a, full_value).astype(jnp.bfloat16)
    outgate = product(rows_a, full_outgate)
    width = full_query.shape[1]
    columns = lax.dynamic_slice_in_dim(low_second, place * width, width, 1)
    bias_part = lax.dynamic_slice_in_dim(decay_bias, place * width, width, 0)
    rows_wide = rows_a.astype(jnp.float32)
    lowrank = jnp.dot(rows_wide, low_first, precision=HIGH_ACCURACY)
    decays, pull_gate = jax.vjp(gate_logits, lowrank, columns, bias_part)

    def mixer(query_in, key_in, value_in, decay_in):
        return linear_core(query_in, key_in, value_in, decay_in, segment)

    core, pull_core = jax.vjp(
        mixer,
        queries.astype(jnp.float32),
        keys_low.astype(jnp.float32),
        values_low.astype(jnp.float32),
        decays,
    )
    gated, pull_post = jax.vjp(post_gate, core, head_gain, outgate)
    gated_low = gated.astype(jnp.bfloat16)
    mixed = lax.psum_scatter(
        product(gated_low, full_output), "tensor", scatter_dimension=0, tiled=True
    )
    middle = resid + mixed
    normed_b, pull_second = jax.vjp(norm_small, middle, feed_gain)
    rows_b = lax.all_gather(normed_b.astype(jnp.bfloat16), "tensor", axis=0, tiled=True)
    gate_pre = product(rows_b, full_gate)
    up_pre = product(rows_b, full_up)
    activ, pull_act = jax.vjp(swiglu, gate_pre, up_pre)
    activ_low = activ.astype(jnp.bfloat16)
    feed_out = lax.psum_scatter(
        product(activ_low, full_down).astype(jnp.bfloat16),
        "tensor",
        scatter_dimension=0,
        tiled=True,
    ).astype(jnp.float32)
    block_out = (middle + feed_out).astype(jnp.bfloat16)
    back_feed = lax.all_gather(cotangent, "tensor", axis=0, tiled=True)
    down_trans = inner_rows(back_feed, activ_low)
    act_grad = times_trans(back_feed, full_down)
    gate_back, up_back = pull_act(act_grad)
    gate_low = gate_back.astype(jnp.bfloat16)
    up_low = up_back.astype(jnp.bfloat16)
    gate_grad = inner_rows(rows_b, gate_low)
    up_grad = inner_rows(rows_b, up_low)
    feed_in_grad = times_trans(gate_low, full_gate) + times_trans(up_low, full_up)
    feed_back = lax.psum_scatter(
        feed_in_grad.astype(jnp.bfloat16), "tensor", scatter_dimension=0, tiled=True
    ).astype(jnp.float32)
    middle_norm_grad, feed_gain_grad = pull_second(feed_back)
    middle_grad = cotangent.astype(jnp.float32) + middle_norm_grad
    back_mix = lax.all_gather(middle_grad.astype(jnp.bfloat16), "tensor", axis=0, tiled=True)
    output_trans = inner_rows(back_mix, gated_low)
    gated_grad = times_trans(back_mix, full_output)
    core_grad, head_gain_grad, outgate_back = pull_post(gated_grad)
    outgate_low = outgate_back.astype(jnp.bfloat16)
    query_back, key_back, value_back, decay_back = pull_core(core_grad)
    query_low = query_back.astype(jnp.bfloat16)
    key_low = key_back.astype(jnp.bfloat16)
    value_low = value_back.astype(jnp.bfloat16)
    lowrank_grad, columns_grad, bias_grad = pull_gate(decay_back)
    query_grad = inner_rows(rows_a, query_low) * scale
    key_grad = inner_rows(rows_a, key_low)
    value_grad = inner_rows(rows_a, value_low)
    outgate_grad = inner_rows(rows_a, outgate_low)
    low_first_grad = lax.dot_general(
        rows_wide,
        lowrank_grad,
        (((0,), (0,)), ((), ())),
        precision=HIGH_ACCURACY,
        preferred_element_type=jnp.float32,
    )
    mixer_in_grad = (
        times_trans(query_low, full_query) * scale
        + times_trans(key_low, full_key)
        + times_trans(value_low, full_value)
        + times_trans(outgate_low, full_outgate)
    )
    mixer_in_grad = mixer_in_grad + lax.dot_general(
        lowrank_grad,
        low_first,
        (((1,), (1,)), ((), ())),
        precision=HIGH_ACCURACY,
        preferred_element_type=jnp.float32,
    )
    mix_back = lax.psum_scatter(
        mixer_in_grad.astype(jnp.bfloat16), "tensor", scatter_dimension=0, tiled=True
    ).astype(jnp.float32)
    resid_norm_grad, mixer_gain_grad = pull_first(mix_back)
    input_grad = (middle_grad + resid_norm_grad).astype(jnp.bfloat16)
    low_second_grad = lax.dynamic_update_slice_in_dim(
        jnp.zeros_like(low_second), columns_grad, place * width, 1
    )
    decay_bias_grad = lax.dynamic_update_slice_in_dim(
        jnp.zeros_like(decay_bias), bias_grad, place * width, 0
    )
    owned = (
        lax.psum_scatter(query_grad, "dp", scatter_dimension=0, tiled=True),
        lax.psum_scatter(key_grad, "dp", scatter_dimension=0, tiled=True),
        lax.psum_scatter(value_grad, "dp", scatter_dimension=0, tiled=True),
        lax.psum_scatter(outgate_grad, "dp", scatter_dimension=0, tiled=True),
        lax.psum_scatter(output_trans, "dp", scatter_dimension=0, tiled=True),
        lax.psum_scatter(gate_grad, "dp", scatter_dimension=0, tiled=True),
        lax.psum_scatter(up_grad, "dp", scatter_dimension=0, tiled=True),
        lax.psum_scatter(down_trans, "dp", scatter_dimension=0, tiled=True),
    )
    (
        owned_query,
        owned_key,
        owned_value,
        owned_outgate,
        owned_output,
        owned_gate,
        owned_up,
        owned_down,
    ) = owned
    small = lax.psum(
        (
            mixer_gain_grad,
            feed_gain_grad,
            low_first_grad,
            low_second_grad,
            decay_bias_grad,
            head_gain_grad,
        ),
        ("dp", "tensor"),
    )
    return (
        block_out,
        input_grad,
        owned_query,
        owned_key,
        owned_value,
        owned_outgate,
        owned_output.T,
        owned_gate,
        owned_up,
        owned_down.T,
        small[0],
        small[1],
        small[2],
        small[3],
        small[4],
        small[5],
    )


def solution(mesh):
    in_specs = (
        P(("dp", "tensor"), None),
        P("dp", None),
        P(("dp", "tensor"), None),
        P("dp", "tensor"),
        P("dp", "tensor"),
        P("dp", "tensor"),
        P("dp", "tensor"),
        P("tensor", "dp"),
        P("dp", "tensor"),
        P("dp", "tensor"),
        P("tensor", "dp"),
        P(),
        P(),
        P(),
        P(),
        P(),
        P(),
    )
    out_specs = (
        P(("dp", "tensor"), None),
        P(("dp", "tensor"), None),
        P("dp", "tensor"),
        P("dp", "tensor"),
        P("dp", "tensor"),
        P("dp", "tensor"),
        P("tensor", "dp"),
        P("dp", "tensor"),
        P("dp", "tensor"),
        P("tensor", "dp"),
        P(),
        P(),
        P(),
        P(),
        P(),
        P(),
    )
    return jax.shard_map(local, mesh=mesh, in_specs=in_specs, out_specs=out_specs, check_vma=False)
```

profile of v0, /device:TPU:0, one launch (start us, length us, event | category | flops | bytes accessed | tf_op | source)
XLA Modules:
  0.0 2704.5 jit_solution(168607135208262997)
XLA Ops:
  16.8 24.6 all_gather.39
  41.3 18.9 all_gather.37
  142.4 501.2 %while.70 = (s32[]{:T(128)}, f32[2,128,256]{2,1,0:T(8,128)S(1)}, s32[]{:T(128)}, f32[32,2,64,256]{3,2,1,0:T(8,128)}, f32[32,2,64,128]{3,2,1,0:T(8,128)}, /*index...) while((s32[]{:T(128)}, f32[2,128,256]{2,1,0:T(8,128)S(1)}, ...), condition=%wide.region_5.6_spmd.clone.clone.clone, body=%wide.region_3.5_spmd.clone.clone.sunk.clone | while | flops 140092160 | bytes 3576386 | solution.py:85
  679.9 97.7 %reduce-scatter.15.cloned.1.call-done = f32[1024,1024]{1,0:T(8,128)} async-done(((f32[2048,1024]{1,0:T(8,128)}), f32[1024,1024]{1,0:T(8,128)}) %reduce-scatter.15.cloned.1.call-update) | async-done | bytes 4194320 | tf_op jit(solution)/shard_map/reduce_scatter | solution.py:169
  786.3 38.1 %all-gather.21.cloned.1.call-done = bf16[1024,1408]{1,0:T(8,128)(2,1)} async-done(((bf16[64,1408]{1,0:T(8,128)(2,1)}), bf16[1024,1408]{1,0:T(8,128)(2,1)}) %all-gather.21.cloned.1.call-update) | async-done | bytes 2883600 | tf_op jit(solution)/shard_map/all_gather | solution.py:136
  824.4 56.7 %all-gather.19.cloned.1.call-done = bf16[2048,1024]{1,0:T(8,128)(2,1)} async-done(((bf16[1024,1024]{1,0:T(8,128)(2,1)}), bf16[2048,1024]{1,0:T(8,128)(2,1)}) %all-gather.19.cloned.1.call-update) | async-done | bytes 4194320 | tf_op jit(solution)/shard_map/all_gather | solution.py:174
  892.9 35.2 %all-gather.23.cloned.1.call-done = bf16[1024,1408]{1,0:T(8,128)(2,1)} async-done(((bf16[64,1408]{1,0:T(8,128)(2,1)}), bf16[1024,1408]{1,0:T(8,128)(2,1)}) %all-gather.23.cloned.1.call-update) | async-done | bytes 2883600 | tf_op jit(solution)/shard_map/all_gather | solution.py:137
  939.9 44.9 %all-gather.27.cloned.1.call-done = bf16[2048,1024]{1,0:T(8,128)(2,1)} async-done(((bf16[1024,1024]{1,0:T(8,128)(2,1)}), bf16[2048,1024]{1,0:T(8,128)(2,1)}) %all-gather.27.cloned.1.call-update) | async-done | bytes 4194320 | tf_op jit(solution)/shard_map/all_gather | solution.py:186
  984.8 46.8 %all-gather.25.cloned.1.call-done = bf16[1408,1024]{0,1:T(8,128)(2,1)} async-done(((bf16[1408,64]{0,1:T(8,128)(2,1)}), bf16[1408,1024]{0,1:T(8,128)(2,1)}) %all-gather.25.cloned.1.call-update) | async-done | bytes 2883600 | tf_op jit(solution)/shard_map/all_gather | solution.py:141
  1031.6 21.2 multiply_convert_fusion
  1070.5 52.7 %reduce-scatter.19.cloned.1.call-done = bf16[1024,1024]{1,0:T(8,128)(2,1)} async-done(((bf16[2048,1024]{1,0:T(8,128)(2,1)}), bf16[1024,1024]{1,0:T(8,128)(2,1)}) %reduce-scatter.19.cloned.1.call-update) | async-done | bytes 2097168 | tf_op jit(solution)/shard_map/reduce_scatter | solution.py:195
  1132.0 55.3 %all-gather.29.cloned.1.call-done = bf16[2048,1024]{1,0:T(8,128)(2,1)} async-done(((bf16[1024,1024]{1,0:T(8,128)(2,1)}), bf16[2048,1024]{1,0:T(8,128)(2,1)}) %all-gather.29.cloned.1.call-update) | async-done | bytes 4194320 | tf_op jit(solution)/shard_map/all_gather | solution.py:200
  1216.3 627.2 %while.69 = (s32[]{:T(128)}, f32[2,128,256]{2,1,0:T(8,128)S(1)}, bf16[32,2,64,128]{3,2,1,0:T(8,128)(2,1)S(1)}, bf16[32,2,64,128]{3,2,1,0:T(8,128)(2,1)}, bf16[32...) while((s32[]{:T(128)}, f32[2,128,256]{2,1,0:T(8,128)S(1)}, ...), condition=%wide.region_17.18_spmd.clone.clone, body=%wide.region_13.17_spmd.clone.sunk.clone | while | flops 278814976 | bytes 5252164 | solution.py:85
  1872.8 14.3 add_convert_fusion
  1980.0 41.5 %all-reduce.1 = (f32[1024]{0:T(1024)}, f32[1024]{0:T(1024)}, f32[16,512]{1,0:T(8,128)}, f32[512]{0:T(512)}, f32[256]{0:T(256)}) all-reduce(f32[1024]{0:T(1024)S(1)} %get-tuple-element.1044, f32[1024]{0:T(1024)S(1)} %get-tuple-element.1042, f32[16,512]{1,0:T(8,128)S(1)} %fusion.130, ...), channel_id=1, replica_groups=mesh['dp'=16,'tensor'=2] {'dp','tensor'}, use_global_device_ids=true, to_apply=%region_29.30 | all-reduce | flops 11008 | bytes 88064 | tf_op jit(solution)/shard_map/psum | solution.py:265
  2029.3 55.5 %reduce-scatter.33.cloned.1.call-done = f32[64,1408]{1,0:T(8,128)} async-done(((f32[1024,1408]{1,0:T(8,128)}), f32[64,1408]{1,0:T(8,128)}) %reduce-scatter.33.cloned.1.call-update) | async-done | bytes 360464 | tf_op jit(solution)/shard_map/reduce_scatter | solution.py:251
  2084.9 85.1 %reduce-scatter.35.cloned.1.call-done = f32[64,1408]{1,0:T(8,128)} async-done(((f32[1024,1408]{1,0:T(8,128)}), f32[64,1408]{1,0:T(8,128)}) %reduce-scatter.35.cloned.1.call-update) | async-done | bytes 360464 | tf_op jit(solution)/shard_map/reduce_scatter | solution.py:252
  2169.9 85.1 %reduce-scatter.37.cloned.1.call-done = f32[64,1408]{1,0:T(8,128)} async-done(((f32[1024,1408]{1,0:T(8,128)}), f32[64,1408]{1,0:T(8,128)}) %reduce-scatter.37.cloned.1.call-update) | async-done | bytes 360464
  2255.0 122.8 %all-reduce.4.cloned.1.call-done = f32[1024,16]{0,1:T(8,128)} async-done(((f32[1024,16]{0,1:T(8,128)}), f32[1024,16]{0,1:T(8,128)}) %all-reduce.4.cloned.1.call-update) | async-done | bytes 65552 | tf_op jit(solution)/shard_map/psum | solution.py:265
  2377.8 62.3 %reduce-scatter.23.cloned.1.call-done = f32[64,256]{1,0:T(8,128)} async-done(((f32[1024,256]{1,0:T(8,128)}), f32[64,256]{1,0:T(8,128)}) %reduce-scatter.23.cloned.1.call-update) | async-done | bytes 65552 | tf_op jit(solution)/shard_map/reduce_scatter | solution.py:246
  2440.1 60.9 %reduce-scatter.25.cloned.1.call-done = f32[64,256]{1,0:T(8,128)} async-done(((f32[1024,256]{1,0:T(8,128)}), f32[64,256]{1,0:T(8,128)}) %reduce-scatter.25.cloned.1.call-update) | async-done | bytes 65552 | tf_op jit(solution)/shard_map/reduce_scatter | solution.py:247
  2501.1 65.0 %reduce-scatter.27.cloned.1.call-done = f32[64,512]{1,0:T(8,128)} async-done(((f32[1024,512]{1,0:T(8,128)}), f32[64,512]{1,0:T(8,128)}) %reduce-scatter.27.cloned.1.call-update) | async-done | bytes 131088 | tf_op jit(solution)/shard_map/reduce_scatter | solution.py:248
  2566.0 65.4 %reduce-scatter.29.cloned.1.call-done = f32[64,512]{1,0:T(8,128)} async-done(((f32[1024,512]{1,0:T(8,128)}), f32[64,512]{1,0:T(8,128)}) %reduce-scatter.29.cloned.1.call-update) | async-done | bytes 131088 | tf_op jit(solution)/shard_map/reduce_scatter | solution.py:249
  2631.4 64.9 %reduce-scatter.31.cloned.1.call-done = f32[64,512]{1,0:T(8,128)} async-done(((f32[1024,512]{1,0:T(8,128)}), f32[64,512]{1,0:T(8,128)}) %reduce-scatter.31.cloned.1.call-update) | async-done | bytes 131088 | tf_op jit(solution)/shard_map/reduce_scatter | solution.py:250
  (1511 shorter events, 1428.4 us)
Async XLA Ops:
  7.2 66.5 %all-gather.11.cloned.1.call-start = ((), (), s32[]{:S(2)}) async-start(), calls=%async_computation.12 | async-start | bytes 6291456 | tf_op jit(solution)/shard_map/all_gather | solution.py:145
  14.1 99.7 %all-gather.13.cloned.1.call-start = ((), (), s32[]{:S(2)}) async-start(), calls=%async_computation.13 | async-start | bytes 1114112 | tf_op jit(solution)/shard_map/all_gather | solution.py:134
  14.8 645.4 %all-gather.15.cloned.1.call-start = ((), (), s32[]{:S(2)}) async-start(), calls=%async_computation.14 | async-start | bytes 1114112 | tf_op jit(solution)/shard_map/all_gather | solution.py:135
  15.5 656.0 %all-gather.17.cloned.1.call-start = ((), (), s32[]{:S(2)}) async-start(), calls=%async_computation.15 | async-start | bytes 1114112 | tf_op jit(solution)/shard_map/all_gather | solution.py:140
  16.1 761.5 %reduce-scatter.15.cloned.1.call-start = ((), (), s32[]{:S(2)}) async-start(), calls=%async_computation.16 | async-start | bytes 12582912 | tf_op jit(solution)/shard_map/reduce_scatter | solution.py:169
  16.3 643.9 %copy-start.44 = (f32[1,2,2,128]{3,1,2,0:T(2,128)}, f32[1,2,2,128]{3,1,2,0:T(2,128)S(1)}, u32[]{:S(2)}) copy-start(f32[1,2,2,128]{3,1,2,0:T(2,128)S(1)} %copy.115) | copy-start | bytes 6148
  679.3 145.1 %all-gather.21.cloned.1.call-start = ((), (), s32[]{:S(2)}) async-start(), calls=%async_computation.18 | async-start | bytes 3063808 | tf_op jit(solution)/shard_map/all_gather | solution.py:136
  679.9 201.3 %all-gather.19.cloned.1.call-start = ((), (), s32[]{:S(2)}) async-start(), calls=%async_computation.17 | async-start | bytes 6291456 | tf_op jit(solution)/shard_map/all_gather | solution.py:174
  784.2 143.9 %all-gather.23.cloned.1.call-start = ((), (), s32[]{:S(2)}) async-start(), calls=%async_computation.19 | async-start | bytes 3063808 | tf_op jit(solution)/shard_map/all_gather | solution.py:137
  784.9 199.9 %all-gather.27.cloned.1.call-start = ((), (), s32[]{:S(2)}) async-start(), calls=%async_computation.22 | async-start | bytes 6291456 | tf_op jit(solution)/shard_map/all_gather | solution.py:186
  785.7 245.9 %all-gather.25.cloned.1.call-start = ((), (), s32[]{:S(2)}) async-start(), calls=%async_computation.20 | async-start | bytes 3063808 | tf_op jit(solution)/shard_map/all_gather | solution.py:141
  786.2 337.0 %reduce-scatter.19.cloned.1.call-start = ((), (), s32[]{:S(2)}) async-start(), calls=%async_computation.23 | async-start | bytes 6291456 | tf_op jit(solution)/shard_map/reduce_scatter | solution.py:195
  1070.5 116.8 %all-gather.29.cloned.1.call-start = ((), (), s32[]{:S(2)}) async-start(), calls=%async_computation.24 | async-start | bytes 6291456 | tf_op jit(solution)/shard_map/all_gather | solution.py:200
  1130.4 846.3 %reduce-scatter.21.cloned.1.call-start = ((), (), s32[]{:S(2)}) async-start(), calls=%async_computation.25 | async-start | bytes 6291456 | tf_op jit(solution)/shard_map/reduce_scatter | solution.py:234
  1887.2 134.4 %reduce-scatter.17.cloned.1.call-start = ((), (), s32[]{:S(2)}) async-start(), calls=%async_computation.21 | async-start | bytes 6291456 | tf_op jit(solution)/shard_map/reduce_scatter | solution.py:179
  1898.7 186.1 %reduce-scatter.33.cloned.1.call-start = ((), (), s32[]{:S(2)}) async-start(), calls=%async_computation.31 | async-start | bytes 6127616 | tf_op jit(solution)/shard_map/reduce_scatter | solution.py:251
  1911.0 258.9 %reduce-scatter.35.cloned.1.call-start = ((), (), s32[]{:S(2)}) async-start(), calls=%async_computation.32 | async-start | bytes 6127616 | tf_op jit(solution)/shard_map/reduce_scatter | solution.py:252
  1923.0 332.0 %reduce-scatter.37.cloned.1.call-start = ((), (), s32[]{:S(2)}) async-start(), calls=%async_computation.34 | async-start | bytes 6127616
  1940.8 437.1 %all-reduce.4.cloned.1.call-start = ((), (), s32[]{:S(2)}) async-start(), calls=%async_computation.33 | async-start | bytes 131072 | tf_op jit(solution)/shard_map/psum | solution.py:265
  1945.5 494.7 %reduce-scatter.23.cloned.1.call-start = ((), (), s32[]{:S(2)}) async-start(), calls=%async_computation.26 | async-start | bytes 1114112 | tf_op jit(solution)/shard_map/reduce_scatter | solution.py:246
  1950.4 550.7 %reduce-scatter.25.cloned.1.call-start = ((), (), s32[]{:S(2)}) async-start(), calls=%async_computation.27 | async-start | bytes 1114112 | tf_op jit(solution)/shard_map/reduce_scatter | solution.py:247
  1955.1 611.0 %reduce-scatter.27.cloned.1.call-start = ((), (), s32[]{:S(2)}) async-start(), calls=%async_computation.28 | async-start | bytes 2228224 | tf_op jit(solution)/shard_map/reduce_scatter | solution.py:248
  1961.0 670.4 %reduce-scatter.29.cloned.1.call-start = ((), (), s32[]{:S(2)}) async-start(), calls=%async_computation.29 | async-start | bytes 2228224 | tf_op jit(solution)/shard_map/reduce_scatter | solution.py:249
  1967.8 728.5 %reduce-scatter.31.cloned.1.call-start = ((), (), s32[]{:S(2)}) async-start(), calls=%async_computation.30 | async-start | bytes 2228224 | tf_op jit(solution)/shard_map/reduce_scatter | solution.py:250
  (85 other events, 1357.0 us)
Sparse Core Ops, SparseCore 0:
  14.2 59.4 all-gather.10
  75.8 37.9 all-gather.12
  116.0 36.8 all-gather.14
  154.9 36.9 all-gather.16
  679.4 98.1 reduce-scatter.14
  780.0 44.3 all-gather.20
  826.0 55.0 all-gather.18
  883.7 44.3 all-gather.22
  929.7 55.0 all-gather.26
  987.2 44.3 all-gather.24
  1070.6 52.6 reduce-scatter.18
  1130.5 56.7 all-gather.28
  1887.3 54.2 reduce-scatter.20
  1943.9 55.0 reduce-scatter.16
  2003.3 81.5 reduce-scatter.32
  2089.2 80.7 reduce-scatter.34
  2174.2 80.7 reduce-scatter.36
  2261.0 116.7 all-reduce.3
  2382.0 58.0 reduce-scatter.22
  2444.6 56.4 reduce-scatter.24
  2505.4 60.6 reduce-scatter.26
  2570.8 60.5 reduce-scatter.28
  2635.7 60.5 reduce-scatter.30
where the time goes:
time: 2730 us; the launch traced here: 2700 us
  waiting for transfers between devices  1120 us (41%)
  matrix products  772 us (28%)
  other arithmetic  369 us (14%)
  local copies, waits for them, and re-layouts  293 us (11%)
  blocking collectives  84.9 us (3%)
  loops' own time  46.1 us (2%)
    dynamic_update_slice x160, other arithmetic, linear_core(): unused, outs = lax.scan(advance, start, items)  150 us
    dot_general x96, matrix products, advance(): jnp.einsum('hik,hjk->hij', query_decayed, key_dec, precision=HIGH_ACCURACY)  148 us
    dot_general x96, matrix products, advance(): jnp.einsum('hij,hjv->hiv', scores, block_values, precision=HIGH_ACCURACY)  137 us
    dot_general x96, matrix products, advance(): jnp.einsum('wcb,wba->wca', query_decayed, state_matrix, precision=HIGH_AC...  128 us
    dot_general x96, matrix products, advance(): jnp.einsum('zco,zcr->zor', key_tail_decay, block_values, precision=HIGH_A...  125 us
    psum x1, waiting for transfers between devices, local(): lax.psum((mixer_gain_grad, feed_gain_grad, low_first_grad, low_second_gra...  123 us
    another operation x96, other arithmetic, advance(): cumul = jnp.cumsum(decay_block, axis=1)  101 us
    reduce_scatter x1, waiting for transfers between devices, local(): lax.psum_scatter(product(gated_low, full_output), 'tensor', scatter_dimen...  97.7 us
  transfers between devices with their start and end apart: 23, of which 19 were waited for; matrix products, arithmetic and copies ran while one was open for 25% of the time, Pallas kernels for 0%

commit v1 on v0

v1 whole, which is shorter than its diff:
```python
import jax
import jax.numpy as jnp
from jax import lax
from jax.experimental import pallas as pl
from jax.experimental.pallas import tpu as pltpu
from jax.sharding import PartitionSpec as P

HEADS = 4
KEY = 128
VAL = 256
CHUNK = 128
SCALE = KEY ** (-0.5)
F32 = jnp.float32
BF16 = jnp.bfloat16
HIGHEST = lax.Precision.HIGHEST
ALL = ("tensor", "dp")
VMEM_BYTES = 48 * 1024 * 1024


def nn(a, b):
    return lax.dot_general(a, b, (((1,), (0,)), ((), ())), preferred_element_type=F32)


def nt(a, b):
    return lax.dot_general(a, b, (((1,), (1,)), ((), ())), preferred_element_type=F32)


def tn(a, b):
    return lax.dot_general(a, b, (((0,), (0,)), ((), ())), preferred_element_type=F32)


def triangle(lower):
    rows = lax.broadcasted_iota(jnp.int32, (CHUNK, CHUNK), 0)
    cols = lax.broadcasted_iota(jnp.int32, (CHUNK, CHUNK), 1)
    return rows >= cols if lower else rows <= cols


def split_sum(tri, x, terms):
    total = None
    for _ in range(terms):
        part = x.astype(BF16)
        x = x - part.astype(F32)
        term = nn(tri, part)
        total = term if total is None else total + term
    return total


def head_cols(h, width):
    return h // 2, slice((h % 2) * width, (h % 2 + 1) * width)


def gate_kernel(info, low_ref, second_ref, bias_ref, k_ref, v_ref, seg_ref, cum_ref, sig_ref, state_ref):
    c = pl.program_id(0)

    @pl.when(c == 0)
    def _():
        state_ref[...] = jnp.zeros_like(state_ref)

    logit = (
        jnp.dot(low_ref[...], second_ref[...], precision=HIGHEST, preferred_element_type=F32)
        + bias_ref[...]
    )
    e = jnp.exp(-jnp.abs(logit))
    decays = (jnp.minimum(logit, 0.0) - jnp.log1p(e)) * (1.0 / 16.0)
    sig_ref[...] = (jnp.where(logit >= 0, e, 1.0) / (1.0 + e)).astype(BF16)
    tri = triangle(True).astype(F32).astype(BF16)
    cum = split_sum(tri, decays, 3)
    cum_ref[...] = cum
    final = cum[CHUNK - 1 :, :]
    tail = (seg_ref[...] == info[1, c]).astype(F32)
    retain = (info[1, c] == info[0, c]).astype(F32)
    tail_decay = jnp.exp(final - cum) * tail
    keep = jnp.exp(final) * retain
    for h in range(HEADS):
        p, kc = head_cols(h, KEY)
        _, vc = head_cols(h, VAL)
        hk = slice(h * KEY, (h + 1) * KEY)
        kt = (k_ref[p, :, kc].astype(F32) * tail_decay[:, hk]).astype(BF16)
        state_ref[h] = state_ref[h] * keep[:, hk].reshape(KEY, 1) + tn(kt, v_ref[p, :, vc])


def core_kernel(
    info, q_ref, k_ref, v_ref, og_ref, cum_ref, seg_ref, row_ref, first_ref, gain_ref,
    mixed_ref, core_ref, states_ref, state,
):
    c = pl.program_id(0)

    @pl.when(c == 0)
    def _():
        state[...] = first_ref[...].astype(F32)

    before, last = info[0, c], info[1, c]
    seg = seg_ref[...]
    mask = triangle(True) & (seg == row_ref[0])
    running = (seg == before).astype(F32)
    tail = (seg == last).astype(F32)
    retain = (last == before).astype(F32)
    cum = cum_ref[...]
    final = cum[CHUNK - 1 :, :]
    mid = cum[CHUNK // 2 - 1 : CHUNK // 2, :]
    up, down = jnp.exp(cum - mid), jnp.exp(mid - cum)
    whole = jnp.exp(cum) * running
    rest = jnp.exp(final - cum) * tail
    keep = jnp.exp(final) * retain
    for h in range(HEADS):
        p, kc = head_cols(h, KEY)
        _, vc = head_cols(h, VAL)
        hk = slice(h * KEY, (h + 1) * KEY)
        q = q_ref[p, :, kc].astype(F32) * SCALE
        k = k_ref[p, :, kc].astype(F32)
        v = v_ref[p, :, vc]
        s = state[h]
        s_low = s.astype(BF16)
        states_ref[0, h] = s_low
        scores = nt((q * up[:, hk]).astype(BF16), (k * down[:, hk]).astype(BF16))
        scores = jnp.where(mask, scores, 0.0).astype(BF16)
        core = nn((q * whole[:, hk]).astype(BF16), s_low) + nn(scores, v)
        state[h] = s * keep[:, hk].reshape(KEY, 1) + tn((k * rest[:, hk]).astype(BF16), v)
        normed = core * lax.rsqrt(jnp.mean(core * core, axis=-1, keepdims=True) + 1.0)
        og = og_ref[p, :, vc].astype(F32)
        hv = slice(h * VAL, (h + 1) * VAL)
        mixed_ref[:, hv] = (normed * gain_ref[...] * (og * jax.nn.sigmoid(og))).astype(BF16)
        core_ref[:, hv] = core.astype(BF16)


def post_kernel(
    info, dm_ref, core_ref, og_ref, q_ref, cum_ref, seg_ref, gain_ref,
    dcore_ref, dog_ref, dgain_ref, dstate_ref, prefix,
):
    c = pl.program_id(0)

    @pl.when(c == 0)
    def _():
        prefix[...] = jnp.zeros_like(prefix)
        dgain_ref[...] = jnp.zeros_like(dgain_ref)
        dstate_ref[...] = jnp.zeros_like(dstate_ref)

    running = (seg_ref[...] == info[0, 0]).astype(F32)
    cum = cum_ref[...]
    decay = jnp.exp(cum + prefix[...]) * running * SCALE
    prefix[...] += cum[CHUNK - 1 :, :]
    gain = gain_ref[...]
    total = jnp.zeros((1, VAL), F32)
    for h in range(HEADS):
        p, kc = head_cols(h, KEY)
        _, vc = head_cols(h, VAL)
        hk = slice(h * KEY, (h + 1) * KEY)
        hv = slice(h * VAL, (h + 1) * VAL)
        core = core_ref[:, hv].astype(F32)
        scale = lax.rsqrt(jnp.mean(core * core, axis=-1, keepdims=True) + 1.0)
        normed = core * scale
        og = og_ref[p, :, vc].astype(F32)
        sig = jax.nn.sigmoid(og)
        silu = og * sig
        dm = dm_ref[:, hv].astype(F32)
        both = dm * normed
        total += jnp.sum(both * silu, axis=0, keepdims=True)
        dog_ref[p, :, vc] = (both * gain * (sig * (1.0 + og * (1.0 - sig)))).astype(BF16)
        dn = dm * gain * silu
        dcore = scale * (dn - normed * jnp.mean(dn * normed, axis=-1, keepdims=True))
        dcore = dcore.astype(BF16)
        dcore_ref[:, hv] = dcore
        qa = (q_ref[p, :, kc].astype(F32) * decay[:, hk]).astype(BF16)
        dstate_ref[h] += tn(qa, dcore)
    dgain_ref[...] += total


def back_kernel(
    info, q_ref, k_ref, v_ref, cum_ref, sig_ref, states_ref, dcore_ref, seg_ref, row_ref,
    first_ref, second_ref, low_ref, dqkv_ref, drank_ref, dsecond_ref, dbias_ref, dstate,
):
    i = pl.program_id(0)
    c = pl.num_programs(0) - 1 - i

    @pl.when(i == 0)
    def _():
        dstate[...] = first_ref[...].astype(F32)
        dsecond_ref[...] = jnp.zeros_like(dsecond_ref)
        dbias_ref[...] = jnp.zeros_like(dbias_ref)

    before, last = info[0, c], info[1, c]
    seg = seg_ref[...]
    mask = triangle(True) & (seg == row_ref[0])
    upper = triangle(False).astype(F32).astype(BF16)
    running = (seg == before).astype(F32)
    tail = (seg == last).astype(F32)
    retain = (last == before).astype(F32)
    cum = cum_ref[...]
    final = cum[CHUNK - 1 :, :]
    mid = cum[CHUNK // 2 - 1 : CHUNK // 2, :]
    up, down = jnp.exp(cum - mid), jnp.exp(mid - cum)
    whole = jnp.exp(cum) * running
    rest = jnp.exp(final - cum) * tail
    keep = jnp.exp(final) * retain
    logits = []
    for h in range(HEADS):
        p, kc = head_cols(h, KEY)
        _, vc = head_cols(h, VAL)
        hk = slice(h * KEY, (h + 1) * KEY)
        hv = slice(h * VAL, (h + 1) * VAL)
        q = q_ref[p, :, kc].astype(F32) * SCALE
        k = k_ref[p, :, kc].astype(F32)
        v = v_ref[p, :, vc]
        do = dcore_ref[:, hv]
        s = states_ref[0, h]
        ds = dstate[h]
        ds_low = ds.astype(BF16)
        q_up = (q * up[:, hk]).astype(BF16)
        k_down = (k * down[:, hk]).astype(BF16)
        q_whole = (q * whole[:, hk]).astype(BF16)
        k_rest = (k * rest[:, hk]).astype(BF16)
        scores = jnp.where(mask, nt(q_up, k_down), 0.0).astype(BF16)
        dscores = jnp.where(mask, nt(do, v), 0.0).astype(BF16)
        dq_up = nn(dscores, k_down)
        dk_down = tn(dscores, q_up)
        dq_whole = nt(do, s)
        dk_rest = nt(v, ds_low)
        dv = tn(scores, do) + nn(k_rest, ds_low)
        dq = dq_up * up[:, hk] + dq_whole * whole[:, hk]
        dk = dk_down * down[:, hk] + dk_rest * rest[:, hk]
        from_rest = k_rest.astype(F32) * dk_rest
        dcum = (
            q_up.astype(F32) * dq_up
            - k_down.astype(F32) * dk_down
            + q_whole.astype(F32) * dq_whole
            - from_rest
        )
        kept = keep[:, hk].reshape(KEY, 1)
        through = jnp.sum(s.astype(F32) * ds, axis=1, keepdims=True) * kept
        dfinal = through.reshape(1, KEY) + jnp.sum(from_rest, axis=0, keepdims=True)
        ddecay = split_sum(upper, dcum, 2) + dfinal
        dstate[h] = ds * kept + tn(q_whole, do)
        logits.append(ddecay * (sig_ref[:, hk].astype(F32) * (1.0 / 16.0)))
        dqkv_ref[p, :, kc] = (dq * SCALE).astype(BF16)
        dqkv_ref[p, :, slice(256 + kc.start, 256 + kc.stop)] = dk.astype(BF16)
        dqkv_ref[p, :, slice(512 + vc.start, 512 + vc.stop)] = dv.astype(BF16)
    dlogit = jnp.concatenate(logits, axis=1)
    dbias_ref[...] += jnp.sum(dlogit, axis=0, keepdims=True)
    low = dlogit.astype(BF16)
    dsecond_ref[...] += tn(low_ref[...].astype(BF16), low)
    drank_ref[...] = nt(low, second_ref[...].astype(BF16))


def shape(dims, dtype):
    return jax.ShapeDtypeStruct(dims, dtype)


def call(kernel, blocks, in_specs, out_specs, out_shape, scratch, cost):
    return pl.pallas_call(
        kernel,
        grid_spec=pltpu.PrefetchScalarGridSpec(
            num_scalar_prefetch=1,
            grid=(blocks,),
            in_specs=in_specs,
            out_specs=out_specs,
            scratch_shapes=scratch,
        ),
        out_shape=out_shape,
        compiler_params=pltpu.CompilerParams(
            dimension_semantics=("arbitrary",), vmem_limit_bytes=VMEM_BYTES
        ),
        cost_estimate=pl.CostEstimate(flops=cost, bytes_accessed=16 << 20, transcendentals=1 << 20),
    )


def specs(blocks, backward=False):
    def at(c):
        return blocks - 1 - c if backward else c

    def proj(width, place):
        return pl.BlockSpec((2, CHUNK, width), lambda c, _: (0, at(c), place))

    def rows(width):
        return pl.BlockSpec((CHUNK, width), lambda c, _: (at(c), 0))

    def full(*dims):
        return pl.BlockSpec(dims, lambda c, _: (0,) * len(dims))

    row = pl.BlockSpec((1, 1, CHUNK), lambda c, _: (at(c), 0, 0))
    states = pl.BlockSpec((1, HEADS, KEY, VAL), lambda c, _: (at(c), 0, 0, 0))
    return proj, rows, full, row, states


def rms(x, eps):
    return x * lax.rsqrt(jnp.mean(x * x, axis=-1, keepdims=True) + eps)


def rms_back(x, gain, eps, grad):
    scale = lax.rsqrt(jnp.mean(x * x, axis=-1, keepdims=True) + eps)
    normed = x * scale
    dn = grad * gain
    back = scale * (dn - normed * jnp.mean(dn * normed, axis=-1, keepdims=True))
    return back, jnp.sum(grad * normed, axis=0)


def gather(shard):
    return lax.all_gather(shard, ALL, axis=0, tiled=True).reshape(2, -1, shard.shape[1])


def scatter(grad):
    flat = grad.reshape(-1, grad.shape[-1])
    return lax.psum_scatter(flat, ALL, scatter_dimension=0, tiled=True).astype(F32)


def total_sum(x):
    x = x + lax.ppermute(x, "tensor", [(0, 1), (1, 0)])
    n = lax.axis_size("dp")
    stride = 1
    while stride < n:
        x = x + lax.ppermute(x, "dp", [(i, i ^ stride) for i in range(n)])
        stride *= 2
    return x


def local(
    hidden_in, lengths, cotangent, query_weight, key_weight, value_weight, outgate_weight,
    output_weight, gate_weight, up_weight, down_weight, mixer_gain, feed_gain, low_first,
    low_second, decay_bias, head_gain,
):
    rows, width = hidden_in.shape
    blocks = rows // CHUNK
    place = lax.axis_index("tensor")
    half = gate_weight.shape[1]

    starts = jnp.cumsum(lengths[0]) - lengths[0]
    spots = place * rows + jnp.arange(-1, rows, dtype=jnp.int32)
    segments = jnp.sum((spots[:, None] >= starts[None, 1:]).astype(jnp.int32), axis=1)
    segments = jnp.where(spots < 0, -1, segments)
    seg = segments[1:].reshape(rows, 1)
    seg_row = segments[1:].reshape(blocks, 1, CHUNK)
    info = jnp.stack([segments[:-1].reshape(blocks, CHUNK)[:, 0], seg_row[:, 0, -1]])

    w_in = gather(jnp.concatenate([query_weight, key_weight, value_weight, outgate_weight], axis=1))
    w_out = gather(output_weight.T)
    w_gu = gather(jnp.concatenate([gate_weight, up_weight], axis=1))
    w_down = gather(down_weight.T)

    resid = hidden_in.astype(F32)
    normed_a = (rms(resid, 1e-6) * mixer_gain).astype(BF16)
    proj = jnp.einsum("td,pdc->ptc", normed_a, w_in, preferred_element_type=F32).astype(BF16)
    lowrank = jnp.dot(normed_a.astype(F32), low_first, precision=HIGHEST)
    gain = head_gain.reshape(1, VAL)
    p_spec, r_spec, f_spec, row_spec, s_spec = specs(blocks)
    state_f32 = shape((HEADS, KEY, VAL), F32)
    cum, sig, final_state = call(
        gate_kernel,
        blocks,
        [r_spec(16), f_spec(16, 512), f_spec(1, 512), p_spec(256, 1), p_spec(512, 1), r_spec(1)],
        [r_spec(512), r_spec(512), f_spec(HEADS, KEY, VAL)],
        [shape((rows, 512), F32), shape((rows, 512), BF16), state_f32],
        [],
        1 << 29,
    )(info, lowrank, low_second, decay_bias.reshape(1, 512), proj, proj, seg)
    state_in = lax.ppermute(final_state.astype(BF16), "tensor", [(0, 1)])
    mixed, core, states = call(
        core_kernel,
        blocks,
        [p_spec(256, 0), p_spec(256, 1), p_spec(512, 1), p_spec(512, 2), r_spec(512), r_spec(1),
         row_spec, f_spec(HEADS, KEY, VAL), f_spec(1, VAL)],
        [r_spec(1024), r_spec(1024), s_spec],
        [shape((rows, 1024), BF16), shape((rows, 1024), BF16),
         shape((blocks, HEADS, KEY, VAL), BF16)],
        [pltpu.VMEM((HEADS, KEY, VAL), F32)],
        1 << 30,
    )(info, proj, proj, proj, proj, cum, seg, seg_row, state_in, gain)
    middle = resid + nt(mixed[:, :512], w_out[0]) + nt(mixed[:, 512:], w_out[1])

    normed_b = (rms(middle, 1e-6) * feed_gain).astype(BF16)
    pre = jnp.einsum("td,pdc->ptc", normed_b, w_gu, preferred_element_type=F32).astype(BF16)
    gate_pre, up_pre = pre[..., :half].astype(F32), pre[..., half:].astype(F32)
    sig_gate = jax.nn.sigmoid(gate_pre)
    silu = gate_pre * sig_gate
    activ = (silu * up_pre).astype(BF16)
    feed_out = nt(activ[0], w_down[0]) + nt(activ[1], w_down[1])
    block_out = (middle + feed_out).astype(BF16)

    down_grad = jnp.einsum("to,ptc->poc", cotangent, activ, preferred_element_type=F32).astype(BF16)
    own_down = scatter(down_grad)
    d_activ = jnp.einsum("to,poc->ptc", cotangent, w_down, preferred_element_type=F32)
    d_gate = (d_activ * up_pre * (sig_gate * (1.0 + gate_pre * (1.0 - sig_gate)))).astype(BF16)
    d_up = (d_activ * silu).astype(BF16)
    d_pre = jnp.concatenate([d_gate, d_up], axis=-1)
    gu_grad = jnp.einsum("td,ptc->pdc", normed_b, d_pre, preferred_element_type=F32).astype(BF16)
    own_gu = scatter(gu_grad)
    d_normed_b = nt(d_pre[0], w_gu[0]) + nt(d_pre[1], w_gu[1])
    back, feed_gain_grad = rms_back(middle, feed_gain, 1e-6, d_normed_b)
    d_middle = cotangent.astype(F32) + back
    d_mix = d_middle.astype(BF16)

    out_grad = jnp.einsum(
        "to,tpc->poc", d_mix, mixed.reshape(rows, 2, 512), preferred_element_type=F32
    ).astype(BF16)
    d_mixed = jnp.concatenate([nn(d_mix, w_out[0]), nn(d_mix, w_out[1])], axis=1).astype(BF16)
    d_core, d_og, head_gain_grad, d_state = call(
        post_kernel,
        blocks,
        [r_spec(1024), r_spec(1024), p_spec(512, 2), p_spec(256, 0), r_spec(512), r_spec(1),
         f_spec(1, VAL)],
        [r_spec(1024), p_spec(512, 0), f_spec(1, VAL), f_spec(HEADS, KEY, VAL)],
        [shape((rows, 1024), BF16), shape((2, rows, 512), BF16), shape((1, VAL), F32), state_f32],
        [pltpu.VMEM((1, 512), F32)],
        1 << 29,
    )(info, d_mixed, core, proj, proj, cum, seg, gain)
    d_state_in = lax.ppermute(d_state.astype(BF16), "tensor", [(1, 0)])
    p_spec, r_spec, f_spec, row_spec, s_spec = specs(blocks, True)
    d_qkv, d_rank, low_second_grad, bias_grad = call(
        back_kernel,
        blocks,
        [p_spec(256, 0), p_spec(256, 1), p_spec(512, 1), r_spec(512), r_spec(512), s_spec,
         r_spec(1024), r_spec(1), row_spec, f_spec(HEADS, KEY, VAL), f_spec(16, 512), r_spec(16)],
        [p_spec(1024, 0), r_spec(16), f_spec(16, 512), f_spec(1, 512)],
        [shape((2, rows, 1024), BF16), shape((rows, 16), F32), shape((16, 512), F32),
         shape((1, 512), F32)],
        [pltpu.VMEM((HEADS, KEY, VAL), F32)],
        3 << 30,
    )(info, proj, proj, proj, cum, sig, states, d_core, seg, seg_row, d_state_in, low_second, lowrank)
    d_proj = jnp.concatenate([d_qkv, d_og], axis=-1)
    in_grad = jnp.einsum("td,ptc->pdc", normed_a, d_proj, preferred_element_type=F32).astype(BF16)
    own_mix = scatter(jnp.concatenate([in_grad, out_grad], axis=-1))
    low_first_grad = tn(normed_a, d_rank.astype(BF16))
    d_normed_a = (
        nt(d_proj[0], w_in[0])
        + nt(d_proj[1], w_in[1])
        + nt(d_rank.astype(BF16), low_first.astype(BF16))
    )
    back, mixer_gain_grad = rms_back(resid, mixer_gain, 1e-6, d_normed_a)
    input_grad = (d_middle + back).astype(BF16)

    parts = (mixer_gain_grad, feed_gain_grad, low_first_grad, low_second_grad, bias_grad, head_gain_grad)
    flat = total_sum(jnp.concatenate([part.reshape(-1, 128) for part in parts]))
    small, spot = [], 0
    for part, dims in zip(
        parts, ((width,), (width,), low_first.shape, low_second.shape, (512,), (VAL,))
    ):
        size = part.size // 128
        small.append(flat[spot : spot + size].reshape(dims))
        spot += size
    return (
        block_out,
        input_grad,
        own_mix[:, :256],
        own_mix[:, 256:512],
        own_mix[:, 512:1024],
        own_mix[:, 1024:1536],
        own_mix[:, 1536:].T,
        own_gu[:, :half],
        own_gu[:, half:],
        own_down.T,
        *small,
    )


def solution(mesh):
    tokens = P(("dp", "tensor"), None)
    split_in = P("dp", "tensor")
    split_out = P("tensor", "dp")
    weights = (split_in,) * 4 + (split_out,) + (split_in,) * 2 + (split_out,)
    in_specs = (tokens, P("dp", None), tokens) + weights + (P(),) * 6
    out_specs = (tokens, tokens) + weights + (P(),) * 6
    return jax.shard_map(local, mesh=mesh, in_specs=in_specs, out_specs=out_specs, check_vma=False)
```

time: 2730 us -> 800 us (0.29)
  waiting for transfers between devices: 1120 us -> 486 us
  matrix products: 772 us -> 157 us
  other arithmetic: 369 us -> 25.1 us
  local copies, waits for them, and re-layouts: 293 us -> 51.8 us
  blocking collectives: 84.9 us -> 0 us
  Pallas kernels: 0 us -> 51.3 us
  loops' own time: 46.1 us -> 0 us
    dot_general x414 -> x20, matrix products: 772 us -> 157 us  [the longest x9 54.9 us: nt(): lax.dot_general(a, b, (((1,), (1,)), ((), ())), preferred_element_type=F32)]
    reduce_scatter x11 -> x3, waiting for transfers between devices: 610 us -> 246 us  [scatter(): lax.psum_scatter(flat, ALL, scatter_dimension=0, tiled=True).astype(F32)]
    dynamic_update_slice x161 -> x0, other arithmetic: 150 us -> none  [the longest x160 150 us: linear_core(): unused, outs = lax.scan(advance, start, items)]
    psum x1 -> x0, waiting for transfers between devices: 123 us -> none  [local(): lax.psum((mixer_gain_grad, feed_gain_grad, low_first_grad, low_second_gra...]
    another operation x100 -> x2, other arithmetic: 101 us -> 0.19 us  [the longest x96 101 us: advance(): cumul = jnp.cumsum(decay_block, axis=1)]
    unnamed x24 -> x7, waiting for transfers between devices: 89.5 us -> 1.3 us
    all_gather x10 -> x4, waiting for transfers between devices: 302 us -> 214 us  [gather(): lax.all_gather(shard, ALL, axis=0, tiled=True)]
    mul x97 -> x0, local copies, waits for them, and re-layouts: 70.7 us -> none  [the longest x32 24.6 us: advance(): jnp.einsum('hik,hjk->hij', query_decayed, key_dec, precision=HIGH_ACCURACY)]
  transfers between devices with their start and end apart: 23 -> 14, of which waited for: 19 -> 10; matrix products, arithmetic and copies ran while one was open for 25% -> 24% of each run, Pallas kernels for 0% -> 6%
where the time goes in v1:
time: 800 us; the launch traced here: 792 us
  waiting for transfers between devices  486 us (61%)
  matrix products  157 us (20%)
  local copies, waits for them, and re-layouts  51.8 us (6%)
  Pallas kernels  51.3 us (6%)
  other arithmetic  25.1 us (3%)
  between operations  15.2 us (2%)
    reduce_scatter x3, waiting for transfers between devices, scatter(): lax.psum_scatter(flat, ALL, scatter_dimension=0, tiled=True).astype(F32)  246 us
    all_gather x4, waiting for transfers between devices, gather(): lax.all_gather(shard, ALL, axis=0, tiled=True)  214 us
    dot_general x9, matrix products, nt(): lax.dot_general(a, b, (((1,), (1,)), ((), ())), preferred_element_type=F32)  54.9 us
    unnamed x80, local copies, waits for them, and re-layouts  28.9 us
    dot_general x1, matrix products, local(): jnp.einsum('to,poc->ptc', cotangent, w_down, preferred_element_type=F32)  22.3 us
    pallas_call x1, Pallas kernels, local(): call(back_kernel, blocks, [p_spec(256, 0), p_spec(256, 1), p_spec(512, 1)...  20.6 us
    dot_general x1, matrix products, local(): jnp.einsum('td,ptc->pdc', normed_b, d_pre, preferred_element_type=F32)  19.1 us
    dot_general x1, matrix products, local(): jnp.einsum('td,pdc->ptc', normed_b, w_gu, preferred_element_type=F32)  19.1 us
  transfers between devices with their start and end apart: 14, of which 10 were waited for; matrix products, arithmetic and copies ran while one was open for 24% of the time, Pallas kernels for 6%

profile of v1, /device:TPU:0, one launch (start us, length us, event | category | flops | bytes accessed | tf_op | source)
XLA Modules:
  0.0 791.7 jit_solution(7875835798304980173)
XLA Ops:
  19.2 64.5 %all-gather.5.cloned.1.call-done = bf16[2048,1536]{1,0:T(8,128)(2,1)} async-done(((bf16[64,1536]{1,0:T(8,128)(2,1)}), bf16[2048,1536]{1,0:T(8,128)(2,1)}) %all-gather.5.cloned.1.call-update) | async-done | bytes 6291472 | tf_op jit(solution)/shard_map/all_gather | solution.py:297
  83.7 11.7 %convert_bitcast_fusion.2.k_ref.v_ref.q_ref.og_ref = bf16[2,1024,1536]{2,1,0:T(8,128)(2,1)} fusion(bf16[2,1024,1536]{2,1,0:T(8,128)(2,1)} %bitcast.130, bf16[1024,1024]{0,1:T(8,128)(2,1)S(1)} %copy.128, f32[1024]{0:T(1024)S(1)} %copy-done.29, f32[1024]{0:T(1024)S(1)} %add_rsqrt_fusion.1), kind=kOutput, calls=%fused_computation.25 | convolution fusion | flops 6449790976 | bytes 14688256 | tf_op jit(solution)/shard_map/td,pdc->ptc/dot_general | solution.py:340
  95.5 10.2 %shard_map.288 = (f32[1024,512]{1,0:T(8,128)S(1)}, bf16[1024,512]{1,0:T(8,128)(2,1)S(1)}, f32[4,128,256]{2,1,0:T(8,128)S(1)}) custom-call(s32[2,8]{1,0:T(2,128)S(1)} %pad_add_fusion.info, f32[1024,16]{1,0:T(8,128)S(1)} %fusion.83.low_ref, f32[16,512]{1,0:T(8,128)S(1)} %copy-done.8, f32[1,512]{1,0:T(1,128)S(1)} %bitcast.117, ...), custom_call_target="tpu_custom_call" | custom-call | flops 536870912 | bytes 16777216 | tf_op jit(solution)/shard_map/pallas_call | solution.py:345
  117.4 10.5 %shard_map.289 = (bf16[1024,1024]{1,0:T(8,128)(2,1)S(1)}, bf16[1024,1024]{1,0:T(8,128)(2,1)S(1)}, bf16[8,4,128,256]{3,2,1,0:T(8,128)(2,1)}) custom-call(s32[2,8]{1,0:T(2,128)S(1)} %pad_add_fusion.info, bf16[2,1024,1536]{2,1,0:T(8,128)(2,1)} %convert_bitcast_fusion.2.k_ref.v_ref.q_ref.og_ref, ...), custom_call_target="tpu_custom_call" | custom-call | flops 1073741824 | bytes 16777216 | tf_op jit(solution)/shard_map/pallas_call | solution.py:355
  129.2 12.5 %all-gather.7.cloned.1.call-done = bf16[2048,512]{1,0:T(8,128)(2,1)} async-done(((bf16[64,512]{1,0:T(8,128)(2,1)}), bf16[2048,512]{1,0:T(8,128)(2,1)}) %all-gather.7.cloned.1.call-update) | async-done | bytes 2097168 | tf_op jit(solution)/shard_map/all_gather | solution.py:297
  147.8 87.4 %all-gather.9.cloned.1.call-done = bf16[2048,2816]{1,0:T(8,128)(2,1)} async-done(((bf16[64,2816]{1,0:T(8,128)(2,1)}), bf16[2048,2816]{1,0:T(8,128)(2,1)}) %all-gather.9.cloned.1.call-update) | async-done | bytes 11534352 | tf_op jit(solution)/shard_map/all_gather | solution.py:297
  235.2 19.1 %convert_bitcast_fusion = bf16[2,1024,2816]{1,2,0:T(8,128)(2,1)} fusion(bf16[2,1024,2816]{2,1,0:T(8,128)(2,1)} %bitcast.129, f32[1024,1024]{0,1:T(8,128)} %get-tuple-element.126, f32[1024]{0:T(1024)S(1)} %copy-done.31, f32[1024]{0:T(1024)S(1)} %add_rsqrt_fusion), kind=kOutput, calls=%fused_computation.21 | convolution fusion | flops 11820072960 | bytes 27271168 | tf_op jit(solution)/shard_map/td,pdc->ptc/dot_general | solution.py:369
  254.3 49.3 %all-gather.11.cloned.1.call-done = bf16[2048,1408]{1,0:T(8,128)(2,1)} async-done(((bf16[64,1408]{1,0:T(8,128)(2,1)}), bf16[2048,1408]{1,0:T(8,128)(2,1)}) %all-gather.11.cloned.1.call-update) | async-done | bytes 5767184 | tf_op jit(solution)/shard_map/all_gather | solution.py:297
  303.6 22.3 %fusion.9 = (bf16[2,1024,1408]{1,2,0:T(8,128)(2,1)}, bf16[2,1024,1408]{1,2,0:T(8,128)(2,1)}, bf16[2,1024,1408]{1,2,0:T(8,128)(2,1)}) fusion(bf16[2,1024,2816]{1,2,0:T(8,128)(2,1)} %convert_bitcast_fusion, bf16[2,1024,1408]{2,1,0:T(8,128)(2,1)} %bitcast.131, bf16[1024,1024]{1,0:T(8,128)(2,1)} %param.19), kind=kOutput, calls=%fused_computation.20 | convolution fusion | flops 5954600960 | bytes 36700160 | tf_op jit(solution)/shard_map/to,poc->ptc/dot_general | solution.py:379
  325.8 10.8 %convolution_convert_fusion = bf16[2,1408,1024]{1,2,0:T(8,128)(2,1)} fusion(bf16[2,1024,1408]{1,2,0:T(8,128)(2,1)} %get-tuple-element.114, bf16[1024,1024]{1,0:T(8,128)(2,1)S(1)} %copy-done.20), kind=kOutput, calls=%fused_computation.41 | convolution fusion | flops 5908463616 | bytes 13631488 | tf_op jit(solution)/shard_map/to,ptc->poc/dot_general | solution.py:377
  343.4 9.9 %fusion.17 = f32[1024,1024]{0,1:T(8,128)S(1)} fusion(bf16[2,1024,1408]{1,2,0:T(8,128)(2,1)} %get-tuple-element.113, bf16[2,1024,1408]{1,2,0:T(8,128)(2,1)} %get-tuple-element.112, bf16[2048,2816]{1,0:T(8,128)(2,1)} %all-gather.9.cloned.1.call-done), kind=kOutput, calls=%fused_computation.35 | convolution fusion | flops 5917114368 | bytes 21495808 | tf_op jit(solution)/shard_map/dot_general | solution.py:25
  353.3 12.0 %multiply_reduce_fusion = (f32[1024]{0:T(1024)S(1)}, f32[1024]{0:T(1024)S(1)}, f32[1024,1024]{0,1:T(8,128)}) fusion(f32[1024,1024]{0,1:T(8,128)S(1)} %copy-done.15, f32[1024]{0:T(1024)S(1)} %add_rsqrt_fusion, f32[1024]{0:T(1024)S(1)} %copy-done.31, f32[1024,1024]{0,1:T(8,128)S(1)} %fusion.17, bf16[2,1024,1408]{1,2,0:T(8,128)(2,1)} %get-tuple-element.113, ...), kind=kOutput, calls=%fused_computation.51 | convolution fusion | flops 5924452352 | bytes 29900800 | tf_op jit(solution)/shard_map/dot_general | solution.py:25
  373.2 10.0 %shard_map.290 = (bf16[1024,1024]{1,0:T(8,128)(2,1)S(1)}, bf16[2,1024,512]{2,1,0:T(8,128)(2,1)S(1)}, f32[1,256]{1,0:T(1,128)S(1)}, f32[4,128,256]{2,1,0:T(8,128)S(1)}) custom-call(s32[2,8]{1,0:T(2,128)S(1)} %pad_add_fusion.info, bf16[1024,1024]{1,0:T(8,128)(2,1)} %pad_maximum_fusion.5.dm_ref, bf16[1024,1024]{1,0:T(8,128)(2,1)} %copy-done.2, ...), custom_call_target="tpu_custom_call" | custom-call | flops 536870912 | bytes 16777216 | tf_op jit(solution)/shard_map/pallas_call | solution.py:394
  389.6 7.2 collective-permute-done.1.first_ref
  396.8 20.6 %shard_map.291 = (bf16[2,1024,1024]{2,1,0:T(8,128)(2,1)}, f32[1024,16]{1,0:T(8,128)S(1)}, f32[16,512]{1,0:T(8,128)S(1)}, f32[1,512]{1,0:T(1,128)S(1)}) custom-call(s32[2,8]{1,0:T(2,128)S(1)} %pad_add_fusion.info, bf16[2,1024,1536]{2,1,0:T(8,128)(2,1)} %convert_bitcast_fusion.2.k_ref.v_ref.q_ref.og_ref, ...), custom_call_target="tpu_custom_call" | custom-call | flops 3221225472 | bytes 16777216 | tf_op jit(solution)/shard_map/pallas_call | solution.py:406
  423.2 9.2 %convert_bitcast_fusion.1 = bf16[2,1024,1536]{1,2,0:T(8,128)(2,1)} fusion(bf16[2,1024,1536]{2,1,0:T(8,128)(2,1)S(1)} %constant_dynamic-update-slice_fusion, bf16[1024,1024]{0,1:T(8,128)(2,1)S(1)} %copy-done.13, f32[1024]{0:T(1024)S(1)} %copy-done.30, f32[1024]{0:T(1024)S(1)} %copy-done.28), kind=kOutput, calls=%fused_computation.24 | convolution fusion | flops 6449790976 | bytes 14688256 | tf_op jit(solution)/shard_map/td,ptc->pdc/dot_general | solution.py:418
  432.4 7.0 pad_maximum_fusion.2
  439.5 11.7 %copy.155 = bf16[2,1024,2048]{2,1,0:T(8,128)(2,1)} copy(bf16[2,1024,2048]{1,2,0:T(8,128)(2,1)} %pad_maximum_fusion.2) | data formatting | bytes 16777216 | tf_op jit(solution)/shard_map/concatenate | solution.py:419
  451.2 19.1 %fusion.10 = bf16[2,2816,1024]{1,2,0:T(8,128)(2,1)} fusion(bf16[2,1024,1408]{1,2,0:T(8,128)(2,1)} %get-tuple-element.112, bf16[2,1024,1408]{1,2,0:T(8,128)(2,1)} %get-tuple-element.113, f32[1024,1024]{0,1:T(8,128)} %get-tuple-element.126, f32[1024]{0:T(1024)S(1)} %copy-done.31, f32[1024]{0:T(1024)S(1)} %add_rsqrt_fusion), kind=kOutput, calls=%fused_computation.23 | convolution fusion | flops 11843141632 | bytes 27271168 | tf_op jit(solution)/shard_map/td,ptc->pdc/dot_general | solution.py:383
  473.1 6.3 fusion.34
  479.4 6.3 fusion.36
  489.4 6.3 collective-permute-done.2
  532.6 95.7 %reduce-scatter.4.cloned.1.call-done = bf16[64,2048]{1,0:T(8,128)(2,1)} async-done(((bf16[2048,2048]{1,0:T(8,128)(2,1)}), bf16[64,2048]{1,0:T(8,128)(2,1)}) %reduce-scatter.4.cloned.1.call-update) | async-done | bytes 262160 | tf_op jit(solution)/shard_map/reduce_scatter | solution.py:302
  632.4 150.0 %reduce-scatter.6.cloned.1.call-done = bf16[64,2816]{1,0:T(8,128)(2,1)} async-done(((bf16[2048,2816]{1,0:T(8,128)(2,1)}), bf16[64,2816]{1,0:T(8,128)(2,1)}) %reduce-scatter.6.cloned.1.call-update) | async-done | bytes 360464 | tf_op jit(solution)/shard_map/reduce_scatter | solution.py:302
  (164 shorter events, 106.8 us)
Async XLA Ops:
  7.2 76.5 %all-gather.5.cloned.1.call-start = ((), (), s32[]{:S(2)}) async-start(), calls=%async_computation.3 | async-start | bytes 6488064 | tf_op jit(solution)/shard_map/all_gather | solution.py:297
  8.8 132.8 %all-gather.7.cloned.1.call-start = ((), (), s32[]{:S(2)}) async-start(), calls=%async_computation.4 | async-start | bytes 2162688 | tf_op jit(solution)/shard_map/all_gather | solution.py:297
  9.6 225.6 %all-gather.9.cloned.1.call-start = ((), (), s32[]{:S(2)}) async-start(), calls=%async_computation.5 | async-start | bytes 11894784 | tf_op jit(solution)/shard_map/all_gather | solution.py:297
  11.4 292.1 %all-gather.11.cloned.1.call-start = ((), (), s32[]{:S(2)}) async-start(), calls=%async_computation.6 | async-start | bytes 5947392 | tf_op jit(solution)/shard_map/all_gather | solution.py:297
  12.0 518.9 %reduce-scatter.8.cloned.1.call-start = ((), (), s32[]{:S(2)}) async-start(), calls=%async_computation.9 | async-start | bytes 5947392 | tf_op jit(solution)/shard_map/reduce_scatter | solution.py:302
  14.9 80.5 %copy-start.11 = (bf16[1024,1024]{0,1:T(8,128)(2,1)}, bf16[1024,1024]{0,1:T(8,128)(2,1)S(1)}, u32[]{:S(2)}) copy-start(bf16[1024,1024]{0,1:T(8,128)(2,1)S(1)} %copy.128) | copy-start | bytes 6291460
  16.6 78.8 %copy-start.27 = (f32[1024]{0:T(1024)}, f32[1024]{0:T(1024)S(1)}, u32[]{:S(2)}) copy-start(f32[1024]{0:T(1024)S(1)} %add_rsqrt_fusion.1) | copy-start | bytes 12292
  83.7 11.7 %copy-start.8 = (f32[16,512]{1,0:T(8,128)S(1)}, f32[16,512]{1,0:T(8,128)}, u32[]{:S(2)}) copy-start(f32[16,512]{1,0:T(8,128)} %second_ref.3) | copy-start | bytes 98308
  83.7 11.7 %copy-start.10 = (f32[512]{0:T(512)S(1)}, f32[512]{0:T(512)}, u32[]{:S(2)}) copy-start(f32[512]{0:T(512)} %param.32) | copy-start | bytes 6148
  95.4 21.9 %copy-start.9 = (f32[256]{0:T(256)S(1)}, f32[256]{0:T(256)}, u32[]{:S(2)}) copy-start(f32[256]{0:T(256)} %param.33) | copy-start | bytes 3076
  108.0 9.3 %collective-permute-start = (bf16[4,128,256]{2,1,0:T(8,128)(2,1)S(1)}, bf16[4,128,256]{2,1,0:T(8,128)(2,1)S(1)}, u32[]{:S(2)}, u32[]{:S(2)}) collective-permute-start(bf16[4,128,256]{2,1,0:T(8,128)(2,1)S(1)} %convert_element_type.101), channel_id=1, source_target_pairs={{0,1},{2,3},{4,5},{6,7},{8,9},{10,11},{12,13},{14,15},{16,17},{18,... | collective-permute-start | bytes 786440 | tf_op jit(solution)/shard_map/ppermute | solution.py:354
  144.4 90.8 %copy-start.31 = (f32[1024]{0:T(1024)S(1)}, f32[1024]{0:T(1024)}, u32[]{:S(2)}) copy-start(f32[1024]{0:T(1024)} %param.29) | copy-start | bytes 12292
  303.6 22.3 %copy-start.20 = (bf16[1024,1024]{1,0:T(8,128)(2,1)S(1)}, bf16[1024,1024]{1,0:T(8,128)(2,1)}, u32[]{:S(2)}) copy-start(bf16[1024,1024]{1,0:T(8,128)(2,1)} %param.19) | copy-start | bytes 6291460
  336.6 291.7 %reduce-scatter.4.cloned.1.call-start = ((), (), s32[]{:S(2)}) async-start(), calls=%async_computation.7 | async-start | bytes 8650752 | tf_op jit(solution)/shard_map/reduce_scatter | solution.py:302
  353.3 12.0 %copy-start.18 = (bf16[1024,1024]{0,1:T(8,128)(2,1)S(1)}, bf16[1024,1024]{0,1:T(8,128)(2,1)}, u32[]{:S(2)}) copy-start(bf16[1024,1024]{0,1:T(8,128)(2,1)} %copy.139) | copy-start | bytes 6291460
  368.9 16.9 %copy-start.17 = (f32[1024,1024]{0,1:T(8,128)}, f32[1024,1024]{0,1:T(8,128)S(1)}, u32[]{:S(2)}) copy-start(f32[1024,1024]{0,1:T(8,128)S(1)} %multiply_add_fusion) | copy-start | bytes 12582916
  373.2 12.6 %copy-start.21 = (bf16[1024,1024]{0,1:T(8,128)(2,1)S(1)}, bf16[1024,1024]{0,1:T(8,128)(2,1)}, u32[]{:S(2)}) copy-start(bf16[1024,1024]{0,1:T(8,128)(2,1)} %copy.189) | copy-start | bytes 6291460
  384.5 12.3 %collective-permute-start.1 = (bf16[4,128,256]{2,1,0:T(8,128)(2,1)S(1)}, bf16[4,128,256]{2,1,0:T(8,128)(2,1)S(1)}, u32[]{:S(2)}, u32[]{:S(2)}) collective-permute-start(bf16[4,128,256]{2,1,0:T(8,128)(2,1)S(1)} %convert_element_type.113), channel_id=1, source_target_pairs={{1,0},{3,2},{5,4},{7,6},{9,8},{11,10},{13,12},{15,14},{17,16},{19,... | collective-permute-start | bytes 786440 | tf_op jit(solution)/shard_map/ppermute | solution.py:404
  451.1 331.3 %reduce-scatter.6.cloned.1.call-start = ((), (), s32[]{:S(2)}) async-start(), calls=%async_computation.8 | async-start | bytes 11894784 | tf_op jit(solution)/shard_map/reduce_scatter | solution.py:302
  489.3 6.3 collective-permute-start.2
  495.7 6.3 collective-permute-start.3
  502.0 9.4 %collective-permute-start.4 = (f32[214,128]{1,0:T(8,128)S(1)}, f32[214,128]{1,0:T(8,128)S(1)}, u32[]{:S(2)}, u32[]{:S(2)}) collective-permute-start(f32[214,128]{1,0:T(8,128)S(1)} %add.110), channel_id=1, source_target_pairs={{0,4},{2,6},{4,0},{6,2},{8,12},{10,14},{12,8},{14,10},{16,20},{18,... | collective-permute-start | bytes 328712 | tf_op jit(solution)/shard_map/ppermute | solution.py:310
  511.5 6.1 collective-permute-start.5
  517.6 9.9 %collective-permute-start.6 = (f32[214,128]{1,0:T(8,128)S(1)}, f32[214,128]{1,0:T(8,128)S(1)}, u32[]{:S(2)}, u32[]{:S(2)}) collective-permute-start(f32[214,128]{1,0:T(8,128)S(1)} %add.112), channel_id=1, source_target_pairs={{0,16},{2,18},{4,20},{6,22},{8,24},{10,26},{12,28},{14,30},{16,0},... | collective-permute-start | bytes 328712 | tf_op jit(solution)/shard_map/ppermute | solution.py:310
  (27 other events, 135.2 us)
Sparse Core Ops, SparseCore 0:
  11.5 72.2 all-gather.4
  86.6 55.0 all-gather.6
  145.1 89.9 all-gather.8
  237.9 65.5 all-gather.10
  336.7 143.1 reduce-scatter.7
  482.1 146.1 reduce-scatter.3
  630.7 151.7 reduce-scatter.5

commit v2 on v1

--- a/solution.py
+++ b/solution.py
@@ -49,7 +49,11 @@
     return h // 2, slice((h % 2) * width, (h % 2 + 1) * width)
 
 
-def gate_kernel(info, low_ref, second_ref, bias_ref, k_ref, v_ref, seg_ref, cum_ref, sig_ref, state_ref):
+def head_pick(h, first, second):
+    return (first if h % 2 == 0 else second)[h // 2]
+
+
+def gate_kernel(info, low_ref, second_ref, bias_ref, k_ref, v0_ref, v1_ref, seg_ref, cum_ref, sig_ref, state_ref):
     c = pl.program_id(0)
 
     @pl.when(c == 0)
@@ -73,14 +77,13 @@
     keep = jnp.exp(final) * retain
     for h in range(HEADS):
         p, kc = head_cols(h, KEY)
-        _, vc = head_cols(h, VAL)
         hk = slice(h * KEY, (h + 1) * KEY)
         kt = (k_ref[p, :, kc].astype(F32) * tail_decay[:, hk]).astype(BF16)
-        state_ref[h] = state_ref[h] * keep[:, hk].reshape(KEY, 1) + tn(kt, v_ref[p, :, vc])
+        state_ref[h] = state_ref[h] * keep[:, hk].reshape(KEY, 1) + tn(kt, head_pick(h, v0_ref, v1_ref))
 
 
 def core_kernel(
-    info, q_ref, k_ref, v_ref, og_ref, cum_ref, seg_ref, row_ref, first_ref, gain_ref,
+    info, q_ref, k_ref, v0_ref, v1_ref, og0_ref, og1_ref, cum_ref, seg_ref, row_ref, first_ref, gain_ref,
     mixed_ref, core_ref, states_ref, state,
 ):
     c = pl.program_id(0)
@@ -104,11 +107,10 @@
     keep = jnp.exp(final) * retain
     for h in range(HEADS):
         p, kc = head_cols(h, KEY)
-        _, vc = head_cols(h, VAL)
         hk = slice(h * KEY, (h + 1) * KEY)
         q = q_ref[p, :, kc].astype(F32) * SCALE
         k = k_ref[p, :, kc].astype(F32)
-        v = v_ref[p, :, vc]
+        v = head_pick(h, v0_ref, v1_ref)
         s = state[h]
         s_low = s.astype(BF16)
         states_ref[0, h] = s_low
@@ -117,14 +119,14 @@
         core = nn((q * whole[:, hk]).astype(BF16), s_low) + nn(scores, v)
         state[h] = s * keep[:, hk].reshape(KEY, 1) + tn((k * rest[:, hk]).astype(BF16), v)
         normed = core * lax.rsqrt(jnp.mean(core * core, axis=-1, keepdims=True) + 1.0)
-        og = og_ref[p, :, vc].astype(F32)
+        og = head_pick(h, og0_ref, og1_ref).astype(F32)
         hv = slice(h * VAL, (h + 1) * VAL)
         mixed_ref[:, hv] = (normed * gain_ref[...] * (og * jax.nn.sigmoid(og))).astype(BF16)
         core_ref[:, hv] = core.astype(BF16)
 
 
 def post_kernel(
-    info, dm_ref, core_ref, og_ref, q_ref, cum_ref, seg_ref, gain_ref,
+    info, dm_ref, core_ref, og0_ref, og1_ref, q_ref, cum_ref, seg_ref, gain_ref,
     dcore_ref, dog_ref, dgain_ref, dstate_ref, prefix,
 ):
     c = pl.program_id(0)
@@ -143,19 +145,18 @@
     total = jnp.zeros((1, VAL), F32)
     for h in range(HEADS):
         p, kc = head_cols(h, KEY)
-        _, vc = head_cols(h, VAL)
         hk = slice(h * KEY, (h + 1) * KEY)
         hv = slice(h * VAL, (h + 1) * VAL)
         core = core_ref[:, hv].astype(F32)
         scale = lax.rsqrt(jnp.mean(core * core, axis=-1, keepdims=True) + 1.0)
         normed = core * scale
-        og = og_ref[p, :, vc].astype(F32)
+        og = head_pick(h, og0_ref, og1_ref).astype(F32)
         sig = jax.nn.sigmoid(og)
         silu = og * sig
         dm = dm_ref[:, hv].astype(F32)
         both = dm * normed
         total += jnp.sum(both * silu, axis=0, keepdims=True)
-        dog_ref[p, :, vc] = (both * gain * (sig * (1.0 + og * (1.0 - sig)))).astype(BF16)
+        dog_ref[p, :, head_cols(h, VAL)[1]] = (both * gain * (sig * (1.0 + og * (1.0 - sig)))).astype(BF16)
         dn = dm * gain * silu
         dcore = scale * (dn - normed * jnp.mean(dn * normed, axis=-1, keepdims=True))
         dcore = dcore.astype(BF16)
@@ -166,8 +167,8 @@
 
 
 def back_kernel(
-    info, q_ref, k_ref, v_ref, cum_ref, sig_ref, states_ref, dcore_ref, seg_ref, row_ref,
-    first_ref, second_ref, low_ref, dqkv_ref, drank_ref, dsecond_ref, dbias_ref, dstate,
+    info, q_ref, k_ref, v0_ref, v1_ref, dog_ref, cum_ref, sig_ref, states_ref, dcore_ref, seg_ref, row_ref,
+    first_ref, second_ref, low_ref, da_ref, db_ref, drank_ref, dsecond_ref, dbias_ref, dstate,
 ):
     i = pl.program_id(0)
     c = pl.num_programs(0) - 1 - i
@@ -195,12 +196,11 @@
     logits = []
     for h in range(HEADS):
         p, kc = head_cols(h, KEY)
-        _, vc = head_cols(h, VAL)
         hk = slice(h * KEY, (h + 1) * KEY)
         hv = slice(h * VAL, (h + 1) * VAL)
         q = q_ref[p, :, kc].astype(F32) * SCALE
         k = k_ref[p, :, kc].astype(F32)
-        v = v_ref[p, :, vc]
+        v = head_pick(h, v0_ref, v1_ref)
         do = dcore_ref[:, hv]
         s = states_ref[0, h]
         ds = dstate[h]
@@ -231,9 +231,13 @@
         ddecay = split_sum(upper, dcum, 2) + dfinal
         dstate[h] = ds * kept + tn(q_whole, do)
         logits.append(ddecay * (sig_ref[:, hk].astype(F32) * (1.0 / 16.0)))
-        dqkv_ref[p, :, kc] = (dq * SCALE).astype(BF16)
-        dqkv_ref[p, :, slice(256 + kc.start, 256 + kc.stop)] = dk.astype(BF16)
-        dqkv_ref[p, :, slice(512 + vc.start, 512 + vc.stop)] = dv.astype(BF16)
+        da_ref[p, :, kc] = (dq * SCALE).astype(BF16)
+        da_ref[p, :, slice(256 + kc.start, 256 + kc.stop)] = dk.astype(BF16)
+        if h % 2 == 0:
+            da_ref[p, :, 512:] = dv.astype(BF16)
+        else:
+            db_ref[p, :, :256] = dv.astype(BF16)
+    db_ref[:, :, 256:] = dog_ref[...]
     dlogit = jnp.concatenate(logits, axis=1)
     dbias_ref[...] += jnp.sum(dlogit, axis=0, keepdims=True)
     low = dlogit.astype(BF16)
@@ -297,9 +301,78 @@
     return lax.all_gather(shard, ALL, axis=0, tiled=True).reshape(2, -1, shard.shape[1])
 
 
-def scatter(grad):
-    flat = grad.reshape(-1, grad.shape[-1])
-    return lax.psum_scatter(flat, ALL, scatter_dimension=0, tiled=True).astype(F32)
+def swap(x, stride):
+    if stride == 0:
+        return lax.ppermute(x, "tensor", [(0, 1), (1, 0)])
+    return lax.ppermute(x, "dp", [(i, i ^ stride) for i in range(lax.axis_size("dp"))])
+
+
+def own_bit(stride):
+    return lax.axis_index("tensor") if stride == 0 else (lax.axis_index("dp") // stride) % 2
+
+
+def long_strides():
+    strides, stride = [], 4
+    while stride < lax.axis_size("dp"):
+        strides.append(stride)
+        stride *= 2
+    return strides
+
+
+def grow(x, stride):
+    other = swap(x, stride)
+    return jnp.where(own_bit(stride) == 0, jnp.stack([x, other]), jnp.stack([other, x]))
+
+
+def gather_steps(shard, mid):
+    for stride in long_strides()[::-1] + list(mid) + [1]:
+        shard = grow(shard, stride)
+    steps = len(shard.shape) - 2
+    z = steps - 3
+    x_at, t_at = (2, 1) if mid[0] == 2 else (1, 2)
+    z_axes = list(range(3, 3 + z))[::-1]
+    order = [t_at] + z_axes + [x_at, 0, steps, steps + 1]
+    return shard.transpose(order).reshape(2, -1, shard.shape[-1])
+
+
+def by_core(act):
+    rows = act.shape[0]
+    z = len(long_strides())
+    own = act.shape[1] // lax.axis_size("dp")
+    split = act.reshape((rows,) + (2,) * (z + 2) + (own,))
+    split = split.transpose([0, z + 2, z + 1] + list(range(1, z + 1))[::-1] + [z + 3])
+    core = own_bit(1)
+    other = lax.dynamic_index_in_dim(split, 1 - core, 1, keepdims=False).reshape(rows, -1)
+    mine = lax.dynamic_index_in_dim(split, core, 1, keepdims=False).reshape(rows, -1)
+    return other, mine
+
+
+def halve(x, stride, axis):
+    bit = own_bit(stride)
+    send = lax.dynamic_index_in_dim(x, 1 - bit, axis, keepdims=False)
+    keep = lax.dynamic_index_in_dim(x, bit, axis, keepdims=False)
+    return keep + swap(send, stride)
+
+
+def scatter(parts, equation, act):
+    other, mine = by_core(act)
+    sent = [jnp.einsum(equation, other, part, preferred_element_type=F32).astype(BF16) for part in parts]
+    got = [swap(part, 1) for part in sent]
+    kept = [jnp.einsum(equation, mine, part, preferred_element_type=F32).astype(BF16) for part in parts]
+    kept = lax.optimization_barrier(kept)
+    done = []
+    for place, (x, extra) in enumerate(zip(kept, got)):
+        x = x + extra
+        cols = x.shape[-1]
+        x = x.reshape((2, 2) + (2,) * len(long_strides()) + (-1, cols))
+        if place % 2 == 0:
+            x = halve(halve(x, 2, 1), 0, 0)
+        else:
+            x = halve(halve(x, 0, 0), 2, 0)
+        for stride in long_strides():
+            x = halve(x, stride, 0)
+        done.append(x.astype(F32))
+    return done
 
 
 def total_sum(x):
@@ -330,14 +403,19 @@
     seg_row = segments[1:].reshape(blocks, 1, CHUNK)
     info = jnp.stack([segments[:-1].reshape(blocks, CHUNK)[:, 0], seg_row[:, 0, -1]])
 
-    w_in = gather(jnp.concatenate([query_weight, key_weight, value_weight, outgate_weight], axis=1))
-    w_out = gather(output_weight.T)
-    w_gu = gather(jnp.concatenate([gate_weight, up_weight], axis=1))
+    w_in_a = gather_steps(
+        jnp.concatenate([query_weight, key_weight, value_weight[:, :256]], axis=1), (2, 0)
+    )
+    w_in_b = gather_steps(jnp.concatenate([value_weight[:, 256:], outgate_weight], axis=1), (0, 2))
+    w_gu = gather(jnp.concatenate([gate_weight, up_weight, output_weight.T], axis=1))
+    w_out = w_gu[..., 2 * half :]
+    w_gu = w_gu[..., : 2 * half]
     w_down = gather(down_weight.T)
 
     resid = hidden_in.astype(F32)
     normed_a = (rms(resid, 1e-6) * mixer_gain).astype(BF16)
-    proj = jnp.einsum("td,pdc->ptc", normed_a, w_in, preferred_element_type=F32).astype(BF16)
+    proj_a = jnp.einsum("td,pdc->ptc", normed_a, w_in_a, preferred_element_type=F32).astype(BF16)
+    proj_b = jnp.einsum("td,pdc->ptc", normed_a, w_in_b, preferred_element_type=F32).astype(BF16)
     lowrank = jnp.dot(normed_a.astype(F32), low_first, precision=HIGHEST)
     gain = head_gain.reshape(1, VAL)
     p_spec, r_spec, f_spec, row_spec, s_spec = specs(blocks)
@@ -345,24 +423,25 @@
     cum, sig, final_state = call(
         gate_kernel,
         blocks,
-        [r_spec(16), f_spec(16, 512), f_spec(1, 512), p_spec(256, 1), p_spec(512, 1), r_spec(1)],
+        [r_spec(16), f_spec(16, 512), f_spec(1, 512), p_spec(256, 1), p_spec(256, 2),
+         p_spec(256, 0), r_spec(1)],
         [r_spec(512), r_spec(512), f_spec(HEADS, KEY, VAL)],
         [shape((rows, 512), F32), shape((rows, 512), BF16), state_f32],
         [],
         1 << 29,
-    )(info, lowrank, low_second, decay_bias.reshape(1, 512), proj, proj, seg)
+    )(info, lowrank, low_second, decay_bias.reshape(1, 512), proj_a, proj_a, proj_b, seg)
     state_in = lax.ppermute(final_state.astype(BF16), "tensor", [(0, 1)])
     mixed, core, states = call(
         core_kernel,
         blocks,
-        [p_spec(256, 0), p_spec(256, 1), p_spec(512, 1), p_spec(512, 2), r_spec(512), r_spec(1),
-         row_spec, f_spec(HEADS, KEY, VAL), f_spec(1, VAL)],
+        [p_spec(256, 0), p_spec(256, 1), p_spec(256, 2), p_spec(256, 0), p_spec(256, 1), p_spec(256, 2),
+         r_spec(512), r_spec(1), row_spec, f_spec(HEADS, KEY, VAL), f_spec(1, VAL)],
         [r_spec(1024), r_spec(1024), s_spec],
         [shape((rows, 1024), BF16), shape((rows, 1024), BF16),
          shape((blocks, HEADS, KEY, VAL), BF16)],
         [pltpu.VMEM((HEADS, KEY, VAL), F32)],
         1 << 30,
-    )(info, proj, proj, proj, proj, cum, seg, seg_row, state_in, gain)
+    )(info, proj_a, proj_a, proj_a, proj_b, proj_b, proj_b, cum, seg, seg_row, state_in, gain)
     middle = resid + nt(mixed[:, :512], w_out[0]) + nt(mixed[:, 512:], w_out[1])
 
     normed_b = (rms(middle, 1e-6) * feed_gain).astype(BF16)
@@ -374,53 +453,50 @@
     feed_out = nt(activ[0], w_down[0]) + nt(activ[1], w_down[1])
     block_out = (middle + feed_out).astype(BF16)
 
-    down_grad = jnp.einsum("to,ptc->poc", cotangent, activ, preferred_element_type=F32).astype(BF16)
-    own_down = scatter(down_grad)
+    own_down = scatter([activ[..., :768], activ[..., 768:]], "to,ptc->poc", cotangent)
     d_activ = jnp.einsum("to,poc->ptc", cotangent, w_down, preferred_element_type=F32)
     d_gate = (d_activ * up_pre * (sig_gate * (1.0 + gate_pre * (1.0 - sig_gate)))).astype(BF16)
     d_up = (d_activ * silu).astype(BF16)
+    own_gate, own_up = scatter([d_gate, d_up], "td,ptc->pdc", normed_b)
     d_pre = jnp.concatenate([d_gate, d_up], axis=-1)
-    gu_grad = jnp.einsum("td,ptc->pdc", normed_b, d_pre, preferred_element_type=F32).astype(BF16)
-    own_gu = scatter(gu_grad)
     d_normed_b = nt(d_pre[0], w_gu[0]) + nt(d_pre[1], w_gu[1])
     back, feed_gain_grad = rms_back(middle, feed_gain, 1e-6, d_normed_b)
     d_middle = cotangent.astype(F32) + back
     d_mix = d_middle.astype(BF16)
 
-    out_grad = jnp.einsum(
-        "to,tpc->poc", d_mix, mixed.reshape(rows, 2, 512), preferred_element_type=F32
-    ).astype(BF16)
+    mixed_split = mixed.reshape(rows, 2, 512).transpose(1, 0, 2)
+    own_out = scatter([mixed_split[..., :256], mixed_split[..., 256:]], "to,ptc->poc", d_mix)
     d_mixed = jnp.concatenate([nn(d_mix, w_out[0]), nn(d_mix, w_out[1])], axis=1).astype(BF16)
     d_core, d_og, head_gain_grad, d_state = call(
         post_kernel,
         blocks,
-        [r_spec(1024), r_spec(1024), p_spec(512, 2), p_spec(256, 0), r_spec(512), r_spec(1),
+        [r_spec(1024), r_spec(1024), p_spec(256, 1), p_spec(256, 2), p_spec(256, 0), r_spec(512), r_spec(1),
          f_spec(1, VAL)],
         [r_spec(1024), p_spec(512, 0), f_spec(1, VAL), f_spec(HEADS, KEY, VAL)],
         [shape((rows, 1024), BF16), shape((2, rows, 512), BF16), shape((1, VAL), F32), state_f32],
         [pltpu.VMEM((1, 512), F32)],
         1 << 29,
-    )(info, d_mixed, core, proj, proj, cum, seg, gain)
+    )(info, d_mixed, core, proj_b, proj_b, proj_a, cum, seg, gain)
     d_state_in = lax.ppermute(d_state.astype(BF16), "tensor", [(1, 0)])
     p_spec, r_spec, f_spec, row_spec, s_spec = specs(blocks, True)
-    d_qkv, d_rank, low_second_grad, bias_grad = call(
+    d_a, d_b, d_rank, low_second_grad, bias_grad = call(
         back_kernel,
         blocks,
-        [p_spec(256, 0), p_spec(256, 1), p_spec(512, 1), r_spec(512), r_spec(512), s_spec,
+        [p_spec(256, 0), p_spec(256, 1), p_spec(256, 2), p_spec(256, 0), p_spec(512, 0), r_spec(512), r_spec(512), s_spec,
          r_spec(1024), r_spec(1), row_spec, f_spec(HEADS, KEY, VAL), f_spec(16, 512), r_spec(16)],
-        [p_spec(1024, 0), r_spec(16), f_spec(16, 512), f_spec(1, 512)],
-        [shape((2, rows, 1024), BF16), shape((rows, 16), F32), shape((16, 512), F32),
+        [p_spec(768, 0), p_spec(768, 0), r_spec(16), f_spec(16, 512), f_spec(1, 512)],
+        [shape((2, rows, 768), BF16), shape((2, rows, 768), BF16), shape((rows, 16), F32), shape((16, 512), F32),
          shape((1, 512), F32)],
         [pltpu.VMEM((HEADS, KEY, VAL), F32)],
         3 << 30,
-    )(info, proj, proj, proj, cum, sig, states, d_core, seg, seg_row, d_state_in, low_second, lowrank)
-    d_proj = jnp.concatenate([d_qkv, d_og], axis=-1)
-    in_grad = jnp.einsum("td,ptc->pdc", normed_a, d_proj, preferred_element_type=F32).astype(BF16)
-    own_mix = scatter(jnp.concatenate([in_grad, out_grad], axis=-1))
+    )(info, proj_a, proj_a, proj_a, proj_b, d_og, cum, sig, states, d_core, seg, seg_row, d_state_in, low_second, lowrank)
+    own_a, own_b = scatter([d_a, d_b], "td,ptc->pdc", normed_a)
     low_first_grad = tn(normed_a, d_rank.astype(BF16))
     d_normed_a = (
-        nt(d_proj[0], w_in[0])
-        + nt(d_proj[1], w_in[1])
+        nt(d_a[0], w_in_a[0])
+        + nt(d_a[1], w_in_a[1])
+        + nt(d_b[0], w_in_b[0])
+        + nt(d_b[1], w_in_b[1])
         + nt(d_rank.astype(BF16), low_first.astype(BF16))
     )
     back, mixer_gain_grad = rms_back(resid, mixer_gain, 1e-6, d_normed_a)
@@ -438,20 +514,20 @@
     return (
         block_out,
         input_grad,
-        own_mix[:, :256],
-        own_mix[:, 256:512],
-        own_mix[:, 512:1024],
-        own_mix[:, 1024:1536],
-        own_mix[:, 1536:].T,
-        own_gu[:, :half],
-        own_gu[:, half:],
-        own_down.T,
+        own_a[:, :256],
+        own_a[:, 256:512],
+        jnp.concatenate([own_a[:, 512:], own_b[:, :256]], axis=1),
+        own_b[:, 256:],
+        jnp.concatenate([part.T for part in own_out], axis=0),
+        own_gate,
+        own_up,
+        jnp.concatenate([part.T for part in own_down], axis=0),
         *small,
     )
 
 
 def solution(mesh):
-    tokens = P(("dp", "tensor"), None)
+    tokens = P(("dp", "tensor"))
     split_in = P("dp", "tensor")
     split_out = P("tensor", "dp")
     weights = (split_in,) * 4 + (split_out,) + (split_in,) * 2 + (split_out,)

time: 800 us -> 623 us (0.78)
  waiting for transfers between devices: 486 us -> 179 us
  starting transfers between devices: 5.51 us -> 59.6 us
  other arithmetic: 25.1 us -> 66.4 us
  matrix products: 157 us -> 173 us
  local copies, waits for them, and re-layouts: 51.8 us -> 66.6 us
    reduce_scatter x3 -> x0, waiting for transfers between devices: 246 us -> none  [scatter(): lax.psum_scatter(flat, ALL, scatter_dimension=0, tiled=True).astype(F32)]
    all_gather x4 -> x2, waiting for transfers between devices: 214 us -> 30.5 us  [gather(): lax.all_gather(shard, ALL, axis=0, tiled=True)]
    ppermute x0 -> x50, waiting for transfers between devices: none -> 139 us  [the longest x40 129 us: swap(): lax.ppermute(x, 'dp', [(i, i ^ stride) for i in range(lax.axis_size('dp'))])]
    ppermute x0 -> x50, starting transfers between devices: none -> 46.7 us  [the longest x40 36.5 us: swap(): lax.ppermute(x, 'dp', [(i, i ^ stride) for i in range(lax.axis_size('dp'))])]
    add x1 -> x32, other arithmetic: 3.57 us -> 32.8 us  [the longest x8 21.7 us: scatter(): x = x + extra]
    add x0 -> x8, local copies, waits for them, and re-layouts: none -> 14.2 us  [scatter(): x = x + extra]
    concatenate x2 -> x0, local copies, waits for them, and re-layouts: 11.8 us -> none  [the longest x1 11.7 us: local(): own_mix = scatter(jnp.concatenate([in_grad, out_grad], axis=-1))]
    squeeze x0 -> x32, local copies, waits for them, and re-layouts: none -> 9.85 us  [halve(): send = lax.dynamic_index_in_dim(x, 1 - bit, axis, keepdims=False)]
  transfers between devices with their start and end apart: 14 -> 59, of which waited for: 10 -> 33; matrix products, arithmetic and copies ran while one was open for 24% -> 33% of each run, Pallas kernels for 6% -> 7%
where the time goes in v2:
time: 623 us; the launch traced here: 613 us
  waiting for transfers between devices  179 us (29%)
  matrix products  173 us (28%)
  local copies, waits for them, and re-layouts  66.6 us (11%)
  other arithmetic  66.4 us (11%)
  starting transfers between devices  59.6 us (10%)
  Pallas kernels  51.9 us (8%)
  between operations  16 us (3%)
    ppermute x40, waiting for transfers between devices, swap(): lax.ppermute(x, 'dp', [(i, i ^ stride) for i in range(lax.axis_size('dp'))])  129 us
    dot_general x11, matrix products, nt(): lax.dot_general(a, b, (((1,), (1,)), ((), ())), preferred_element_type=F32)  63.2 us
    ppermute x40, starting transfers between devices, swap(): lax.ppermute(x, 'dp', [(i, i ^ stride) for i in range(lax.axis_size('dp'))])  36.5 us
    all_gather x2, waiting for transfers between devices, gather(): lax.all_gather(shard, ALL, axis=0, tiled=True)  30.5 us
    unnamed x165, local copies, waits for them, and re-layouts  28.4 us
    dot_general x8, matrix products, scatter(): jnp.einsum(equation, mine, part, preferred_element_type=F32).astype(BF16)  26.6 us
    dot_general x8, matrix products, scatter(): jnp.einsum(equation, other, part, preferred_element_type=F32).astype(BF16)  26.1 us
    add x8, other arithmetic, scatter(): x = x + extra  21.7 us
  transfers between devices with their start and end apart: 59, of which 33 were waited for; matrix products, arithmetic and copies ran while one was open for 33% of the time, Pallas kernels for 7%

profile of v2, /device:TPU:0, one launch (start us, length us, event | category | flops | bytes accessed | tf_op | source)
XLA Modules:
  0.0 613.3 jit_solution(1988655065703236996)
XLA Ops:
  25.1 10.4 %collective-permute-done.6 = bf16[2,64,768]{2,1,0:T(8,128)(2,1)S(1)} collective-permute-done((bf16[2,64,768]{2,1,0:T(8,128)(2,1)S(1)}, bf16[2,64,768]{2,1,0:T(8,128)(2,1)S(1)}, u32[]{:S(2)}, u32[]{:S(2)}) %collective-permute-start.6) | collective-permute-done | bytes 196640 | tf_op jit(solution)/shard_map/ppermute | solution.py:307
  45.0 11.8 %collective-permute-done.2 = bf16[2,2,64,768]{3,2,0,1:T(8,128)(2,1)S(1)} collective-permute-done((bf16[2,2,64,768]{3,2,0,1:T(8,128)(2,1)S(1)}, bf16[2,2,64,768]{3,2,0,1:T(8,128)(2,1)S(1)}, u32[]{:S(2)}, u32[]{:S(2)}) %collective-permute-start.2) | collective-permute-done | bytes 393248 | tf_op jit(solution)/shard_map/ppermute | solution.py:307
  59.5 19.7 %collective-permute-done.8 = bf16[2,2,2,64,768]{4,3,2,1,0:T(8,128)(2,1)S(1)} collective-permute-done((bf16[2,2,2,64,768]{4,3,2,1,0:T(8,128)(2,1)S(1)}, bf16[2,2,2,64,768]{4,3,2,1,0:T(8,128)(2,1)S(1)}, u32[]{:S(2)}, u32[]{:S(2)}) %collective-permute-start.8) | collective-permute-done | bytes 786464 | tf_op jit(solution)/shard_map/ppermute | solution.py:307
  103.9 5.4 convert_bitcast_fusion.2.k_ref.v0_ref.q_ref
  109.3 10.3 %shard_map.288 = (f32[1024,512]{1,0:T(8,128)S(1)}, bf16[1024,512]{1,0:T(8,128)(2,1)S(1)}, f32[4,128,256]{2,1,0:T(8,128)S(1)}) custom-call(s32[2,8]{1,0:T(2,128)S(1)} %pad_add_fusion.info, f32[1024,16]{1,0:T(8,128)S(1)} %fusion.139.low_ref, f32[16,512]{1,0:T(8,128)S(1)} %copy-done.8, f32[1,512]{1,0:T(1,128)S(1)} %bitcast.465, ...), custom_call_target="tpu_custom_call" | custom-call | flops 536870912 | bytes 16777216 | tf_op jit(solution)/shard_map/pallas_call | solution.py:423
  129.8 10.6 %shard_map.289 = (bf16[1024,1024]{1,0:T(8,128)(2,1)S(1)}, bf16[1024,1024]{1,0:T(8,128)(2,1)S(1)}, bf16[8,4,128,256]{3,2,1,0:T(8,128)(2,1)}) custom-call(s32[2,8]{1,0:T(2,128)S(1)} %pad_add_fusion.info, bf16[2,1024,768]{2,1,0:T(8,128)(2,1)} %convert_bitcast_fusion.2.k_ref.v0_ref.q_ref, bf16[2,1024,768]{2,1,0:T(8,128)(2,1)} %convert_bitcast_fusion.2.k_ref.v0_ref.q_ref, ...), custom_call_target="tpu_custom_call" | custom-call | flops 1073741824 | bytes 16777216 | tf_op jit(solution)/shard_map/pallas_call | solution.py:434
  152.2 19.0 %convert_bitcast_fusion = bf16[2,1024,2816]{1,2,0:T(8,128)(2,1)} fusion(bf16[2,1024,3328]{2,1,0:T(8,128)(2,1)} %bitcast.537, bf16[1024,1024]{0,1:T(8,128)(2,1)S(1)} %multiply_convert_fusion), kind=kOutput, calls=%fused_computation.19 | convolution fusion | flops 11816927232 | bytes 25165824 | tf_op jit(solution)/shard_map/td,pdc->ptc/dot_general | solution.py:448
  171.2 30.5 %all-gather.5.cloned.1.call-done = bf16[2048,1408]{1,0:T(8,128)(2,1)} async-done(((bf16[64,1408]{1,0:T(8,128)(2,1)}), bf16[2048,1408]{1,0:T(8,128)(2,1)}) %all-gather.5.cloned.1.call-update) | async-done | bytes 5767184 | tf_op jit(solution)/shard_map/all_gather | solution.py:301
  201.6 19.6 %fusion.10 = (bf16[2,1024,1408]{1,2,0:T(8,128)(2,1)}, bf16[2,1024,1408]{1,2,0:T(8,128)(2,1)S(1)}, bf16[2,1024,1408]{1,2,0:T(8,128)(2,1)}) fusion(bf16[2,1024,2816]{1,2,0:T(8,128)(2,1)} %convert_bitcast_fusion, bf16[2,1024,1408]{2,1,0:T(8,128)(2,1)} %bitcast.548, bf16[1024,1024]{1,0:T(8,128)(2,1)} %param.19), kind=kOutput, calls=%fused_computation.18 | convolution fusion | flops 5954600960 | bytes 36700160 | tf_op jit(solution)/shard_map/to,poc->ptc/dot_general | solution.py:457
  223.7 10.9 %fusion.19 = f32[1024,1024]{0,1:T(8,128)} fusion(bf16[2,1024,1408]{1,2,0:T(8,128)(2,1)S(1)} %get-tuple-element.131, bf16[2,1024,1408]{1,2,0:T(8,128)(2,1)} %get-tuple-element.130, bf16[2,1024,3328]{2,1,0:T(8,128)(2,1)} %bitcast.538), kind=kOutput, calls=%fused_computation.29 | convolution fusion | flops 5917114368 | bytes 21495808 | tf_op jit(solution)/shard_map/dot_general | solution.py:25
  234.6 11.5 %multiply_reduce_fusion = (f32[1024]{0:T(1024)S(1)}, f32[1024]{0:T(1024)S(1)}, f32[1024,1024]{0,1:T(8,128)S(1)}) fusion(f32[1024,1024]{0,1:T(8,128)S(1)} %copy-done.21, f32[1024]{0:T(1024)S(1)} %add_rsqrt_fusion, f32[1024]{0:T(1024)S(1)} %copy-done.59, f32[1024,1024]{0,1:T(8,128)} %fusion.19, bf16[2,1024,1408]{1,2,0:T(8,128)(2,1)} %get-tuple-element.130, ...), kind=kOutput, calls=%fused_computation.45 | convolution fusion | flops 5924452352 | bytes 29900800 | tf_op jit(solution)/shard_map/dot_general | solution.py:25
  294.1 10.1 %shard_map.290 = (bf16[1024,1024]{1,0:T(8,128)(2,1)S(1)}, bf16[2,1024,512]{2,1,0:T(8,128)(2,1)S(1)}, f32[1,256]{1,0:T(1,128)S(1)}, f32[4,128,256]{2,1,0:T(8,128)S(1)}) custom-call(s32[2,8]{1,0:T(2,128)S(1)} %copy-done.13, bf16[1024,1024]{1,0:T(8,128)(2,1)} %pad_maximum_fusion.1.dm_ref, bf16[1024,1024]{1,0:T(8,128)(2,1)} %copy-done.3, ...), custom_call_target="tpu_custom_call" | custom-call | flops 536870912 | bytes 16777216 | tf_op jit(solution)/shard_map/pallas_call | solution.py:470
  307.7 5.2 fusion.39
  323.0 20.9 %shard_map.291 = (bf16[2,1024,768]{2,1,0:T(8,128)(2,1)}, bf16[2,1024,768]{2,1,0:T(8,128)(2,1)}, f32[1024,16]{1,0:T(8,128)S(1)}, f32[16,512]{1,0:T(8,128)S(1)}, f32[1,512]{1,0:T(1,128)S(1)}) custom-call(s32[2,8]{1,0:T(2,128)S(1)} %copy-done.13, bf16[2,1024,768]{2,1,0:T(8,128)(2,1)} %convert_bitcast_fusion.2.k_ref.v0_ref.q_ref, ...), custom_call_target="tpu_custom_call" | custom-call | flops 3221225472 | bytes 16777216 | tf_op jit(solution)/shard_map/pallas_call | solution.py:482
  343.9 5.5 fusion.76
  362.5 8.4 %fusion.31 = (f32[1024]{0:T(1024)S(1)}, f32[1024]{0:T(1024)S(1)}, f32[1024,1024]{0,1:T(8,128)}) fusion(bf16[1024,1024]{0,1:T(8,128)(2,1)S(1)} %copy-done.19, f32[1024]{0:T(1024)S(1)} %copy-done.58, f32[1024]{0:T(1024)S(1)} %copy-done.61, f32[1024,16]{0,1:T(8,128)S(1)} %copy-done.56, f32[1024,16]{1,0:T(8,128)} %copy-done.5, f32[1024,1024]{0,1:T(8,128)} %fusion.72, ...), kind=kOutput, calls=%fused_computation.42 | convolution fusion | flops 45119488 | bytes 23216128 | tf_op jit(solution)/shard_map/dot_general | solution.py:25
  378.8 5.9 fusion.30
  394.7 5.2 fusion.86
  411.7 7.6 %collective-permute-done.28 = bf16[2,2,2,64,256]{4,3,2,1,0:T(8,128)(2,1)S(1)} collective-permute-done((bf16[2,2,2,64,256]{4,3,2,1,0:T(8,128)(2,1)S(1)}, bf16[2,2,2,64,256]{4,3,2,1,0:T(8,128)(2,1)S(1)}, u32[]{:S(2)}, u32[]{:S(2)}) %collective-permute-start.28) | collective-permute-done | bytes 262176 | tf_op jit(solution)/shard_map/ppermute | solution.py:306
  421.4 5.9 collective-permute-done.56
  481.7 5.8 collective-permute-done.49
  558.1 9.1 %collective-permute-done.33 = bf16[2,2,2,64,1408]{4,3,2,1,0:T(8,128)(2,1)S(1)} collective-permute-done((bf16[2,2,2,64,1408]{4,3,2,1,0:T(8,128)(2,1)S(1)}, bf16[2,2,2,64,1408]{4,3,2,1,0:T(8,128)(2,1)S(1)}, u32[]{:S(2)}, u32[]{:S(2)}) %collective-permute-start.33) | collective-permute-done | bytes 1441824 | tf_op jit(solution)/shard_map/ppermute | solution.py:307
  568.6 10.1 %collective-permute-done.39 = bf16[2,2,64,1408]{3,2,1,0:T(8,128)(2,1)S(1)} collective-permute-done((bf16[2,2,64,1408]{3,2,1,0:T(8,128)(2,1)S(1)}, bf16[2,2,64,1408]{3,2,1,0:T(8,128)(2,1)S(1)}, u32[]{:S(2)}, u32[]{:S(2)}) %collective-permute-start.39) | collective-permute-done | bytes 720928 | tf_op jit(solution)/shard_map/ppermute | solution.py:307
  581.1 10.0 %collective-permute-done.40 = bf16[2,64,1408]{2,1,0:T(8,128)(2,1)S(1)} collective-permute-done((bf16[2,64,1408]{2,1,0:T(8,128)(2,1)S(1)}, bf16[2,64,1408]{2,1,0:T(8,128)(2,1)S(1)}, u32[]{:S(2)}, u32[]{:S(2)}) %collective-permute-start.40) | collective-permute-done | bytes 360480 | tf_op jit(solution)/shard_map/ppermute | solution.py:307
  (469 shorter events, 327.8 us)
Async XLA Ops:
  7.2 137.1 %all-gather.3.cloned.1.call-start = ((), (), s32[]{:S(2)}) async-start(), calls=%async_computation | async-start | bytes 14057472 | tf_op jit(solution)/shard_map/all_gather | solution.py:301
  9.1 192.5 %all-gather.5.cloned.1.call-start = ((), (), s32[]{:S(2)}) async-start(), calls=%async_computation.1 | async-start | bytes 5947392 | tf_op jit(solution)/shard_map/all_gather | solution.py:301
  24.1 16.9 %collective-permute-start.1 = (bf16[2,64,768]{2,1,0:T(8,128)(2,1)S(1)}, bf16[2,64,768]{2,1,0:T(8,128)(2,1)S(1)}, u32[]{:S(2)}, u32[]{:S(2)}) collective-permute-start(bf16[2,64,768]{2,1,0:T(8,128)(2,1)S(1)} %maximum_select_fusion.11), channel_id=1, source_target_pairs={{0,8},{2,10},{4,12},{6,14},{8,0},{10,2},{12,4},{14,6},{16,24},{18,... | collective-permute-start | bytes 589832 | tf_op jit(solution)/shard_map/ppermute | solution.py:307
  43.6 35.5 %collective-permute-start.8 = (bf16[2,2,2,64,768]{4,3,2,1,0:T(8,128)(2,1)S(1)}, bf16[2,2,2,64,768]{4,3,2,1,0:T(8,128)(2,1)S(1)}, u32[]{:S(2)}, u32[]{:S(2)}) collective-permute-start(bf16[2,2,2,64,768]{4,3,2,1,0:T(8,128)(2,1)S(1)} %maximum_select_fusion.7), channel_id=1, source_target_pairs={{0,4},{2,6},{4,0},{6,2},{8,12},{10,14},{12,8},{14,10},{16,20},{18,... | collective-permute-start | bytes 2359304 | tf_op jit(solution)/shard_map/ppermute | solution.py:307
  56.9 23.7 %collective-permute-start.3 = (bf16[2,2,2,64,768]{4,3,0,1,2:T(8,128)(2,1)S(1)}, bf16[2,2,2,64,768]{4,3,0,1,2:T(8,128)(2,1)S(1)}, u32[]{:S(2)}, u32[]{:S(2)}) collective-permute-start(bf16[2,2,2,64,768]{4,3,0,1,2:T(8,128)(2,1)S(1)} %maximum_select_fusion.5), channel_id=1, source_target_pairs={{0,1},{1,0},{2,3},{3,2},{4,5},{5,4},{6,7},{7,6},{8,9},{9,8},{10,11... | collective-permute-start | bytes 2359304 | tf_op jit(solution)/shard_map/ppermute | solution.py:306
  306.6 149.5 %collective-permute-start.42 = (bf16[2,512,768]{1,2,0:T(8,128)(2,1)}, bf16[2,512,768]{1,2,0:T(8,128)(2,1)}, u32[]{:S(2)}, u32[]{:S(2)}) collective-permute-start(bf16[2,512,768]{1,2,0:T(8,128)(2,1)} %fusion.88), channel_id=1, source_target_pairs={{0,2},{2,0},{4,6},{6,4},{8,10},{10,8},{12,14},{14,12},{16,18},{18,... | collective-permute-start | bytes 4718600 | tf_op jit(solution)/shard_map/ppermute | solution.py:307
  306.9 139.6 %collective-permute-start.47 = (bf16[2,512,640]{1,2,0:T(8,128)(2,1)}, bf16[2,512,640]{1,2,0:T(8,128)(2,1)}, u32[]{:S(2)}, u32[]{:S(2)}) collective-permute-start(bf16[2,512,640]{1,2,0:T(8,128)(2,1)} %fusion.94), channel_id=1, source_target_pairs={{0,2},{2,0},{4,6},{6,4},{8,10},{10,8},{12,14},{14,12},{16,18},{18,... | collective-permute-start | bytes 3932168 | tf_op jit(solution)/shard_map/ppermute | solution.py:307
  307.1 85.3 %collective-permute-start.22 = (bf16[2,512,256]{1,2,0:T(8,128)(2,1)}, bf16[2,512,256]{1,2,0:T(8,128)(2,1)}, u32[]{:S(2)}, u32[]{:S(2)}) collective-permute-start(bf16[2,512,256]{1,2,0:T(8,128)(2,1)} %fusion.104), channel_id=1, source_target_pairs={{0,2},{2,0},{4,6},{6,4},{8,10},{10,8},{12,14},{14,12},{16,18},{18,... | collective-permute-start | bytes 1572872 | tf_op jit(solution)/shard_map/ppermute | solution.py:307
  307.4 95.0 %collective-permute-start.27 = (bf16[2,512,256]{1,2,0:T(8,128)(2,1)}, bf16[2,512,256]{1,2,0:T(8,128)(2,1)}, u32[]{:S(2)}, u32[]{:S(2)}) collective-permute-start(bf16[2,512,256]{1,2,0:T(8,128)(2,1)} %fusion.105), channel_id=1, source_target_pairs={{0,2},{2,0},{4,6},{6,4},{8,10},{10,8},{12,14},{14,12},{16,18},{18,... | collective-permute-start | bytes 1572872 | tf_op jit(solution)/shard_map/ppermute | solution.py:307
  371.0 16.9 %collective-permute-start.52 = (f32[214,128]{1,0:T(8,128)S(1)}, f32[214,128]{1,0:T(8,128)S(1)}, u32[]{:S(2)}, u32[]{:S(2)}) collective-permute-start(f32[214,128]{1,0:T(8,128)S(1)} %concatenate.264), channel_id=1, source_target_pairs={{0,1},{1,0},{2,3},{3,2},{4,5},{5,4},{6,7},{7,6},{8,9},{9,8},{10,11... | collective-permute-start | bytes 328712 | tf_op jit(solution)/shard_map/ppermute | solution.py:379
  402.4 64.8 %collective-permute-start.17 = (bf16[2,512,768]{1,2,0:T(8,128)(2,1)}, bf16[2,512,768]{1,2,0:T(8,128)(2,1)}, u32[]{:S(2)}, u32[]{:S(2)}) collective-permute-start(bf16[2,512,768]{1,2,0:T(8,128)(2,1)} %fusion.87), channel_id=1, source_target_pairs={{0,2},{2,0},{4,6},{6,4},{8,10},{10,8},{12,14},{14,12},{16,18},{18,... | collective-permute-start | bytes 4718600 | tf_op jit(solution)/shard_map/ppermute | solution.py:307
  410.5 62.4 %collective-permute-start.12 = (bf16[2,512,768]{1,2,0:T(8,128)(2,1)}, bf16[2,512,768]{1,2,0:T(8,128)(2,1)}, u32[]{:S(2)}, u32[]{:S(2)}) collective-permute-start(bf16[2,512,768]{1,2,0:T(8,128)(2,1)} %fusion.86), channel_id=1, source_target_pairs={{0,2},{2,0},{4,6},{6,4},{8,10},{10,8},{12,14},{14,12},{16,18},{18,... | collective-permute-start | bytes 4718600 | tf_op jit(solution)/shard_map/ppermute | solution.py:307
  456.0 56.1 %collective-permute-start.37 = (bf16[2,512,1408]{1,2,0:T(8,128)(2,1)}, bf16[2,512,1408]{1,2,0:T(8,128)(2,1)}, u32[]{:S(2)}, u32[]{:S(2)}) collective-permute-start(bf16[2,512,1408]{1,2,0:T(8,128)(2,1)} %fusion.37), channel_id=1, source_target_pairs={{0,2},{2,0},{4,6},{6,4},{8,10},{10,8},{12,14},{14,12},{16,18},{18,... | collective-permute-start | bytes 8650760 | tf_op jit(solution)/shard_map/ppermute | solution.py:307
  460.3 29.5 %collective-permute-start.43 = (bf16[2,2,2,64,768]{4,3,2,1,0:T(8,128)(2,1)}, bf16[2,2,2,64,768]{4,3,2,1,0:T(8,128)(2,1)}, u32[]{:S(2)}, u32[]{:S(2)}) collective-permute-start(bf16[2,2,2,64,768]{4,3,2,1,0:T(8,128)(2,1)} %dynamic-slice_bitcast_fusion.4), channel_id=1, source_target_pairs={{0,4},{2,6},{4,0},{6,2},{8,12},{10,14},{12,8},{14,10},{16,20},{18,... | collective-permute-start | bytes 2359304 | tf_op jit(solution)/shard_map/ppermute | solution.py:307
  465.3 22.2 %collective-permute-start.49 = (bf16[2,2,64,640]{3,2,1,0:T(8,128)(2,1)}, bf16[2,2,64,640]{3,2,1,0:T(8,128)(2,1)S(1)}, u32[]{:S(2)}, u32[]{:S(2)}) collective-permute-start(bf16[2,2,64,640]{3,2,1,0:T(8,128)(2,1)} %dynamic-slice_bitcast_fusion.15), channel_id=1, source_target_pairs={{0,4},{2,6},{4,0},{6,2},{8,12},{10,14},{12,8},{14,10},{16,20},{18,... | collective-permute-start | bytes 983048 | tf_op jit(solution)/shard_map/ppermute | solution.py:307
  467.2 55.0 %collective-permute-start.32 = (bf16[2,512,1408]{1,2,0:T(8,128)(2,1)}, bf16[2,512,1408]{1,2,0:T(8,128)(2,1)}, u32[]{:S(2)}, u32[]{:S(2)}) collective-permute-start(bf16[2,512,1408]{1,2,0:T(8,128)(2,1)} %fusion.36), channel_id=1, source_target_pairs={{0,2},{2,0},{4,6},{6,4},{8,10},{10,8},{12,14},{14,12},{16,18},{18,... | collective-permute-start | bytes 8650760 | tf_op jit(solution)/shard_map/ppermute | solution.py:307
  472.9 29.3 %collective-permute-start.18 = (bf16[2,2,2,64,768]{4,3,2,1,0:T(8,128)(2,1)}, bf16[2,2,2,64,768]{4,3,2,1,0:T(8,128)(2,1)}, u32[]{:S(2)}, u32[]{:S(2)}) collective-permute-start(bf16[2,2,2,64,768]{4,3,2,1,0:T(8,128)(2,1)} %dynamic-slice_bitcast_fusion.5), channel_id=1, source_target_pairs={{0,1},{1,0},{2,3},{3,2},{4,5},{5,4},{6,7},{7,6},{8,9},{9,8},{10,11... | collective-permute-start | bytes 2359304 | tf_op jit(solution)/shard_map/ppermute | solution.py:306
  487.5 20.4 %collective-permute-start.13 = (bf16[2,2,2,64,768]{4,3,2,1,0:T(8,128)(2,1)S(1)}, bf16[2,2,2,64,768]{4,3,2,1,0:T(8,128)(2,1)S(1)}, u32[]{:S(2)}, u32[]{:S(2)}) collective-permute-start(bf16[2,2,2,64,768]{4,3,2,1,0:T(8,128)(2,1)S(1)} %dynamic-slice_bitcast_fusion.6), channel_id=1, source_target_pairs={{0,4},{2,6},{4,0},{6,2},{8,12},{10,14},{12,8},{14,10},{16,20},{18,... | collective-permute-start | bytes 2359304 | tf_op jit(solution)/shard_map/ppermute | solution.py:307
  504.3 31.3 %collective-permute-start.19 = (bf16[2,2,64,768]{3,2,1,0:T(8,128)(2,1)}, bf16[2,2,64,768]{3,2,1,0:T(8,128)(2,1)}, u32[]{:S(2)}, u32[]{:S(2)}) collective-permute-start(bf16[2,2,64,768]{3,2,1,0:T(8,128)(2,1)} %dynamic-slice_bitcast_fusion.11), channel_id=1, source_target_pairs={{0,4},{2,6},{4,0},{6,2},{8,12},{10,14},{12,8},{14,10},{16,20},{18,... | collective-permute-start | bytes 1179656 | tf_op jit(solution)/shard_map/ppermute | solution.py:307
  509.0 29.3 %collective-permute-start.14 = (bf16[2,2,64,768]{3,2,1,0:T(8,128)(2,1)}, bf16[2,2,64,768]{3,2,1,0:T(8,128)(2,1)}, u32[]{:S(2)}, u32[]{:S(2)}) collective-permute-start(bf16[2,2,64,768]{3,2,1,0:T(8,128)(2,1)} %dynamic-slice_bitcast_fusion.12), channel_id=1, source_target_pairs={{0,1},{1,0},{2,3},{3,2},{4,5},{5,4},{6,7},{7,6},{8,9},{9,8},{10,11... | collective-permute-start | bytes 1179656 | tf_op jit(solution)/shard_map/ppermute | solution.py:306
  510.9 23.0 %collective-permute-start.45 = (bf16[2,64,768]{2,1,0:T(8,128)(2,1)S(1)}, bf16[2,64,768]{2,1,0:T(8,128)(2,1)}, u32[]{:S(2)}, u32[]{:S(2)}) collective-permute-start(bf16[2,64,768]{2,1,0:T(8,128)(2,1)S(1)} %dynamic-slice_bitcast_fusion.18), channel_id=1, source_target_pairs={{0,8},{2,10},{4,12},{6,14},{8,0},{10,2},{12,4},{14,6},{16,24},{18,... | collective-permute-start | bytes 589832 | tf_op jit(solution)/shard_map/ppermute | solution.py:307
  520.9 34.8 %collective-permute-start.38 = (bf16[2,2,2,64,1408]{4,3,2,1,0:T(8,128)(2,1)}, bf16[2,2,2,64,1408]{4,3,2,1,0:T(8,128)(2,1)}, u32[]{:S(2)}, u32[]{:S(2)}) collective-permute-start(bf16[2,2,2,64,1408]{4,3,2,1,0:T(8,128)(2,1)} %dynamic-slice_bitcast_fusion), channel_id=1, source_target_pairs={{0,1},{1,0},{2,3},{3,2},{4,5},{5,4},{6,7},{7,6},{8,9},{9,8},{10,11... | collective-permute-start | bytes 4325384 | tf_op jit(solution)/shard_map/ppermute | solution.py:306
  532.6 34.6 %collective-permute-start.33 = (bf16[2,2,2,64,1408]{4,3,2,1,0:T(8,128)(2,1)S(1)}, bf16[2,2,2,64,1408]{4,3,2,1,0:T(8,128)(2,1)S(1)}, u32[]{:S(2)}, u32[]{:S(2)}) collective-permute-start(bf16[2,2,2,64,1408]{4,3,2,1,0:T(8,128)(2,1)S(1)} %dynamic-slice_bitcast_fusion.1), channel_id=1, source_target_pairs={{0,4},{2,6},{4,0},{6,2},{8,12},{10,14},{12,8},{14,10},{16,20},{18,... | collective-permute-start | bytes 4325384 | tf_op jit(solution)/shard_map/ppermute | solution.py:307
  557.3 21.4 %collective-permute-start.39 = (bf16[2,2,64,1408]{3,2,1,0:T(8,128)(2,1)S(1)}, bf16[2,2,64,1408]{3,2,1,0:T(8,128)(2,1)S(1)}, u32[]{:S(2)}, u32[]{:S(2)}) collective-permute-start(bf16[2,2,64,1408]{3,2,1,0:T(8,128)(2,1)S(1)} %dynamic-slice_bitcast_fusion.7), channel_id=1, source_target_pairs={{0,4},{2,6},{4,0},{6,2},{8,12},{10,14},{12,8},{14,10},{16,20},{18,... | collective-permute-start | bytes 2162696 | tf_op jit(solution)/shard_map/ppermute | solution.py:307
  (112 other events, 830.6 us)
Sparse Core Ops, SparseCore 0:
  10.9 122.2 all-gather.2
  136.2 65.4 all-gather.4

commit v3 on v2

--- a/solution.py
+++ b/solution.py
@@ -347,40 +347,55 @@
     return other, mine
 
 
-def halve(x, stride, axis):
-    bit = own_bit(stride)
-    send = lax.dynamic_index_in_dim(x, 1 - bit, axis, keepdims=False)
-    keep = lax.dynamic_index_in_dim(x, bit, axis, keepdims=False)
-    return keep + swap(send, stride)
-
-
-def scatter(parts, equation, act):
-    other, mine = by_core(act)
-    sent = [jnp.einsum(equation, other, part, preferred_element_type=F32).astype(BF16) for part in parts]
-    got = [swap(part, 1) for part in sent]
-    kept = [jnp.einsum(equation, mine, part, preferred_element_type=F32).astype(BF16) for part in parts]
-    kept = lax.optimization_barrier(kept)
-    done = []
-    for place, (x, extra) in enumerate(zip(kept, got)):
-        x = x + extra
-        cols = x.shape[-1]
-        x = x.reshape((2, 2) + (2,) * len(long_strides()) + (-1, cols))
-        if place % 2 == 0:
-            x = halve(halve(x, 2, 1), 0, 0)
-        else:
-            x = halve(halve(x, 0, 0), 2, 0)
-        for stride in long_strides():
-            x = halve(x, stride, 0)
-        done.append(x.astype(F32))
-    return done
+def fence(*values):
+    return lax.optimization_barrier(values)
+
+
+def during(sends, work, *inputs):
+    arrays, inputs = fence([array for array, _ in sends], inputs)
+    got = [swap(array, stride) for array, (_, stride) in zip(arrays, sends)]
+    return fence(work(*inputs), got)
+
+
+def products(equation, act, parts):
+    return [jnp.einsum(equation, act, part, preferred_element_type=F32).astype(BF16) for part in parts]
+
+
+class Halving:
+    def __init__(self, parts, got, firsts):
+        self.orders = [[2, 0] if first == 2 else [0, 2] for first in firsts]
+        self.orders = [order + long_strides() for order in self.orders]
+        self.parts = [
+            (part + extra).reshape((2, 2) + (2,) * len(long_strides()) + (-1, part.shape[-1]))
+            for part, extra in zip(parts, got)
+        ]
+
+    def sends(self):
+        self.kept, out = [], []
+        for i, part in enumerate(self.parts):
+            stride = self.orders[i][0]
+            axis = 1 if stride == 2 and len(self.orders[i]) == len(long_strides()) + 2 else 0
+            bit = own_bit(stride)
+            self.kept.append(lax.dynamic_index_in_dim(part, bit, axis, keepdims=False))
+            out.append((lax.dynamic_index_in_dim(part, 1 - bit, axis, keepdims=False), stride))
+        return out
+
+    def receive(self, got):
+        self.parts = [kept + extra for kept, extra in zip(self.kept, got)]
+        self.orders = [order[1:] for order in self.orders]
+
+    def finish(self):
+        while self.orders[0]:
+            sends = self.sends()
+            self.receive([swap(array, stride) for array, stride in sends])
+        return [part.astype(F32) for part in self.parts]
 
 
 def total_sum(x):
-    x = x + lax.ppermute(x, "tensor", [(0, 1), (1, 0)])
-    n = lax.axis_size("dp")
+    x = x + swap(x, 0)
     stride = 1
-    while stride < n:
-        x = x + lax.ppermute(x, "dp", [(i, i ^ stride) for i in range(n)])
+    while stride < lax.axis_size("dp"):
+        x = x + swap(x, stride)
         stride *= 2
     return x
 
@@ -407,15 +422,18 @@
         jnp.concatenate([query_weight, key_weight, value_weight[:, :256]], axis=1), (2, 0)
     )
     w_in_b = gather_steps(jnp.concatenate([value_weight[:, 256:], outgate_weight], axis=1), (0, 2))
-    w_gu = gather(jnp.concatenate([gate_weight, up_weight, output_weight.T], axis=1))
-    w_out = w_gu[..., 2 * half :]
-    w_gu = w_gu[..., : 2 * half]
-    w_down = gather(down_weight.T)
+    w_rest = gather(
+        jnp.concatenate([gate_weight, up_weight, output_weight.T, down_weight.T], axis=1)
+    )
+    w_gu, w_out = w_rest[..., : 2 * half], w_rest[..., 2 * half : 2 * half + 512]
+    w_down = w_rest[..., 2 * half + 512 :]
 
     resid = hidden_in.astype(F32)
     normed_a = (rms(resid, 1e-6) * mixer_gain).astype(BF16)
     proj_a = jnp.einsum("td,pdc->ptc", normed_a, w_in_a, preferred_element_type=F32).astype(BF16)
-    proj_b = jnp.einsum("td,pdc->ptc", normed_a, w_in_b, preferred_element_type=F32).astype(BF16)
+    proj_v = jnp.einsum(
+        "td,pdc->ptc", normed_a, w_in_b[..., :256], preferred_element_type=F32
+    ).astype(BF16)
     lowrank = jnp.dot(normed_a.astype(F32), low_first, precision=HIGHEST)
     gain = head_gain.reshape(1, VAL)
     p_spec, r_spec, f_spec, row_spec, s_spec = specs(blocks)
@@ -429,78 +447,178 @@
         [shape((rows, 512), F32), shape((rows, 512), BF16), state_f32],
         [],
         1 << 29,
-    )(info, lowrank, low_second, decay_bias.reshape(1, 512), proj_a, proj_a, proj_b, seg)
-    state_in = lax.ppermute(final_state.astype(BF16), "tensor", [(0, 1)])
+    )(info, lowrank, low_second, decay_bias.reshape(1, 512), proj_a, proj_a, proj_v, seg)
+    def outgate_product(act, weight):
+        return jnp.einsum("td,pdc->ptc", act, weight, preferred_element_type=F32).astype(BF16)
+
+    proj_og, (state_in,) = during(
+        [(final_state.astype(BF16), 0)], outgate_product, normed_a, w_in_b[..., 256:]
+    )
+    state_in = jnp.where(place == 0, jnp.zeros_like(state_in), state_in)
     mixed, core, states = call(
         core_kernel,
         blocks,
-        [p_spec(256, 0), p_spec(256, 1), p_spec(256, 2), p_spec(256, 0), p_spec(256, 1), p_spec(256, 2),
+        [p_spec(256, 0), p_spec(256, 1), p_spec(256, 2), p_spec(256, 0), p_spec(256, 0), p_spec(256, 1),
          r_spec(512), r_spec(1), row_spec, f_spec(HEADS, KEY, VAL), f_spec(1, VAL)],
         [r_spec(1024), r_spec(1024), s_spec],
         [shape((rows, 1024), BF16), shape((rows, 1024), BF16),
          shape((blocks, HEADS, KEY, VAL), BF16)],
         [pltpu.VMEM((HEADS, KEY, VAL), F32)],
         1 << 30,
-    )(info, proj_a, proj_a, proj_a, proj_b, proj_b, proj_b, cum, seg, seg_row, state_in, gain)
+    )(info, proj_a, proj_a, proj_a, proj_v, proj_og, proj_og, cum, seg, seg_row, state_in, gain)
     middle = resid + nt(mixed[:, :512], w_out[0]) + nt(mixed[:, 512:], w_out[1])
 
     normed_b = (rms(middle, 1e-6) * feed_gain).astype(BF16)
     pre = jnp.einsum("td,pdc->ptc", normed_b, w_gu, preferred_element_type=F32).astype(BF16)
-    gate_pre, up_pre = pre[..., :half].astype(F32), pre[..., half:].astype(F32)
-    sig_gate = jax.nn.sigmoid(gate_pre)
-    silu = gate_pre * sig_gate
-    activ = (silu * up_pre).astype(BF16)
-    feed_out = nt(activ[0], w_down[0]) + nt(activ[1], w_down[1])
+    activ = (jax.nn.silu(pre[..., :half].astype(F32)) * pre[..., half:].astype(F32)).astype(BF16)
+
+    ff_out, ff_in, mix_in = "to,ptc->poc", "td,ptc->pdc", "td,ptc->pdc"
+    other, mine = by_core(cotangent)
+    halves = [activ[..., :768], activ[..., 768:]]
+    sent = products(ff_out, other, halves)
+    kept, got = during([(part, 1) for part in sent], lambda a, *b: products(ff_out, a, b), mine, *halves)
+    down = Halving(kept, got, (2, 0))
+
+    def activation_back(dout, weight, gate_pre, up_pre):
+        d_activ = jnp.einsum("to,poc->ptc", dout, weight, preferred_element_type=F32)
+        gate_pre, up_pre = gate_pre.astype(F32), up_pre.astype(F32)
+        sig = jax.nn.sigmoid(gate_pre)
+        d_gate = (d_activ * up_pre * (sig * (1.0 + gate_pre * (1.0 - sig)))).astype(BF16)
+        return d_gate, (d_activ * (gate_pre * sig)).astype(BF16)
+
+    (d_gate, d_up), got = during(
+        down.sends(), activation_back, cotangent, w_down, pre[..., :half], pre[..., half:]
+    )
+    down.receive(got)
+
+    other, mine = by_core(normed_b)
+    sent, got = during(
+        down.sends(), lambda a, *b: products(ff_in, a, b), other, d_gate, d_up
+    )
+    down.receive(got)
+
+    def mine_and_out(act, *operands):
+        grads = products(ff_in, act, operands[:2])
+        return grads, nt(operands[2][0], operands[3][0]) + nt(operands[2][1], operands[3][1])
+
+    (kept, feed_out), got = during(
+        [(part, 1) for part in sent] + down.sends(), mine_and_out, mine, d_gate, d_up, activ, w_down
+    )
     block_out = (middle + feed_out).astype(BF16)
-
-    own_down = scatter([activ[..., :768], activ[..., 768:]], "to,ptc->poc", cotangent)
-    d_activ = jnp.einsum("to,poc->ptc", cotangent, w_down, preferred_element_type=F32)
-    d_gate = (d_activ * up_pre * (sig_gate * (1.0 + gate_pre * (1.0 - sig_gate)))).astype(BF16)
-    d_up = (d_activ * silu).astype(BF16)
-    own_gate, own_up = scatter([d_gate, d_up], "td,ptc->pdc", normed_b)
-    d_pre = jnp.concatenate([d_gate, d_up], axis=-1)
-    d_normed_b = nt(d_pre[0], w_gu[0]) + nt(d_pre[1], w_gu[1])
-    back, feed_gain_grad = rms_back(middle, feed_gain, 1e-6, d_normed_b)
-    d_middle = cotangent.astype(F32) + back
-    d_mix = d_middle.astype(BF16)
+    down.receive(got[2:])
+    gate_up = Halving(kept, got[:2], (2, 0))
+
+    def middle_back(d_gate, d_up, w_gu, middle, w_out):
+        d_normed_b = (
+            nt(d_gate[0], w_gu[0, :, :half])
+            + nt(d_up[0], w_gu[0, :, half:])
+            + nt(d_gate[1], w_gu[1, :, :half])
+            + nt(d_up[1], w_gu[1, :, half:])
+        )
+        back, feed_gain_grad = rms_back(middle, feed_gain, 1e-6, d_normed_b)
+        d_middle = cotangent.astype(F32) + back
+        d_mix = d_middle.astype(BF16)
+        d_mixed = jnp.concatenate([nn(d_mix, w_out[0]), nn(d_mix, w_out[1])], axis=1).astype(BF16)
+        return d_middle, d_mix, d_mixed, feed_gain_grad
+
+    (d_middle, d_mix, d_mixed, feed_gain_grad), got = during(
+        gate_up.sends() + down.sends(), middle_back, d_gate, d_up, w_gu, middle, w_out
+    )
+    gate_up.receive(got[:2])
+    down.receive(got[2:])
+    own_down = down.finish()
 
     mixed_split = mixed.reshape(rows, 2, 512).transpose(1, 0, 2)
-    own_out = scatter([mixed_split[..., :256], mixed_split[..., 256:]], "to,ptc->poc", d_mix)
-    d_mixed = jnp.concatenate([nn(d_mix, w_out[0]), nn(d_mix, w_out[1])], axis=1).astype(BF16)
-    d_core, d_og, head_gain_grad, d_state = call(
-        post_kernel,
-        blocks,
-        [r_spec(1024), r_spec(1024), p_spec(256, 1), p_spec(256, 2), p_spec(256, 0), r_spec(512), r_spec(1),
-         f_spec(1, VAL)],
-        [r_spec(1024), p_spec(512, 0), f_spec(1, VAL), f_spec(HEADS, KEY, VAL)],
-        [shape((rows, 1024), BF16), shape((2, rows, 512), BF16), shape((1, VAL), F32), state_f32],
-        [pltpu.VMEM((1, 512), F32)],
-        1 << 29,
-    )(info, d_mixed, core, proj_b, proj_b, proj_a, cum, seg, gain)
-    d_state_in = lax.ppermute(d_state.astype(BF16), "tensor", [(1, 0)])
+    mixed_halves = [mixed_split[..., :256], mixed_split[..., 256:]]
+
+    def post_back(d_mixed, d_mix, *mixed_halves):
+        d_core, d_og, head_gain_grad, d_state = call(
+            post_kernel,
+            blocks,
+            [r_spec(1024), r_spec(1024), p_spec(256, 0), p_spec(256, 1), p_spec(256, 0), r_spec(512),
+             r_spec(1), f_spec(1, VAL)],
+            [r_spec(1024), p_spec(512, 0), f_spec(1, VAL), f_spec(HEADS, KEY, VAL)],
+            [shape((rows, 1024), BF16), shape((2, rows, 512), BF16), shape((1, VAL), F32), state_f32],
+            [pltpu.VMEM((1, 512), F32)],
+            1 << 29,
+        )(info, d_mixed, core, proj_og, proj_og, proj_a, cum, seg, gain)
+        other, mine = by_core(d_mix)
+        (sent, kept), (d_state_in,) = during(
+            [(d_state.astype(BF16), 0)],
+            lambda a, b, *c: (products(ff_out, a, c), products(ff_out, b, c)),
+            other, mine, *mixed_halves,
+        )
+        return d_core, d_og, head_gain_grad, d_state_in, sent, kept
+
+    (d_core, d_og, head_gain_grad, d_state_in, sent, kept), got = during(
+        gate_up.sends(), post_back, d_mixed, d_mix, *mixed_halves
+    )
+    gate_up.receive(got)
+    d_state_in = jnp.where(place == 1, jnp.zeros_like(d_state_in), d_state_in)
     p_spec, r_spec, f_spec, row_spec, s_spec = specs(blocks, True)
-    d_a, d_b, d_rank, low_second_grad, bias_grad = call(
-        back_kernel,
-        blocks,
-        [p_spec(256, 0), p_spec(256, 1), p_spec(256, 2), p_spec(256, 0), p_spec(512, 0), r_spec(512), r_spec(512), s_spec,
-         r_spec(1024), r_spec(1), row_spec, f_spec(HEADS, KEY, VAL), f_spec(16, 512), r_spec(16)],
-        [p_spec(768, 0), p_spec(768, 0), r_spec(16), f_spec(16, 512), f_spec(1, 512)],
-        [shape((2, rows, 768), BF16), shape((2, rows, 768), BF16), shape((rows, 16), F32), shape((16, 512), F32),
-         shape((1, 512), F32)],
-        [pltpu.VMEM((HEADS, KEY, VAL), F32)],
-        3 << 30,
-    )(info, proj_a, proj_a, proj_a, proj_b, d_og, cum, sig, states, d_core, seg, seg_row, d_state_in, low_second, lowrank)
-    own_a, own_b = scatter([d_a, d_b], "td,ptc->pdc", normed_a)
-    low_first_grad = tn(normed_a, d_rank.astype(BF16))
-    d_normed_a = (
-        nt(d_a[0], w_in_a[0])
-        + nt(d_a[1], w_in_a[1])
-        + nt(d_b[0], w_in_b[0])
-        + nt(d_b[1], w_in_b[1])
-        + nt(d_rank.astype(BF16), low_first.astype(BF16))
-    )
-    back, mixer_gain_grad = rms_back(resid, mixer_gain, 1e-6, d_normed_a)
-    input_grad = (d_middle + back).astype(BF16)
+
+    def core_back(d_core, d_og, d_state_in):
+        return call(
+            back_kernel,
+            blocks,
+            [p_spec(256, 0), p_spec(256, 1), p_spec(256, 2), p_spec(256, 0), p_spec(512, 0),
+             r_spec(512), r_spec(512), s_spec, r_spec(1024), r_spec(1), row_spec,
+             f_spec(HEADS, KEY, VAL), f_spec(16, 512), r_spec(16)],
+            [p_spec(768, 0), p_spec(768, 0), r_spec(16), f_spec(16, 512), f_spec(1, 512)],
+            [shape((2, rows, 768), BF16), shape((2, rows, 768), BF16), shape((rows, 16), F32),
+             shape((16, 512), F32), shape((1, 512), F32)],
+            [pltpu.VMEM((HEADS, KEY, VAL), F32)],
+            3 << 30,
+        )(info, proj_a, proj_a, proj_a, proj_v, d_og, cum, sig, states, d_core, seg, seg_row,
+          d_state_in, low_second, lowrank)
+
+    (d_a, d_b, d_rank, low_second_grad, bias_grad), got = during(
+        gate_up.sends() + [(part, 1) for part in sent], core_back, d_core, d_og, d_state_in
+    )
+    gate_up.receive(got[:2])
+    out = Halving(kept, got[2:], (2, 0))
+
+    other, mine = by_core(normed_a)
+    sent, got = during(
+        gate_up.sends() + out.sends(), lambda a, *b: products(mix_in, a, b), other, d_a, d_b
+    )
+    gate_up.receive(got[:2])
+    out.receive(got[2:])
+    own_gate, own_up = gate_up.finish()
+    kept, got = during(
+        [(part, 1) for part in sent] + out.sends(), lambda a, *b: products(mix_in, a, b), mine, d_a, d_b
+    )
+    out.receive(got[2:])
+    mix = Halving(kept, got[:2], (2, 0))
+
+    def input_back(d_a, d_b, d_rank, w_a, w_b):
+        low_first_grad = tn(normed_a, d_rank.astype(BF16))
+        d_normed_a = (
+            nt(d_a[0], w_a[0])
+            + nt(d_a[1], w_a[1])
+            + nt(d_b[0], w_b[0])
+            + nt(d_b[1], w_b[1])
+            + nt(d_rank.astype(BF16), low_first.astype(BF16))
+        )
+        return d_normed_a, low_first_grad
+
+    (d_normed_a, low_first_grad), got = during(
+        mix.sends() + out.sends(), input_back, d_a, d_b, d_rank, w_in_a, w_in_b
+    )
+    mix.receive(got[:2])
+    out.receive(got[2:])
+
+    def input_end(d_normed_a, d_middle):
+        back, mixer_gain_grad = rms_back(resid, mixer_gain, 1e-6, d_normed_a)
+        return (d_middle + back).astype(BF16), mixer_gain_grad
+
+    (input_grad, mixer_gain_grad), got = during(
+        mix.sends() + out.sends(), input_end, d_normed_a, d_middle
+    )
+    mix.receive(got[:2])
+    out.receive(got[2:])
+    own_out = out.finish()
+    own_a, own_b = mix.finish()
 
     parts = (mixer_gain_grad, feed_gain_grad, low_first_grad, low_second_grad, bias_grad, head_gain_grad)
     flat = total_sum(jnp.concatenate([part.reshape(-1, 128) for part in parts]))

time: 623 us -> 635 us (1.019)
  local copies, waits for them, and re-layouts: 66.6 us -> 121 us
  waiting for transfers between devices: 179 us -> 132 us
  other arithmetic: 66.4 us -> 75.5 us
    ppermute x40 -> x44, waiting for transfers between devices: 129 us -> 79.7 us  [swap(): lax.ppermute(x, 'dp', [(i, i ^ stride) for i in range(lax.axis_size('dp'))])]
    ppermute x10 -> x13, waiting for transfers between devices: 10.6 us -> 46 us  [swap(): return lax.ppermute(x, 'tensor', [(0, 1), (1, 0)])]
    all_gather x2 -> x1, waiting for transfers between devices: 30.5 us -> 5.95 us  [gather(): lax.all_gather(shard, ALL, axis=0, tiled=True)]
    slice x4 -> x8, local copies, waits for them, and re-layouts: 4.65 us -> 25.3 us  [the longest x1 10.1 us: local(): pre[..., half:].astype(F32)]
    optimization_barrier x0 -> x2, local copies, waits for them, and re-layouts: none -> 15.4 us  [fence(): return lax.optimization_barrier(values)]
    ppermute x7 -> x0, starting transfers between devices: 12.8 us -> none  [the longest x4 5.47 us: total_sum(): x = x + lax.ppermute(x, 'dp', [(i, i ^ stride) for i in range(n)])]
    unnamed x165 -> x194, local copies, waits for them, and re-layouts: 28.4 us -> 40.4 us
    ppermute x7 -> x0, waiting for transfers between devices: 9.61 us -> none  [the longest x4 9.6 us: total_sum(): x = x + lax.ppermute(x, 'dp', [(i, i ^ stride) for i in range(n)])]
  transfers between devices with their start and end apart: 59 -> 58, of which waited for: 33 -> 17; matrix products, arithmetic and copies ran while one was open for 33% -> 29% of each run, Pallas kernels for 7% -> 7%
where the time goes in v3:
time: 635 us; the launch traced here: 624 us
  matrix products  169 us (27%)
  waiting for transfers between devices  132 us (21%)
  local copies, waits for them, and re-layouts  121 us (19%)
  other arithmetic  75.5 us (12%)
  starting transfers between devices  58 us (9%)
  Pallas kernels  52.5 us (8%)
  between operations  16.2 us (3%)
    ppermute x44, waiting for transfers between devices, swap(): lax.ppermute(x, 'dp', [(i, i ^ stride) for i in range(lax.axis_size('dp'))])  79.7 us
    dot_general x13, matrix products, nt(): lax.dot_general(a, b, (((1,), (1,)), ((), ())), preferred_element_type=F32)  58.1 us
    dot_general x16, matrix products, products(): jnp.einsum(equation, act, part, preferred_element_type=F32).astype(BF16)  56.6 us
    ppermute x13, waiting for transfers between devices, swap(): return lax.ppermute(x, 'tensor', [(0, 1), (1, 0)])  46 us
    ppermute x44, starting transfers between devices, swap(): lax.ppermute(x, 'dp', [(i, i ^ stride) for i in range(lax.axis_size('dp'))])  42.1 us
    unnamed x194, local copies, waits for them, and re-layouts  40.4 us
    pallas_call x1, Pallas kernels, core_back(): call(back_kernel, blocks, [p_spec(256, 0), p_spec(256, 1), p_spec(256, 2)...  20.9 us
    dot_general x1, matrix products, activation_back(): jnp.einsum('to,poc->ptc', dout, weight, preferred_element_type=F32)  19.5 us
  transfers between devices with their start and end apart: 58, of which 17 were waited for; matrix products, arithmetic and copies ran while one was open for 29% of the time, Pallas kernels for 7%

profile of v3, /device:TPU:0, one launch (start us, length us, event | category | flops | bytes accessed | tf_op | source)
XLA Modules:
  0.0 624.0 jit_solution(15080800518070083631)
XLA Ops:
  25.9 20.8 %collective-permute-done.1 = bf16[2,64,768]{2,1,0:T(8,128)(2,1)S(1)} collective-permute-done((bf16[2,64,768]{2,1,0:T(8,128)(2,1)S(1)}, bf16[2,64,768]{2,1,0:T(8,128)(2,1)S(1)}, u32[]{:S(2)}, u32[]{:S(2)}) %collective-permute-start.1) | collective-permute-done | bytes 196640 | tf_op jit(solution)/shard_map/ppermute | solution.py:307
  50.0 15.1 %collective-permute-done.7 = bf16[2,2,64,768]{3,2,1,0:T(8,128)(2,1)S(1)} collective-permute-done((bf16[2,2,64,768]{3,2,1,0:T(8,128)(2,1)S(1)}, bf16[2,2,64,768]{3,2,1,0:T(8,128)(2,1)S(1)}, u32[]{:S(2)}, u32[]{:S(2)}) %collective-permute-start.7) | collective-permute-done | bytes 393248 | tf_op jit(solution)/shard_map/ppermute | solution.py:306
  69.0 22.6 %collective-permute-done.8 = bf16[2,2,2,64,768]{4,3,2,1,0:T(8,128)(2,1)S(1)} collective-permute-done((bf16[2,2,2,64,768]{4,3,2,1,0:T(8,128)(2,1)S(1)}, bf16[2,2,2,64,768]{4,3,2,1,0:T(8,128)(2,1)S(1)}, u32[]{:S(2)}, u32[]{:S(2)}) %collective-permute-start.8) | collective-permute-done | bytes 786464 | tf_op jit(solution)/shard_map/ppermute | solution.py:307
  120.3 10.6 %shard_map.288 = (f32[1024,512]{1,0:T(8,128)S(1)}, bf16[1024,512]{1,0:T(8,128)(2,1)S(1)}, f32[4,128,256]{2,1,0:T(8,128)S(1)}) custom-call(s32[2,8]{1,0:T(2,128)S(1)} %pad_add_fusion.info, f32[1024,16]{1,0:T(8,128)S(1)} %fusion.166.low_ref, f32[16,512]{1,0:T(8,128)S(1)} %copy-done.9, f32[1,512]{1,0:T(1,128)S(1)} %bitcast.515, ...), custom_call_target="tpu_custom_call" | custom-call | flops 536870912 | bytes 16777216 | tf_op jit(solution)/shard_map/pallas_call | solution.py:441
  136.4 8.7 %collective-permute-done.10 = bf16[4,128,256]{2,1,0:T(8,128)(2,1)S(1)} collective-permute-done((bf16[4,128,256]{2,1,0:T(8,128)(2,1)S(1)}, bf16[4,128,256]{2,1,0:T(8,128)(2,1)S(1)}, u32[]{:S(2)}, u32[]{:S(2)}) %collective-permute-start.10) | collective-permute-done | bytes 262176 | tf_op jit(solution)/shard_map/ppermute | solution.py:306
  145.1 10.7 %shard_map.289 = (bf16[1024,1024]{1,0:T(8,128)(2,1)S(1)}, bf16[1024,1024]{1,0:T(8,128)(2,1)S(1)}, bf16[8,4,128,256]{3,2,1,0:T(8,128)(2,1)}) custom-call(s32[2,8]{1,0:T(2,128)S(1)} %pad_add_fusion.info, bf16[2,1024,768]{2,1,0:T(8,128)(2,1)} %convert_bitcast_fusion.1.k_ref.v0_ref.q_ref, bf16[2,1024,768]{2,1,0:T(8,128)(2,1)} %convert_bitcast_fusion.1.k_ref.v0_ref.q_ref, ...), custom_call_target="tpu_custom_call" | custom-call | flops 1073741824 | bytes 16777216 | tf_op jit(solution)/shard_map/pallas_call | solution.py:458
  162.8 6.0 all-gather.2.cloned.1.call-done
  179.8 10.0 %slice.232 = bf16[2,1024,2816]{2,1,0:T(8,128)(2,1)} slice(bf16[2,1024,4736]{2,1,0:T(8,128)(2,1)} %bitcast.521), slice={[0:2], [0:1024], [0:2816]} | slice | bytes 23068672
  194.8 19.2 %convert_bitcast_fusion = bf16[2,1024,2816]{1,2,0:T(8,128)(2,1)} fusion(bf16[1024,1024]{0,1:T(8,128)(2,1)S(1)} %multiply_convert_fusion, bf16[2,1024,4736]{2,1,0:T(8,128)(2,1)} %bitcast.523), kind=kOutput, calls=%fused_computation.19 | convolution fusion | flops 11816927232 | bytes 25165824 | tf_op jit(solution)/shard_map/td,pdc->ptc/dot_general | solution.py:472
  214.8 6.7 %fusion.13 = bf16[2,1024,1408]{1,2,0:T(8,128)(2,1)S(1)} fusion(bf16[2,1024,2816]{1,2,0:T(8,128)(2,1)} %convert_bitcast_fusion), kind=kLoop, calls=%fused_computation.20 | loop fusion | flops 23068672 | bytes 17301504 | tf_op jit(solution)/shard_map/convert_element_type | solution.py:473
  232.4 15.2 %copy.403 = bf16[2,1024,2816]{1,2,0:T(8,128)(2,1)} copy(bf16[2,1024,2816]{2,1,0:T(8,128)(2,1)} %slice.232) | data formatting | bytes 23068672 | tf_op jit(solution)/shard_map/optimization_barrier | solution.py:351
  256.1 10.1 %fusion.162 = (bf16[2,1024,1408]{1,2,0:T(8,128)(2,1)}, bf16[2,1024,1408]{1,2,0:T(8,128)(2,1)}) fusion(bf16[2,1024,2816]{1,2,0:T(8,128)(2,1)} %convert_bitcast_fusion), kind=kLoop, calls=%fused_computation.312 | loop fusion | bytes 23068672 | tf_op jit(solution)/shard_map/slice | solution.py:473
  277.9 19.5 %fusion.12 = (bf16[2,1024,1408]{1,2,0:T(8,128)(2,1)}, bf16[2,1024,1408]{1,2,0:T(8,128)(2,1)}) fusion(bf16[2,1024,1408]{1,2,0:T(8,128)(2,1)} %get-tuple-element.212, bf16[2,1024,1408]{1,2,0:T(8,128)(2,1)} %get-tuple-element.211, bf16[2,1024,1408]{2,1,0:T(8,128)(2,1)} %slice.237, bf16[1024,1024]{1,0:T(8,128)(2,1)} %param.19), kind=kOutput, calls=%fused_computation.17 | convolution fusion | flops 5948833792 | bytes 30932992 | tf_op jit(solution)/shard_map/to,poc->ptc/dot_general | solution.py:483
  299.9 6.2 %fusion.27 = bf16[2,512,1408]{1,2,0:T(8,128)(2,1)S(1)} fusion(bf16[2,1024,1408]{1,2,0:T(8,128)(2,1)} %get-tuple-element.245, bf16[1024,512]{0,1:T(8,128)(2,1)S(1)} %bitcast.575), kind=kOutput, calls=%fused_computation.50 | convolution fusion | flops 2954231808 | bytes 9699328 | tf_op jit(solution)/shard_map/td,ptc->pdc/dot_general | solution.py:361
  316.1 6.6 %fusion.29 = bf16[2,512,1408]{1,2,0:T(8,128)(2,1)S(1)} fusion(bf16[2,1024,1408]{1,2,0:T(8,128)(2,1)} %get-tuple-element.245, bf16[1024,512]{0,1:T(8,128)(2,1)S(1)} %bitcast.573), kind=kOutput, calls=%fused_computation.52 | convolution fusion | flops 2954231808 | bytes 9699328 | tf_op jit(solution)/shard_map/td,ptc->pdc/dot_general | solution.py:361
  327.7 7.2 %fusion.30 = bf16[2,512,1408]{1,2,0:T(8,128)(2,1)} fusion(bf16[2,1024,1408]{1,2,0:T(8,128)(2,1)} %get-tuple-element.247, bf16[1024,512]{0,1:T(8,128)(2,1)S(1)} %bitcast.574), kind=kOutput, calls=%fused_computation.53 | convolution fusion | flops 2954231808 | bytes 9699328 | tf_op jit(solution)/shard_map/td,ptc->pdc/dot_general | solution.py:361
  356.4 8.3 %fusion.32 = f32[1024,1024]{0,1:T(8,128)} fusion(bf16[2,1024,2816]{1,2,0:T(8,128)(2,1)} %copy.403, bf16[2,1024,1408]{1,2,0:T(8,128)(2,1)} %get-tuple-element.247), kind=kOutput, calls=%fused_computation.58 | convolution fusion | flops 2952790016 | bytes 9961472 | tf_op jit(solution)/shard_map/dot_general | solution.py:25
  364.7 7.2 %fusion.38 = f32[1024,1024]{0,1:T(8,128)} fusion(bf16[2,1024,2816]{1,2,0:T(8,128)(2,1)} %copy.403, bf16[2,1024,1408]{1,2,0:T(8,128)(2,1)S(1)} %bitcast.605), kind=kOutput, calls=%fused_computation.64 | convolution fusion | flops 2952790016 | bytes 9961472 | tf_op jit(solution)/shard_map/dot_general | solution.py:25
  377.2 6.9 %fusion.35 = f32[1024,1024]{0,1:T(8,128)} fusion(bf16[2,1024,2816]{1,2,0:T(8,128)(2,1)} %copy.403, bf16[2,1024,1408]{1,2,0:T(8,128)(2,1)S(1)} %bitcast.601), kind=kOutput, calls=%fused_computation.61 | convolution fusion | flops 2952790016 | bytes 9961472 | tf_op jit(solution)/shard_map/dot_general | solution.py:25
  384.1 11.5 %multiply_reduce_fusion = (f32[1024]{0:T(1024)S(1)}, f32[1024]{0:T(1024)S(1)}, f32[1024,1024]{0,1:T(8,128)S(1)}) fusion(f32[1024,1024]{0,1:T(8,128)S(1)} %copy-done.17, f32[1024]{0:T(1024)S(1)} %add_rsqrt_fusion, f32[1024]{0:T(1024)S(1)} %copy-done.76, f32[1024,1024]{0,1:T(8,128)} %fusion.32, f32[1024,1024]{0,1:T(8,128)} %fusion.35, ...), kind=kOutput, calls=%fused_computation.38 | convolution fusion | flops 2962225152 | bytes 26755072 | tf_op jit(solution)/shard_map/dot_general | solution.py:25
  414.4 10.3 %shard_map.290 = (bf16[1024,1024]{1,0:T(8,128)(2,1)S(1)}, bf16[2,1024,512]{2,1,0:T(8,128)(2,1)S(1)}, f32[1,256]{1,0:T(1,128)S(1)}, f32[4,128,256]{2,1,0:T(8,128)S(1)}) custom-call(s32[2,8]{1,0:T(2,128)S(1)} %copy-done.12, bf16[1024,1024]{1,0:T(8,128)(2,1)} %pad_maximum_fusion.dm_ref, bf16[1024,1024]{1,0:T(8,128)(2,1)} %copy-done.6, ...), custom_call_target="tpu_custom_call" | custom-call | flops 536870912 | bytes 16777216 | tf_op jit(solution)/shard_map/pallas_call | solution.py:535
  433.6 13.8 %collective-permute-done.25 = bf16[4,128,256]{2,1,0:T(8,128)(2,1)S(1)} collective-permute-done((bf16[4,128,256]{2,1,0:T(8,128)(2,1)S(1)}, bf16[4,128,256]{2,1,0:T(8,128)(2,1)S(1)}, u32[]{:S(2)}, u32[]{:S(2)}) %collective-permute-start.25) | collective-permute-done | bytes 262176 | tf_op jit(solution)/shard_map/ppermute | solution.py:306
  451.1 20.9 %shard_map.291 = (bf16[2,1024,768]{2,1,0:T(8,128)(2,1)}, bf16[2,1024,768]{2,1,0:T(8,128)(2,1)}, f32[1024,16]{1,0:T(8,128)S(1)}, f32[16,512]{1,0:T(8,128)S(1)}, f32[1,512]{1,0:T(1,128)S(1)}) custom-call(s32[2,8]{1,0:T(2,128)S(1)} %copy-done.12, bf16[2,1024,768]{2,1,0:T(8,128)(2,1)} %convert_bitcast_fusion.1.k_ref.v0_ref.q_ref, ...), custom_call_target="tpu_custom_call" | custom-call | flops 3221225472 | bytes 16777216 | tf_op jit(solution)/shard_map/pallas_call | solution.py:561
  542.1 13.9 %collective-permute-done.40 = bf16[2,2,2,64,768]{4,3,2,1,0:T(8,128)(2,1)S(1)} collective-permute-done((bf16[2,2,2,64,768]{4,3,2,1,0:T(8,128)(2,1)S(1)}, bf16[2,2,2,64,768]{4,3,2,1,0:T(8,128)(2,1)S(1)}, u32[]{:S(2)}, u32[]{:S(2)}) %collective-permute-start.40) | collective-permute-done | bytes 786464 | tf_op jit(solution)/shard_map/ppermute | solution.py:307
  (510 shorter events, 320.0 us)
Async XLA Ops:
  7.2 161.6 %all-gather.2.cloned.1.call-start = ((), (), s32[]{:S(2)}) async-start(), calls=%async_computation | async-start | bytes 20004864 | tf_op jit(solution)/shard_map/all_gather | solution.py:301
  23.6 24.7 %collective-permute-start.6 = (bf16[2,64,768]{2,1,0:T(8,128)(2,1)S(1)}, bf16[2,64,768]{2,1,0:T(8,128)(2,1)S(1)}, u32[]{:S(2)}, u32[]{:S(2)}) collective-permute-start(bf16[2,64,768]{2,1,0:T(8,128)(2,1)S(1)} %maximum_select_fusion.13), channel_id=1, source_target_pairs={{0,8},{2,10},{4,12},{6,14},{8,0},{10,2},{12,4},{14,6},{16,24},{18,... | collective-permute-start | bytes 589832 | tf_op jit(solution)/shard_map/ppermute | solution.py:307
  25.6 21.1 %collective-permute-start.1 = (bf16[2,64,768]{2,1,0:T(8,128)(2,1)S(1)}, bf16[2,64,768]{2,1,0:T(8,128)(2,1)S(1)}, u32[]{:S(2)}, u32[]{:S(2)}) collective-permute-start(bf16[2,64,768]{2,1,0:T(8,128)(2,1)S(1)} %maximum_select_fusion.11), channel_id=1, source_target_pairs={{0,8},{2,10},{4,12},{6,14},{8,0},{10,2},{12,4},{14,6},{16,24},{18,... | collective-permute-start | bytes 589832 | tf_op jit(solution)/shard_map/ppermute | solution.py:307
  46.7 18.7 %collective-permute-start.2 = (bf16[2,2,64,768]{3,2,0,1:T(8,128)(2,1)S(1)}, bf16[2,2,64,768]{3,2,0,1:T(8,128)(2,1)S(1)}, u32[]{:S(2)}, u32[]{:S(2)}) collective-permute-start(bf16[2,2,64,768]{3,2,0,1:T(8,128)(2,1)S(1)} %maximum_select_fusion.8), channel_id=1, source_target_pairs={{0,4},{2,6},{4,0},{6,2},{8,12},{10,14},{12,8},{14,10},{16,20},{18,... | collective-permute-start | bytes 1179656 | tf_op jit(solution)/shard_map/ppermute | solution.py:307
  65.3 26.4 %collective-permute-start.8 = (bf16[2,2,2,64,768]{4,3,2,1,0:T(8,128)(2,1)S(1)}, bf16[2,2,2,64,768]{4,3,2,1,0:T(8,128)(2,1)S(1)}, u32[]{:S(2)}, u32[]{:S(2)}) collective-permute-start(bf16[2,2,2,64,768]{4,3,2,1,0:T(8,128)(2,1)S(1)} %maximum_select_fusion.7), channel_id=1, source_target_pairs={{0,4},{2,6},{4,0},{6,2},{8,12},{10,14},{12,8},{14,10},{16,20},{18,... | collective-permute-start | bytes 2359304 | tf_op jit(solution)/shard_map/ppermute | solution.py:307
  65.4 27.6 %collective-permute-start.3 = (bf16[2,2,2,64,768]{4,3,0,1,2:T(8,128)(2,1)S(1)}, bf16[2,2,2,64,768]{4,3,0,1,2:T(8,128)(2,1)S(1)}, u32[]{:S(2)}, u32[]{:S(2)}) collective-permute-start(bf16[2,2,2,64,768]{4,3,0,1,2:T(8,128)(2,1)S(1)} %maximum_select_fusion.5), channel_id=1, source_target_pairs={{0,1},{1,0},{2,3},{3,2},{4,5},{5,4},{6,7},{7,6},{8,9},{9,8},{10,11... | collective-permute-start | bytes 2359304 | tf_op jit(solution)/shard_map/ppermute | solution.py:306
  247.5 18.7 %collective-permute-start.12 = (bf16[2,512,640]{1,2,0:T(8,128)(2,1)}, bf16[2,512,640]{1,2,0:T(8,128)(2,1)}, u32[]{:S(2)}, u32[]{:S(2)}) collective-permute-start(bf16[2,512,640]{1,2,0:T(8,128)(2,1)} %fusion.107), channel_id=1, source_target_pairs={{0,2},{2,0},{4,6},{6,4},{8,10},{10,8},{12,14},{14,12},{16,18},{18,... | collective-permute-start | bytes 3932168 | tf_op jit(solution)/shard_map/ppermute | solution.py:307
  275.9 21.4 %collective-permute-start.14 = (bf16[2,2,2,64,640]{4,3,2,1,0:T(8,128)(2,1)S(1)}, bf16[2,2,2,64,640]{4,3,2,1,0:T(8,128)(2,1)S(1)}, u32[]{:S(2)}, u32[]{:S(2)}) collective-permute-start(bf16[2,2,2,64,640]{4,3,2,1,0:T(8,128)(2,1)S(1)} %dynamic-slice_bitcast_fusion.9), channel_id=1, source_target_pairs={{0,1},{1,0},{2,3},{3,2},{4,5},{5,4},{6,7},{7,6},{8,9},{9,8},{10,11... | collective-permute-start | bytes 1966088 | tf_op jit(solution)/shard_map/ppermute | solution.py:306
  276.4 20.9 %collective-permute-start.13 = (bf16[2,2,2,64,768]{4,3,2,1,0:T(8,128)(2,1)S(1)}, bf16[2,2,2,64,768]{4,3,2,1,0:T(8,128)(2,1)S(1)}, u32[]{:S(2)}, u32[]{:S(2)}) collective-permute-start(bf16[2,2,2,64,768]{4,3,2,1,0:T(8,128)(2,1)S(1)} %dynamic-slice_bitcast_fusion.6), channel_id=1, source_target_pairs={{0,4},{2,6},{4,0},{6,2},{8,12},{10,14},{12,8},{14,10},{16,20},{18,... | collective-permute-start | bytes 2359304 | tf_op jit(solution)/shard_map/ppermute | solution.py:307
  310.1 24.9 %collective-permute-start.20 = (bf16[2,64,640]{2,1,0:T(8,128)(2,1)S(1)}, bf16[2,64,640]{2,1,0:T(8,128)(2,1)S(1)}, u32[]{:S(2)}, u32[]{:S(2)}) collective-permute-start(bf16[2,64,640]{2,1,0:T(8,128)(2,1)S(1)} %dynamic-slice_bitcast_fusion.23), channel_id=1, source_target_pairs={{0,8},{2,10},{4,12},{6,14},{8,0},{10,2},{12,4},{14,6},{16,24},{18,... | collective-permute-start | bytes 491528 | tf_op jit(solution)/shard_map/ppermute | solution.py:307
  310.3 24.7 %collective-permute-start.19 = (bf16[2,64,768]{2,1,0:T(8,128)(2,1)S(1)}, bf16[2,64,768]{2,1,0:T(8,128)(2,1)S(1)}, u32[]{:S(2)}, u32[]{:S(2)}) collective-permute-start(bf16[2,64,768]{2,1,0:T(8,128)(2,1)S(1)} %dynamic-slice_bitcast_fusion.20), channel_id=1, source_target_pairs={{0,8},{2,10},{4,12},{6,14},{8,0},{10,2},{12,4},{14,6},{16,24},{18,... | collective-permute-start | bytes 589832 | tf_op jit(solution)/shard_map/ppermute | solution.py:307
  312.2 22.8 %collective-permute-start.17 = (bf16[2,512,1408]{1,2,0:T(8,128)(2,1)S(1)}, bf16[2,512,1408]{1,2,0:T(8,128)(2,1)S(1)}, u32[]{:S(2)}, u32[]{:S(2)}) collective-permute-start(bf16[2,512,1408]{1,2,0:T(8,128)(2,1)S(1)} %fusion.27), channel_id=1, source_target_pairs={{0,2},{2,0},{4,6},{6,4},{8,10},{10,8},{12,14},{14,12},{16,18},{18,... | collective-permute-start | bytes 8650760 | tf_op jit(solution)/shard_map/ppermute | solution.py:307
  312.2 22.8 %collective-permute-start.18 = (bf16[2,512,1408]{1,2,0:T(8,128)(2,1)S(1)}, bf16[2,512,1408]{1,2,0:T(8,128)(2,1)S(1)}, u32[]{:S(2)}, u32[]{:S(2)}) collective-permute-start(bf16[2,512,1408]{1,2,0:T(8,128)(2,1)S(1)} %fusion.28), channel_id=1, source_target_pairs={{0,2},{2,0},{4,6},{6,4},{8,10},{10,8},{12,14},{14,12},{16,18},{18,... | collective-permute-start | bytes 8650760 | tf_op jit(solution)/shard_map/ppermute | solution.py:307
  372.3 37.5 %collective-permute-start.24 = (bf16[64,640]{1,0:T(8,128)(2,1)}, bf16[64,640]{1,0:T(8,128)(2,1)}, u32[]{:S(2)}, u32[]{:S(2)}) collective-permute-start(bf16[64,640]{1,0:T(8,128)(2,1)} %dynamic-slice_bitcast_fusion.29), channel_id=1, source_target_pairs={{0,16},{2,18},{4,20},{6,22},{8,24},{10,26},{12,28},{14,30},{16,0},... | collective-permute-start | bytes 245768 | tf_op jit(solution)/shard_map/ppermute | solution.py:307
  373.6 36.1 %collective-permute-start.23 = (bf16[64,768]{1,0:T(8,128)(2,1)S(1)}, bf16[64,768]{1,0:T(8,128)(2,1)}, u32[]{:S(2)}, u32[]{:S(2)}) collective-permute-start(bf16[64,768]{1,0:T(8,128)(2,1)S(1)} %dynamic-slice_bitcast_fusion.28), channel_id=1, source_target_pairs={{0,16},{2,18},{4,20},{6,22},{8,24},{10,26},{12,28},{14,30},{16,0},... | collective-permute-start | bytes 294920 | tf_op jit(solution)/shard_map/ppermute | solution.py:307
  375.3 34.5 %collective-permute-start.21 = (bf16[2,2,2,64,1408]{4,3,2,1,0:T(8,128)(2,1)}, bf16[2,2,2,64,1408]{4,3,2,1,0:T(8,128)(2,1)}, u32[]{:S(2)}, u32[]{:S(2)}) collective-permute-start(bf16[2,2,2,64,1408]{4,3,2,1,0:T(8,128)(2,1)} %dynamic-slice_bitcast_fusion.1), channel_id=1, source_target_pairs={{0,4},{2,6},{4,0},{6,2},{8,12},{10,14},{12,8},{14,10},{16,20},{18,... | collective-permute-start | bytes 4325384 | tf_op jit(solution)/shard_map/ppermute | solution.py:307
  376.7 33.0 %collective-permute-start.22 = (bf16[2,2,2,64,1408]{4,3,2,1,0:T(8,128)(2,1)}, bf16[2,2,2,64,1408]{4,3,2,1,0:T(8,128)(2,1)}, u32[]{:S(2)}, u32[]{:S(2)}) collective-permute-start(bf16[2,2,2,64,1408]{4,3,2,1,0:T(8,128)(2,1)} %dynamic-slice_bitcast_fusion), channel_id=1, source_target_pairs={{0,1},{1,0},{2,3},{3,2},{4,5},{5,4},{6,7},{7,6},{8,9},{9,8},{10,11... | collective-permute-start | bytes 4325384 | tf_op jit(solution)/shard_map/ppermute | solution.py:306
  424.8 22.6 %collective-permute-start.26 = (bf16[2,2,64,1408]{3,2,1,0:T(8,128)(2,1)S(1)}, bf16[2,2,64,1408]{3,2,1,0:T(8,128)(2,1)S(1)}, u32[]{:S(2)}, u32[]{:S(2)}) collective-permute-start(bf16[2,2,64,1408]{3,2,1,0:T(8,128)(2,1)S(1)} %dynamic-slice_bitcast_fusion.8), channel_id=1, source_target_pairs={{0,1},{1,0},{2,3},{3,2},{4,5},{5,4},{6,7},{7,6},{8,9},{9,8},{10,11... | collective-permute-start | bytes 2162696 | tf_op jit(solution)/shard_map/ppermute | solution.py:306
  426.4 21.0 %collective-permute-start.27 = (bf16[2,2,64,1408]{3,2,1,0:T(8,128)(2,1)S(1)}, bf16[2,2,64,1408]{3,2,1,0:T(8,128)(2,1)S(1)}, u32[]{:S(2)}, u32[]{:S(2)}) collective-permute-start(bf16[2,2,64,1408]{3,2,1,0:T(8,128)(2,1)S(1)} %dynamic-slice_bitcast_fusion.7), channel_id=1, source_target_pairs={{0,4},{2,6},{4,0},{6,2},{8,12},{10,14},{12,8},{14,10},{16,20},{18,... | collective-permute-start | bytes 2162696 | tf_op jit(solution)/shard_map/ppermute | solution.py:307
  427.1 20.3 %collective-permute-start.25 = (bf16[4,128,256]{2,1,0:T(8,128)(2,1)S(1)}, bf16[4,128,256]{2,1,0:T(8,128)(2,1)S(1)}, u32[]{:S(2)}, u32[]{:S(2)}) collective-permute-start(bf16[4,128,256]{2,1,0:T(8,128)(2,1)S(1)} %convert_element_type.233), channel_id=1, source_target_pairs={{0,1},{1,0},{2,3},{3,2},{4,5},{5,4},{6,7},{7,6},{8,9},{9,8},{10,11... | collective-permute-start | bytes 786440 | tf_op jit(solution)/shard_map/ppermute | solution.py:306
  447.7 24.2 %collective-permute-start.28 = (bf16[2,64,1408]{2,1,0:T(8,128)(2,1)S(1)}, bf16[2,64,1408]{2,1,0:T(8,128)(2,1)S(1)}, u32[]{:S(2)}, u32[]{:S(2)}) collective-permute-start(bf16[2,64,1408]{2,1,0:T(8,128)(2,1)S(1)} %dynamic-slice_bitcast_fusion.14), channel_id=1, source_target_pairs={{0,8},{2,10},{4,12},{6,14},{8,0},{10,2},{12,4},{14,6},{16,24},{18,... | collective-permute-start | bytes 1081352 | tf_op jit(solution)/shard_map/ppermute | solution.py:307
  448.0 24.1 %collective-permute-start.29 = (bf16[2,64,1408]{2,1,0:T(8,128)(2,1)S(1)}, bf16[2,64,1408]{2,1,0:T(8,128)(2,1)S(1)}, u32[]{:S(2)}, u32[]{:S(2)}) collective-permute-start(bf16[2,64,1408]{2,1,0:T(8,128)(2,1)S(1)} %dynamic-slice_bitcast_fusion.13), channel_id=1, source_target_pairs={{0,8},{2,10},{4,12},{6,14},{8,0},{10,2},{12,4},{14,6},{16,24},{18,... | collective-permute-start | bytes 1081352 | tf_op jit(solution)/shard_map/ppermute | solution.py:307
  449.8 22.2 %collective-permute-start.30 = (bf16[2,512,256]{1,2,0:T(8,128)(2,1)S(1)}, bf16[2,512,256]{1,2,0:T(8,128)(2,1)S(1)}, u32[]{:S(2)}, u32[]{:S(2)}) collective-permute-start(bf16[2,512,256]{1,2,0:T(8,128)(2,1)S(1)} %fusion.116), channel_id=1, source_target_pairs={{0,2},{2,0},{4,6},{6,4},{8,10},{10,8},{12,14},{14,12},{16,18},{18,... | collective-permute-start | bytes 1572872 | tf_op jit(solution)/shard_map/ppermute | solution.py:307
  449.8 22.2 %collective-permute-start.31 = (bf16[2,512,256]{1,2,0:T(8,128)(2,1)S(1)}, bf16[2,512,256]{1,2,0:T(8,128)(2,1)S(1)}, u32[]{:S(2)}, u32[]{:S(2)}) collective-permute-start(bf16[2,512,256]{1,2,0:T(8,128)(2,1)S(1)} %fusion.117), channel_id=1, source_target_pairs={{0,2},{2,0},{4,6},{6,4},{8,10},{10,8},{12,14},{14,12},{16,18},{18,... | collective-permute-start | bytes 1572872 | tf_op jit(solution)/shard_map/ppermute | solution.py:307
  (126 other events, 963.5 us)
Sparse Core Ops, SparseCore 0:
  10.9 157.8 all-gather.1

commit v4 on v3

--- a/solution.py
+++ b/solution.py
@@ -1,3 +1,5 @@
+import functools
+
 import jax
 import jax.numpy as jnp
 from jax import lax
@@ -14,7 +16,8 @@
 BF16 = jnp.bfloat16
 HIGHEST = lax.Precision.HIGHEST
 ALL = ("tensor", "dp")
-VMEM_BYTES = 48 * 1024 * 1024
+VMEM_BYTES = 56 * 1024 * 1024
+TILE = 256
 
 
 def nn(a, b):
@@ -84,7 +87,7 @@
 
 def core_kernel(
     info, q_ref, k_ref, v0_ref, v1_ref, og0_ref, og1_ref, cum_ref, seg_ref, row_ref, first_ref, gain_ref,
-    mixed_ref, core_ref, states_ref, state,
+    mixed_ref, mixed_a_ref, mixed_b_ref, core_ref, states_ref, state,
 ):
     c = pl.program_id(0)
 
@@ -121,7 +124,9 @@
         normed = core * lax.rsqrt(jnp.mean(core * core, axis=-1, keepdims=True) + 1.0)
         og = head_pick(h, og0_ref, og1_ref).astype(F32)
         hv = slice(h * VAL, (h + 1) * VAL)
-        mixed_ref[:, hv] = (normed * gain_ref[...] * (og * jax.nn.sigmoid(og))).astype(BF16)
+        mixed = (normed * gain_ref[...] * (og * jax.nn.sigmoid(og))).astype(BF16)
+        mixed_ref[:, hv] = mixed
+        (mixed_a_ref if h % 2 == 0 else mixed_b_ref)[p] = mixed
         core_ref[:, hv] = core.astype(BF16)
 
 
@@ -245,23 +250,161 @@
     drank_ref[...] = nt(low, second_ref[...].astype(BF16))
 
 
+def rms_rows(x):
+    scale = lax.rsqrt(jnp.mean(x * x, axis=-1, keepdims=True) + 1e-6)
+    return x * scale, scale
+
+
+def rms_rows_back(normed, scale, gain, grad):
+    dn = grad * gain
+    return scale * (dn - normed * jnp.mean(dn * normed, axis=-1, keepdims=True))
+
+
+def output_rows(w_refs, p):
+    return jnp.concatenate([ref[p] for ref in w_refs], axis=1)
+
+
+def middle_kernel(mixed_ref, w0, w1, w2, w3, hidden_ref, gain_ref, middle_ref, normed_ref):
+    middle = hidden_ref[...].astype(F32)
+    for p in range(2):
+        middle += nt(mixed_ref[:, p * 512 : (p + 1) * 512], output_rows((w0, w1, w2, w3), p))
+    middle_ref[...] = middle
+    normed_ref[...] = (rms_rows(middle)[0] * gain_ref[...]).astype(BF16)
+
+
+def ff_kernel(normed_ref, wg_ref, wu_ref, gate_ref, up_ref, first_ref, second_ref):
+    gate = nn(normed_ref[...], wg_ref[0])
+    up = nn(normed_ref[...], wu_ref[0])
+    gate_ref[0] = gate.astype(BF16)
+    up_ref[0] = up.astype(BF16)
+    activ = (gate * jax.nn.sigmoid(gate) * up).astype(BF16)
+    cut = first_ref.shape[-1]
+    first_ref[0] = activ[:, :cut]
+    second_ref[0] = activ[:, cut:]
+
+
+def ff_back_kernel(dout_ref, wd_ref, gate_ref, up_ref, dgate_ref, dup_ref):
+    d_activ = nn(dout_ref[...], wd_ref[0])
+    gate, up = gate_ref[0].astype(F32), up_ref[0].astype(F32)
+    sig = jax.nn.sigmoid(gate)
+    dgate_ref[0] = (d_activ * up * (sig * (1.0 + gate * (1.0 - sig)))).astype(BF16)
+    dup_ref[0] = (d_activ * (gate * sig)).astype(BF16)
+
+
+def feed_kernel(first_ref, second_ref, wd_ref, middle_ref, out_ref):
+    total = middle_ref[...]
+    cut = first_ref.shape[-1]
+    for p in range(2):
+        total += nt(first_ref[p], wd_ref[p, :, :cut]) + nt(second_ref[p], wd_ref[p, :, cut:])
+    out_ref[...] = total.astype(BF16)
+
+
+def middle_back_kernel(
+    dgate_ref, dup_ref, wg_ref, wu_ref, w0, w1, w2, w3, middle_ref, dout_ref, gain_ref,
+    dmiddle_ref, dmix_ref, dmixed_ref, dgain_ref,
+):
+    @pl.when(pl.program_id(0) == 0)
+    def _():
+        dgain_ref[...] = jnp.zeros_like(dgain_ref)
+
+    grad = nt(dgate_ref[0], wg_ref[0]) + nt(dup_ref[0], wu_ref[0])
+    grad += nt(dgate_ref[1], wg_ref[1]) + nt(dup_ref[1], wu_ref[1])
+    normed, scale = rms_rows(middle_ref[...])
+    dgain_ref[...] += jnp.sum(grad * normed, axis=0, keepdims=True)
+    dmiddle = dout_ref[...].astype(F32) + rms_rows_back(normed, scale, gain_ref[...], grad)
+    dmiddle_ref[...] = dmiddle
+    dmix = dmiddle.astype(BF16)
+    dmix_ref[...] = dmix
+    for p in range(2):
+        dmixed_ref[:, p * 512 : (p + 1) * 512] = nn(dmix, output_rows((w0, w1, w2, w3), p)).astype(BF16)
+
+
+def input_back_kernel(
+    da_ref, db_ref, wa_ref, wb_ref, drank_ref, first_ref, hidden_ref, dmiddle_ref, gain_ref,
+    out_ref, dgain_ref,
+):
+    @pl.when(pl.program_id(0) == 0)
+    def _():
+        dgain_ref[...] = jnp.zeros_like(dgain_ref)
+
+    grad = nt(drank_ref[...].astype(BF16), first_ref[...].astype(BF16))
+    for p in range(2):
+        grad += nt(da_ref[p], wa_ref[p]) + nt(db_ref[p], wb_ref[p])
+    normed, scale = rms_rows(hidden_ref[...].astype(F32))
+    dgain_ref[...] += jnp.sum(grad * normed, axis=0, keepdims=True)
+    back = rms_rows_back(normed, scale, gain_ref[...], grad)
+    out_ref[...] = (dmiddle_ref[...] + back).astype(BF16)
+
+
+def grad_other_kernel(pairs, bits, *refs):
+    out = refs[-1]
+    rows = refs[0].shape[1] * refs[0].shape[2]
+    at = 0
+    for i in range(pairs):
+        left, right = refs[2 * i], refs[2 * i + 1]
+        cols = right.shape[-1]
+        result = nn(left[0].reshape(rows, left.shape[-1]), right[0]).astype(BF16)
+        out[0, :, :, at : at + cols] = result.reshape(out.shape[1], out.shape[2], cols)
+        at += cols
+
+
+def grad_mine_kernel(pairs, bits, *refs):
+    got, send, keep = refs[2 * pairs :]
+    first = pl.program_id(0) == 0
+    at = 0
+    for i in range(pairs):
+        left, right = refs[2 * i], refs[2 * i + 1]
+        cols = slice(at, at + right.shape[-1])
+        at += right.shape[-1]
+        result = (nn(left[0, 0], right[0]) + got[0, 0, :, cols].astype(F32)).astype(BF16)
+
+        @pl.when(first)
+        def _(result=result, cols=cols):
+            send[0, :, cols] = result
+
+        @pl.when(jnp.logical_not(first))
+        def _(result=result, cols=cols):
+            keep[0, :, cols] = result
+
+
+def add(x, y):
+    return (x.astype(F32) + y.astype(F32)).astype(BF16)
+
+
+def fold_kernel(bits, ka, ga, kb, gb, sa, na, sb, nb):
+    p, x = bits[2], bits[1]
+    sa[...] = add(ka[1 - p], ga[1 - p])
+    na[...] = add(ka[p], ga[p])
+    sb[...] = add(kb[1 - x], gb[1 - x])
+    nb[...] = add(kb[x], gb[x])
+
+
+def join_kernel(bits, ka, ga, kb, gb, send, keep):
+    z, cut = bits[3], ka.shape[-1]
+    send[:, :cut] = add(ka[1 - z], ga[1 - z])
+    send[:, cut:] = add(kb[1 - z], gb[1 - z])
+    keep[:, :cut] = add(ka[z], ga[z])
+    keep[:, cut:] = add(kb[z], gb[z])
+
+
 def shape(dims, dtype):
     return jax.ShapeDtypeStruct(dims, dtype)
 
 
-def call(kernel, blocks, in_specs, out_specs, out_shape, scratch, cost):
+def call(kernel, grid, in_specs, out_specs, out_shape, scratch, cost, prefetch=1):
+    grid = grid if isinstance(grid, tuple) else (grid,)
     return pl.pallas_call(
         kernel,
         grid_spec=pltpu.PrefetchScalarGridSpec(
-            num_scalar_prefetch=1,
-            grid=(blocks,),
+            num_scalar_prefetch=prefetch,
+            grid=grid,
             in_specs=in_specs,
             out_specs=out_specs,
             scratch_shapes=scratch,
         ),
         out_shape=out_shape,
         compiler_params=pltpu.CompilerParams(
-            dimension_semantics=("arbitrary",), vmem_limit_bytes=VMEM_BYTES
+            dimension_semantics=("arbitrary",) * len(grid), vmem_limit_bytes=VMEM_BYTES
         ),
         cost_estimate=pl.CostEstimate(flops=cost, bytes_accessed=16 << 20, transcendentals=1 << 20),
     )
@@ -335,16 +478,13 @@
     return shard.transpose(order).reshape(2, -1, shard.shape[-1])
 
 
-def by_core(act):
+def owner_rows(act):
     rows = act.shape[0]
     z = len(long_strides())
     own = act.shape[1] // lax.axis_size("dp")
     split = act.reshape((rows,) + (2,) * (z + 2) + (own,))
-    split = split.transpose([0, z + 2, z + 1] + list(range(1, z + 1))[::-1] + [z + 3])
-    core = own_bit(1)
-    other = lax.dynamic_index_in_dim(split, 1 - core, 1, keepdims=False).reshape(rows, -1)
-    mine = lax.dynamic_index_in_dim(split, core, 1, keepdims=False).reshape(rows, -1)
-    return other, mine
+    split = split.transpose([z + 2, z + 1] + list(range(1, z + 1))[::-1] + [z + 3, 0])
+    return split.reshape(2, 2, -1, rows)
 
 
 def fence(*values):
@@ -357,38 +497,111 @@
     return fence(work(*inputs), got)
 
 
-def products(equation, act, parts):
-    return [jnp.einsum(equation, act, part, preferred_element_type=F32).astype(BF16) for part in parts]
+def grad_other(bits, pairs):
+    own, rows = pairs[0][0].shape[2:]
+    cols = sum(right.shape[-1] for _, right in pairs)
+    in_specs = []
+    for _, right in pairs:
+        in_specs.append(pl.BlockSpec((1, 2, own, rows), lambda p, b: (1 - b[0], 0, 0, 0)))
+        in_specs.append(pl.BlockSpec((1, rows, right.shape[-1]), lambda p, b: (p, 0, 0)))
+    return call(
+        functools.partial(grad_other_kernel, len(pairs)),
+        2,
+        in_specs,
+        pl.BlockSpec((1, 2, own, cols), lambda p, b: (p, 0, 0, 0)),
+        shape((2, 2, own, cols), BF16),
+        [],
+        8 * own * rows * cols,
+    )(bits, *[array for pair in pairs for array in pair])
+
+
+def grad_mine(bits, pairs, got, by_x):
+    own, rows = pairs[0][0].shape[2:]
+    cols = got.shape[-1]
+
+    def x_of(s, j, b):
+        return b[1] ^ 1 ^ s if by_x else j
+
+    def p_of(s, j, b):
+        return j if by_x else b[2] ^ 1 ^ s
+
+    in_specs = []
+    for _, right in pairs:
+        in_specs.append(
+            pl.BlockSpec((1, 1, own, rows), lambda s, j, b: (b[0], x_of(s, j, b), 0, 0))
+        )
+        in_specs.append(
+            pl.BlockSpec((1, rows, right.shape[-1]), lambda s, j, b: (p_of(s, j, b), 0, 0))
+        )
+    in_specs.append(
+        pl.BlockSpec((1, 1, own, cols), lambda s, j, b: (p_of(s, j, b), x_of(s, j, b), 0, 0))
+    )
+    return call(
+        functools.partial(grad_mine_kernel, len(pairs)),
+        (2, 2),
+        in_specs,
+        [
+            pl.BlockSpec((1, own, cols), lambda s, j, b: (jnp.where(s == 0, j, 1), 0, 0)),
+            pl.BlockSpec((1, own, cols), lambda s, j, b: (jnp.where(s == 0, 0, j), 0, 0)),
+        ],
+        [shape((2, own, cols), BF16)] * 2,
+        [],
+        8 * own * rows * cols,
+    )(bits, *[array for pair in pairs for array in pair], got)
+
+
+def whole(kernel, bits, arrays, outs):
+    def spec(dims):
+        return pl.BlockSpec(dims, lambda i, b: (0,) * len(dims))
+
+    return call(
+        kernel, 1, [spec(a.shape) for a in arrays], [spec(dims) for dims in outs],
+        [shape(dims, BF16) for dims in outs], [], 1 << 20,
+    )(bits, *arrays)
 
 
 class Halving:
-    def __init__(self, parts, got, firsts):
-        self.orders = [[2, 0] if first == 2 else [0, 2] for first in firsts]
-        self.orders = [order + long_strides() for order in self.orders]
-        self.parts = [
-            (part + extra).reshape((2, 2) + (2,) * len(long_strides()) + (-1, part.shape[-1]))
-            for part, extra in zip(parts, got)
-        ]
+    def __init__(self, bits, first, second):
+        self.bits, self.stage = bits, 0
+        (sa, ka), (sb, kb) = first, second
+        self.keep, self.out, self.cut = [ka, kb], [(sa, 2), (sb, 0)], ka.shape[-1]
 
     def sends(self):
-        self.kept, out = [], []
-        for i, part in enumerate(self.parts):
-            stride = self.orders[i][0]
-            axis = 1 if stride == 2 and len(self.orders[i]) == len(long_strides()) + 2 else 0
-            bit = own_bit(stride)
-            self.kept.append(lax.dynamic_index_in_dim(part, bit, axis, keepdims=False))
-            out.append((lax.dynamic_index_in_dim(part, 1 - bit, axis, keepdims=False), stride))
-        return out
+        return self.out
 
     def receive(self, got):
-        self.parts = [kept + extra for kept, extra in zip(self.kept, got)]
-        self.orders = [order[1:] for order in self.orders]
+        strides = long_strides()
+        if self.stage == 0:
+            (ka, kb), (ga, gb) = self.keep, got
+            half_a, half_b = ka.shape[1:], kb.shape[1:]
+            sa, na, sb, nb = whole(
+                fold_kernel, self.bits, [ka, ga, kb, gb], [half_a, half_a, half_b, half_b]
+            )
+            self.keep, self.out = [na, nb], [(sa, 0), (sb, 2)]
+        elif self.stage == 1:
+            arrays = [
+                a.reshape(2, -1, a.shape[-1]) for a in (self.keep[0], got[0], self.keep[1], got[1])
+            ]
+            dims = (arrays[0].shape[1], arrays[0].shape[2] + arrays[2].shape[2])
+            send, self.keep = whole(join_kernel, self.bits, arrays, [dims, dims])
+            self.out = [(send, strides[0])]
+        else:
+            total = self.keep + got[0]
+            place = self.stage - 1
+            if place < len(strides):
+                total = total.reshape(2, -1, total.shape[-1])
+                bit = own_bit(strides[place])
+                self.keep = lax.dynamic_index_in_dim(total, bit, 0, keepdims=False)
+                send = lax.dynamic_index_in_dim(total, 1 - bit, 0, keepdims=False)
+                self.out = [(send, strides[place])]
+            else:
+                self.keep, self.out = total.astype(F32), []
+        self.stage += 1
 
     def finish(self):
-        while self.orders[0]:
-            sends = self.sends()
-            self.receive([swap(array, stride) for array, stride in sends])
-        return [part.astype(F32) for part in self.parts]
+        while self.out:
+            self.receive([swap(array, stride) for array, stride in self.out])
+        return self.keep[:, : self.cut], self.keep[:, self.cut :]
 
 
 def total_sum(x):
@@ -423,10 +636,10 @@
     )
     w_in_b = gather_steps(jnp.concatenate([value_weight[:, 256:], outgate_weight], axis=1), (0, 2))
     w_rest = gather(
-        jnp.concatenate([gate_weight, up_weight, output_weight.T, down_weight.T], axis=1)
-    )
-    w_gu, w_out = w_rest[..., : 2 * half], w_rest[..., 2 * half : 2 * half + 512]
-    w_down = w_rest[..., 2 * half + 512 :]
+        jnp.concatenate([gate_weight, up_weight, down_weight.T, output_weight.T], axis=1)
+    )
+    dp_at = lax.axis_index("dp")
+    bits = jnp.stack([dp_at % 2, (dp_at // 2) % 2, place, (dp_at // 4) % 2]).astype(jnp.int32)
 
     resid = hidden_in.astype(F32)
     normed_a = (rms(resid, 1e-6) * mixer_gain).astype(BF16)
@@ -455,83 +668,137 @@
         [(final_state.astype(BF16), 0)], outgate_product, normed_a, w_in_b[..., 256:]
     )
     state_in = jnp.where(place == 0, jnp.zeros_like(state_in), state_in)
-    mixed, core, states = call(
+    mixed, mixed_a, mixed_b, core, states = call(
         core_kernel,
         blocks,
         [p_spec(256, 0), p_spec(256, 1), p_spec(256, 2), p_spec(256, 0), p_spec(256, 0), p_spec(256, 1),
          r_spec(512), r_spec(1), row_spec, f_spec(HEADS, KEY, VAL), f_spec(1, VAL)],
-        [r_spec(1024), r_spec(1024), s_spec],
-        [shape((rows, 1024), BF16), shape((rows, 1024), BF16),
+        [r_spec(1024), p_spec(256, 0), p_spec(256, 0), r_spec(1024), s_spec],
+        [shape((rows, 1024), BF16), shape((2, rows, 256), BF16), shape((2, rows, 256), BF16),
+         shape((rows, 1024), BF16),
          shape((blocks, HEADS, KEY, VAL), BF16)],
         [pltpu.VMEM((HEADS, KEY, VAL), F32)],
         1 << 30,
     )(info, proj_a, proj_a, proj_a, proj_v, proj_og, proj_og, cum, seg, seg_row, state_in, gain)
-    middle = resid + nt(mixed[:, :512], w_out[0]) + nt(mixed[:, 512:], w_out[1])
-
-    normed_b = (rms(middle, 1e-6) * feed_gain).astype(BF16)
-    pre = jnp.einsum("td,pdc->ptc", normed_b, w_gu, preferred_element_type=F32).astype(BF16)
-    activ = (jax.nn.silu(pre[..., :half].astype(F32)) * pre[..., half:].astype(F32)).astype(BF16)
-
-    ff_out, ff_in, mix_in = "to,ptc->poc", "td,ptc->pdc", "td,ptc->pdc"
-    other, mine = by_core(cotangent)
-    halves = [activ[..., :768], activ[..., 768:]]
-    sent = products(ff_out, other, halves)
-    kept, got = during([(part, 1) for part in sent], lambda a, *b: products(ff_out, a, b), mine, *halves)
-    down = Halving(kept, got, (2, 0))
-
-    def activation_back(dout, weight, gate_pre, up_pre):
-        d_activ = jnp.einsum("to,poc->ptc", dout, weight, preferred_element_type=F32)
-        gate_pre, up_pre = gate_pre.astype(F32), up_pre.astype(F32)
-        sig = jax.nn.sigmoid(gate_pre)
-        d_gate = (d_activ * up_pre * (sig * (1.0 + gate_pre * (1.0 - sig)))).astype(BF16)
-        return d_gate, (d_activ * (gate_pre * sig)).astype(BF16)
-
+
+    tiles = rows // TILE
+    cut = 768
+    place_out = 3 * half // 128
+
+    def tile(cols):
+        return pl.BlockSpec((TILE, cols), lambda m: (m, 0))
+
+    def tile_pair(cols):
+        return pl.BlockSpec((2, TILE, cols), lambda m: (0, m, 0))
+
+    def keep(*dims, at=None):
+        return pl.BlockSpec(dims, lambda m: at or (0,) * len(dims))
+
+    def part(cols):
+        return pl.BlockSpec((1, TILE, cols), lambda p, m: (p, m, 0))
+
+    def part_weight(at):
+        return pl.BlockSpec((1, width, half), lambda p, m: (p, 0, at))
+
+    part_rows = pl.BlockSpec((TILE, width), lambda p, m: (m, 0))
+    w_out = [keep(2, width, 128, at=(0, 0, place_out + i)) for i in range(4)]
+    gain_b, gain_a = feed_gain.reshape(1, width), mixer_gain.reshape(1, width)
+    middle, normed_b = call(
+        middle_kernel,
+        tiles,
+        [tile(1024), *w_out, tile(width), keep(1, width)],
+        [tile(width), tile(width)],
+        [shape((rows, width), F32), shape((rows, width), BF16)],
+        [],
+        2 * rows * width * 1024,
+        0,
+    )(mixed, w_rest, w_rest, w_rest, w_rest, hidden_in, gain_b)
+    wide = shape((2, rows, half), BF16)
+    gate_pre, up_pre, activ_a, activ_b = call(
+        ff_kernel,
+        (2, tiles),
+        [part_rows, part_weight(0), part_weight(1)],
+        [part(half), part(half), part(cut), part(half - cut)],
+        [wide, wide, shape((2, rows, cut), BF16), shape((2, rows, half - cut), BF16)],
+        [],
+        8 * rows * width * half,
+        0,
+    )(normed_b, w_rest, w_rest)
+
+    def ff_back(dout, weight, gate_pre, up_pre):
+        return call(
+            ff_back_kernel,
+            (2, tiles),
+            [part_rows, part_weight(2), part(half), part(half)],
+            [part(half), part(half)],
+            [wide, wide],
+            [],
+            4 * rows * width * half,
+            0,
+        )(dout, weight, gate_pre, up_pre)
+
+    dout_rows = owner_rows(cotangent)
+    sent = [grad_other(bits, [(dout_rows, activ)]) for activ in (activ_a, activ_b)]
     (d_gate, d_up), got = during(
-        down.sends(), activation_back, cotangent, w_down, pre[..., :half], pre[..., half:]
+        [(array, 1) for array in sent], ff_back, cotangent, w_rest, gate_pre, up_pre
+    )
+    down = Halving(
+        bits,
+        grad_mine(bits, [(dout_rows, activ_a)], got[0], True),
+        grad_mine(bits, [(dout_rows, activ_b)], got[1], False),
+    )
+
+    def feed_and_other(activ_a, activ_b, weight, middle, normed_rows, d_gate, d_up):
+        block_out = call(
+            feed_kernel,
+            tiles,
+            [tile_pair(cut), tile_pair(half - cut), keep(2, width, half, at=(0, 0, 2)), tile(width)],
+            tile(width),
+            shape((rows, width), BF16),
+            [],
+            4 * rows * width * half,
+            0,
+        )(activ_a, activ_b, weight, middle)
+        return block_out, [grad_other(bits, [(normed_rows, grad)]) for grad in (d_gate, d_up)]
+
+    normed_rows = owner_rows(normed_b)
+    (block_out, sent), got = during(
+        down.sends(), feed_and_other, activ_a, activ_b, w_rest, middle, normed_rows, d_gate, d_up
     )
     down.receive(got)
 
-    other, mine = by_core(normed_b)
-    sent, got = during(
-        down.sends(), lambda a, *b: products(ff_in, a, b), other, d_gate, d_up
-    )
+    def middle_back(d_gate, d_up, weight, middle, dout):
+        return call(
+            middle_back_kernel,
+            tiles,
+            [tile_pair(half), tile_pair(half), keep(2, width, half), keep(2, width, half, at=(0, 0, 1)),
+             *w_out, tile(width), tile(width), keep(1, width)],
+            [tile(width), tile(width), tile(1024), keep(1, width)],
+            [shape((rows, width), F32), shape((rows, width), BF16), shape((rows, 1024), BF16),
+             shape((1, width), F32)],
+            [],
+            8 * rows * width * half,
+            0,
+        )(d_gate, d_up, weight, weight, weight, weight, weight, weight, middle, dout, gain_b)
+
+    (d_middle, d_mix, d_mixed, feed_gain_grad), got = during(
+        [(array, 1) for array in sent] + down.sends(), middle_back, d_gate, d_up, w_rest, middle, cotangent
+    )
+    down.receive(got[2:])
+
+    def mine_grads(normed_rows, d_gate, d_up, got_gate, got_up):
+        return (
+            grad_mine(bits, [(normed_rows, d_gate)], got_gate, True),
+            grad_mine(bits, [(normed_rows, d_up)], got_up, False),
+        )
+
+    (first, second), got = during(down.sends(), mine_grads, normed_rows, d_gate, d_up, *got[:2])
     down.receive(got)
-
-    def mine_and_out(act, *operands):
-        grads = products(ff_in, act, operands[:2])
-        return grads, nt(operands[2][0], operands[3][0]) + nt(operands[2][1], operands[3][1])
-
-    (kept, feed_out), got = during(
-        [(part, 1) for part in sent] + down.sends(), mine_and_out, mine, d_gate, d_up, activ, w_down
-    )
-    block_out = (middle + feed_out).astype(BF16)
-    down.receive(got[2:])
-    gate_up = Halving(kept, got[:2], (2, 0))
-
-    def middle_back(d_gate, d_up, w_gu, middle, w_out):
-        d_normed_b = (
-            nt(d_gate[0], w_gu[0, :, :half])
-            + nt(d_up[0], w_gu[0, :, half:])
-            + nt(d_gate[1], w_gu[1, :, :half])
-            + nt(d_up[1], w_gu[1, :, half:])
-        )
-        back, feed_gain_grad = rms_back(middle, feed_gain, 1e-6, d_normed_b)
-        d_middle = cotangent.astype(F32) + back
-        d_mix = d_middle.astype(BF16)
-        d_mixed = jnp.concatenate([nn(d_mix, w_out[0]), nn(d_mix, w_out[1])], axis=1).astype(BF16)
-        return d_middle, d_mix, d_mixed, feed_gain_grad
-
-    (d_middle, d_mix, d_mixed, feed_gain_grad), got = during(
-        gate_up.sends() + down.sends(), middle_back, d_gate, d_up, w_gu, middle, w_out
-    )
-    gate_up.receive(got[:2])
-    down.receive(got[2:])
-    own_down = down.finish()
-
-    mixed_split = mixed.reshape(rows, 2, 512).transpose(1, 0, 2)
-    mixed_halves = [mixed_split[..., :256], mixed_split[..., 256:]]
-
-    def post_back(d_mixed, d_mix, *mixed_halves):
+    gate_up = Halving(bits, first, second)
+
+    p_back, r_back, f_back, row_back, s_back = specs(blocks, True)
+
+    def mixer_back(d_mixed):
         d_core, d_og, head_gain_grad, d_state = call(
             post_kernel,
             blocks,
@@ -542,83 +809,72 @@
             [pltpu.VMEM((1, 512), F32)],
             1 << 29,
         )(info, d_mixed, core, proj_og, proj_og, proj_a, cum, seg, gain)
-        other, mine = by_core(d_mix)
-        (sent, kept), (d_state_in,) = during(
-            [(d_state.astype(BF16), 0)],
-            lambda a, b, *c: (products(ff_out, a, c), products(ff_out, b, c)),
-            other, mine, *mixed_halves,
-        )
-        return d_core, d_og, head_gain_grad, d_state_in, sent, kept
-
-    (d_core, d_og, head_gain_grad, d_state_in, sent, kept), got = during(
-        gate_up.sends(), post_back, d_mixed, d_mix, *mixed_halves
-    )
-    gate_up.receive(got)
-    d_state_in = jnp.where(place == 1, jnp.zeros_like(d_state_in), d_state_in)
-    p_spec, r_spec, f_spec, row_spec, s_spec = specs(blocks, True)
-
-    def core_back(d_core, d_og, d_state_in):
-        return call(
+        mix_rows, (d_state_in,) = during([(d_state.astype(BF16), 0)], owner_rows, d_mix)
+        d_state_in = jnp.where(place == 1, jnp.zeros_like(d_state_in), d_state_in)
+        d_a, d_b, d_rank, low_second_grad, bias_grad = call(
             back_kernel,
             blocks,
-            [p_spec(256, 0), p_spec(256, 1), p_spec(256, 2), p_spec(256, 0), p_spec(512, 0),
-             r_spec(512), r_spec(512), s_spec, r_spec(1024), r_spec(1), row_spec,
-             f_spec(HEADS, KEY, VAL), f_spec(16, 512), r_spec(16)],
-            [p_spec(768, 0), p_spec(768, 0), r_spec(16), f_spec(16, 512), f_spec(1, 512)],
+            [p_back(256, 0), p_back(256, 1), p_back(256, 2), p_back(256, 0), p_back(512, 0),
+             r_back(512), r_back(512), s_back, r_back(1024), r_back(1), row_back,
+             f_back(HEADS, KEY, VAL), f_back(16, 512), r_back(16)],
+            [p_back(768, 0), p_back(768, 0), r_back(16), f_back(16, 512), f_back(1, 512)],
             [shape((2, rows, 768), BF16), shape((2, rows, 768), BF16), shape((rows, 16), F32),
              shape((16, 512), F32), shape((1, 512), F32)],
             [pltpu.VMEM((HEADS, KEY, VAL), F32)],
             3 << 30,
         )(info, proj_a, proj_a, proj_a, proj_v, d_og, cum, sig, states, d_core, seg, seg_row,
           d_state_in, low_second, lowrank)
-
-    (d_a, d_b, d_rank, low_second_grad, bias_grad), got = during(
-        gate_up.sends() + [(part, 1) for part in sent], core_back, d_core, d_og, d_state_in
+        return mix_rows, head_gain_grad, d_a, d_b, d_rank, low_second_grad, bias_grad
+
+    (mix_rows, head_gain_grad, d_a, d_b, d_rank, low_second_grad, bias_grad), got = during(
+        gate_up.sends() + down.sends(), mixer_back, d_mixed
     )
     gate_up.receive(got[:2])
-    out = Halving(kept, got[2:], (2, 0))
-
-    other, mine = by_core(normed_a)
-    sent, got = during(
-        gate_up.sends() + out.sends(), lambda a, *b: products(mix_in, a, b), other, d_a, d_b
-    )
-    gate_up.receive(got[:2])
-    out.receive(got[2:])
+    down.receive(got[2:])
+    own_down = down.finish()
+
+    def other_mix(normed_rows, mix_rows, d_a, d_b, mixed_a, mixed_b):
+        return (
+            grad_other(bits, [(normed_rows, d_a), (mix_rows, mixed_a)]),
+            grad_other(bits, [(normed_rows, d_b), (mix_rows, mixed_b)]),
+        )
+
+    def mine_mix(normed_rows, mix_rows, d_a, d_b, mixed_a, mixed_b, got_a, got_b):
+        return (
+            grad_mine(bits, [(normed_rows, d_a), (mix_rows, mixed_a)], got_a, True),
+            grad_mine(bits, [(normed_rows, d_b), (mix_rows, mixed_b)], got_b, False),
+        )
+
+    mix_operands = (owner_rows(normed_a), mix_rows, d_a, d_b, mixed_a, mixed_b)
+    sent, got = during(gate_up.sends(), other_mix, *mix_operands)
+    gate_up.receive(got)
+
+    def input_back(d_a, d_b, w_a, w_b, d_rank, d_middle):
+        low_first_grad = tn(normed_a, d_rank.astype(BF16))
+        input_grad, mixer_gain_grad = call(
+            input_back_kernel,
+            tiles,
+            [tile_pair(768), tile_pair(768), keep(2, width, 768), keep(2, width, 768), tile(16),
+             keep(width, 16), tile(width), tile(width), keep(1, width)],
+            [tile(width), keep(1, width)],
+            [shape((rows, width), BF16), shape((1, width), F32)],
+            [],
+            4 * rows * width * 1536,
+            0,
+        )(d_a, d_b, w_a, w_b, d_rank, low_first, hidden_in, d_middle, gain_a)
+        return input_grad, mixer_gain_grad, low_first_grad
+
+    (input_grad, mixer_gain_grad, low_first_grad), got = during(
+        [(array, 1) for array in sent] + gate_up.sends(),
+        input_back, d_a, d_b, w_in_a, w_in_b, d_rank, d_middle,
+    )
+    gate_up.receive(got[2:])
+    (first, second), got = during(gate_up.sends(), mine_mix, *mix_operands, *got[:2])
+    gate_up.receive(got)
+    mix = Halving(bits, first, second)
     own_gate, own_up = gate_up.finish()
-    kept, got = during(
-        [(part, 1) for part in sent] + out.sends(), lambda a, *b: products(mix_in, a, b), mine, d_a, d_b
-    )
-    out.receive(got[2:])
-    mix = Halving(kept, got[:2], (2, 0))
-
-    def input_back(d_a, d_b, d_rank, w_a, w_b):
-        low_first_grad = tn(normed_a, d_rank.astype(BF16))
-        d_normed_a = (
-            nt(d_a[0], w_a[0])
-            + nt(d_a[1], w_a[1])
-            + nt(d_b[0], w_b[0])
-            + nt(d_b[1], w_b[1])
-            + nt(d_rank.astype(BF16), low_first.astype(BF16))
-        )
-        return d_normed_a, low_first_grad
-
-    (d_normed_a, low_first_grad), got = during(
-        mix.sends() + out.sends(), input_back, d_a, d_b, d_rank, w_in_a, w_in_b
-    )
-    mix.receive(got[:2])
-    out.receive(got[2:])
-
-    def input_end(d_normed_a, d_middle):
-        back, mixer_gain_grad = rms_back(resid, mixer_gain, 1e-6, d_normed_a)
-        return (d_middle + back).astype(BF16), mixer_gain_grad
-
-    (input_grad, mixer_gain_grad), got = during(
-        mix.sends() + out.sends(), input_end, d_normed_a, d_middle
-    )
-    mix.receive(got[:2])
-    out.receive(got[2:])
-    own_out = out.finish()
     own_a, own_b = mix.finish()
+    own_out = [own_a[:, 768:], own_b[:, 768:]]
 
     parts = (mixer_gain_grad, feed_gain_grad, low_first_grad, low_second_grad, bias_grad, head_gain_grad)
     flat = total_sum(jnp.concatenate([part.reshape(-1, 128) for part in parts]))
@@ -634,8 +890,8 @@
         input_grad,
         own_a[:, :256],
         own_a[:, 256:512],
-        jnp.concatenate([own_a[:, 512:], own_b[:, :256]], axis=1),
-        own_b[:, 256:],
+        jnp.concatenate([own_a[:, 512:768], own_b[:, :256]], axis=1),
+        own_b[:, 256:768],
         jnp.concatenate([part.T for part in own_out], axis=0),
         own_gate,
         own_up,

time: 635 us -> 565 us (0.89)
  Pallas kernels: 52.5 us -> 266 us
  matrix products: 169 us -> 15.7 us
  local copies, waits for them, and re-layouts: 121 us -> 42 us
  other arithmetic: 75.5 us -> 28.2 us
  starting transfers between devices: 58 us -> 41.8 us
  waiting for transfers between devices: 132 us -> 146 us
    pallas_call x2 -> x26, Pallas kernels: 31.1 us -> 242 us  [the longest x6 52.7 us: grad_mine(): call(functools.partial(grad_mine_kernel, len(pairs)), (2, 2), in_specs, [...]
    dot_general x33 -> x0, matrix products: 156 us -> none  [the longest x13 58.1 us: nt(): lax.dot_general(a, b, (((1,), (1,)), ((), ())), preferred_element_type=F32)]
    add x32 -> x3, other arithmetic: 29.7 us -> 0.38 us  [receive(): total = self.keep + got[0]]
    unnamed x194 -> x94, local copies, waits for them, and re-layouts: 40.4 us -> 14.3 us
    slice x10 -> x2, local copies, waits for them, and re-layouts: 25 us -> 1.56 us  [the longest x1 0.9 us: finish(): return (self.keep[:, :self.cut], self.keep[:, self.cut:])]
    add x8 -> x0, local copies, waits for them, and re-layouts: 17.2 us -> none  [__init__(): part + extra]
    convert_element_type x10 -> x4, other arithmetic: 16.6 us -> 1.19 us  [the longest x1 1.07 us: mixer_back(): d_state.astype(BF16)]
    ppermute x44 -> x30, starting transfers between devices: 42.1 us -> 28.9 us  [swap(): lax.ppermute(x, 'dp', [(i, i ^ stride) for i in range(lax.axis_size('dp'))])]
  transfers between devices with their start and end apart: 58 -> 42, of which waited for: 17 -> 19; matrix products, arithmetic and copies ran while one was open for 29% -> 13% of each run, Pallas kernels for 7% -> 36%
where the time goes in v4:
time: 565 us; the launch traced here: 555 us
  Pallas kernels  266 us (47%)
  waiting for transfers between devices  146 us (26%)
  local copies, waits for them, and re-layouts  42 us (7%)
  starting transfers between devices  41.8 us (7%)
  other arithmetic  28.2 us (5%)
  matrix products  15.7 us (3%)
  between operations  15.3 us (3%)
    ppermute x30, waiting for transfers between devices, swap(): lax.ppermute(x, 'dp', [(i, i ^ stride) for i in range(lax.axis_size('dp'))])  80.2 us
    ppermute x11, waiting for transfers between devices, swap(): return lax.ppermute(x, 'tensor', [(0, 1), (1, 0)])  56.7 us
    pallas_call x6, Pallas kernels, grad_mine(): call(functools.partial(grad_mine_kernel, len(pairs)), (2, 2), in_specs, [...  52.7 us
    pallas_call x6, Pallas kernels, grad_other(): call(functools.partial(grad_other_kernel, len(pairs)), 2, in_specs, pl.Bl...  38.1 us
    ppermute x30, starting transfers between devices, swap(): lax.ppermute(x, 'dp', [(i, i ^ stride) for i in range(lax.axis_size('dp'))])  28.9 us
    pallas_call x1, Pallas kernels, middle_back(): call(middle_back_kernel, tiles, [tile_pair(half), tile_pair(half), keep(2...  24.5 us
    pallas_call x6, Pallas kernels, whole(): call(kernel, 1, [spec(a.shape) for a in arrays], [spec(dims) for dims in...  23.4 us
    pallas_call x1, Pallas kernels, mixer_back(): call(back_kernel, blocks, [p_back(256, 0), p_back(256, 1), p_back(256, 2)...  21.4 us
  transfers between devices with their start and end apart: 42, of which 19 were waited for; matrix products, arithmetic and copies ran while one was open for 13% of the time, Pallas kernels for 36%

profile of v4, /device:TPU:0, one launch (start us, length us, event | category | flops | bytes accessed | tf_op | source)
XLA Modules:
  0.0 554.8 jit_solution(12303474082731555006)
XLA Ops:
  25.2 13.1 %collective-permute-done.6 = bf16[2,64,768]{2,1,0:T(8,128)(2,1)S(1)} collective-permute-done((bf16[2,64,768]{2,1,0:T(8,128)(2,1)S(1)}, bf16[2,64,768]{2,1,0:T(8,128)(2,1)S(1)}, u32[]{:S(2)}, u32[]{:S(2)}) %collective-permute-start.6) | collective-permute-done | bytes 196640 | tf_op jit(solution)/shard_map/ppermute | solution.py:450
  48.8 9.3 %collective-permute-done.2 = bf16[2,2,64,768]{3,2,1,0:T(8,128)(2,1)S(1)} collective-permute-done((bf16[2,2,64,768]{3,2,1,0:T(8,128)(2,1)S(1)}, bf16[2,2,64,768]{3,2,1,0:T(8,128)(2,1)S(1)}, u32[]{:S(2)}, u32[]{:S(2)}) %collective-permute-start.2) | collective-permute-done | bytes 393248 | tf_op jit(solution)/shard_map/ppermute | solution.py:450
  61.5 24.6 %collective-permute-done.8 = bf16[2,2,2,64,768]{4,3,2,1,0:T(8,128)(2,1)S(1)} collective-permute-done((bf16[2,2,2,64,768]{4,3,2,1,0:T(8,128)(2,1)}, bf16[2,2,2,64,768]{4,3,2,1,0:T(8,128)(2,1)S(1)}, u32[]{:S(2)}, u32[]{:S(2)}) %collective-permute-start.8) | collective-permute-done | bytes 786464 | tf_op jit(solution)/shard_map/ppermute | solution.py:450
  120.4 11.4 %shard_map.288 = (f32[1024,512]{1,0:T(8,128)}, bf16[1024,512]{1,0:T(8,128)(2,1)}, f32[4,128,256]{2,1,0:T(8,128)}) custom-call(s32[2,8]{1,0:T(2,128)} %pad_add_fusion.info, f32[1024,16]{1,0:T(8,128)} %fusion.30.low_ref, f32[16,512]{1,0:T(8,128)} %second_ref.3, f32[1,512]{1,0:T(1,128)} %bitcast.248, ...), custom_call_target="tpu_custom_call" | custom-call | flops 536870912 | bytes 16777216 | tf_op jit(solution)/shard_map/pallas_call | solution.py:654
  138.5 9.0 %collective-permute-done.10 = bf16[4,128,256]{2,1,0:T(8,128)(2,1)S(1)} collective-permute-done((bf16[4,128,256]{2,1,0:T(8,128)(2,1)S(1)}, bf16[4,128,256]{2,1,0:T(8,128)(2,1)S(1)}, u32[]{:S(2)}, u32[]{:S(2)}) %collective-permute-start.10) | collective-permute-done | bytes 262176 | tf_op jit(solution)/shard_map/ppermute | solution.py:449
  148.1 12.6 %shard_map.289 = (bf16[1024,1024]{1,0:T(8,128)(2,1)}, bf16[2,1024,256]{2,1,0:T(8,128)(2,1)}, bf16[2,1024,256]{2,1,0:T(8,128)(2,1)}, bf16[1024,1024]{1,0:T(8,128)(2,1)}, bf16[8,4,128,256]{3,2,1,0:T(8,128)(2,1)}) custom-call(s32[2,8]{1,0:T(2,128)} %pad_add_fusion.info, bf16[2,1024,768]{2,1,0:T(8,128)(2,1)} %convert_bitcast_fusion.k_ref.v0_ref.q_ref, ...), custom_call_target="tpu_custom_call" | custom-call | flops 1073741824 | bytes 16777216 | tf_op jit(solution)/shard_map/pallas_call | solution.py:671
  160.8 9.2 %all-gather.2.cloned.1.call-done = bf16[2048,4736]{1,0:T(8,128)(2,1)} async-done(((bf16[64,4736]{1,0:T(8,128)(2,1)}), bf16[2048,4736]{1,0:T(8,128)(2,1)}) %all-gather.2.cloned.1.call-update) | async-done | bytes 19398672 | tf_op jit(solution)/shard_map/all_gather | solution.py:444
  177.3 20.9 %shard_map.291 = (bf16[2,1024,1408]{2,1,0:T(8,128)(2,1)}, bf16[2,1024,1408]{2,1,0:T(8,128)(2,1)}, bf16[2,1024,768]{2,1,0:T(8,128)(2,1)}, bf16[2,1024,640]{2,1,0:T(8,128)(2,1)}) custom-call(bf16[1024,1024]{1,0:T(8,128)(2,1)} %get-tuple-element.201.normed_ref, bf16[2,1024,4736]{2,1,0:T(8,128)(2,1)} %bitcast.165, bf16[2,1024,4736]{2,1,0:T(8,128)(2,1)} %bitcast.166), custom_call_target="tpu_custom_call" | custom-call | flops 11811160064 | bytes 16777216 | tf_op jit(solution)/shard_map/pallas_call | solution.py:717
  216.2 16.8 %shard_map.294 = (bf16[2,1024,1408]{2,1,0:T(8,128)(2,1)}, bf16[2,1024,1408]{2,1,0:T(8,128)(2,1)}) custom-call(bf16[1024,1024]{1,0:T(8,128)(2,1)} %dout_ref.1, bf16[2,1024,4736]{2,1,0:T(8,128)(2,1)} %bitcast.167, bf16[2,1024,1408]{2,1,0:T(8,128)(2,1)} %get-tuple-element.208.gate_ref, bf16[2,1024,1408]{2,1,0:T(8,128)(2,1)} %get-tuple-element.209.up_ref), custom_call_target="tpu_custom_call" | custom-call | flops 5905580032 | bytes 16777216 | tf_op jit(solution)/shard_map/pallas_call | solution.py:729
  257.0 7.5 %shard_map.298 = bf16[2,2,256,1408]{3,2,1,0:T(8,128)(2,1)} custom-call(s32[4]{0:T(128)} %pad_add_fusion.1.bits, bf16[2,2,256,1024]{3,2,1,0:T(8,128)(2,1)} %bitcast.209, bf16[2,1024,1408]{2,1,0:T(8,128)(2,1)} %get-tuple-element.260.refs_1_.dgate_ref), custom_call_target="tpu_custom_call" | custom-call | flops 2952790016 | bytes 16777216 | tf_op jit(solution)/shard_map/pallas_call | solution.py:507
  264.5 11.6 %shard_map.297 = bf16[1024,1024]{1,0:T(8,128)(2,1)} custom-call(bf16[2,1024,768]{2,1,0:T(8,128)(2,1)} %get-tuple-element.221.refs_1_.first_ref, bf16[2,1024,640]{2,1,0:T(8,128)(2,1)} %get-tuple-element.222.refs_1_.second_ref, bf16[2,1024,4736]{2,1,0:T(8,128)(2,1)} %bitcast.168, f32[1024,1024]{1,0:T(8,128)} %get-tuple-element.243.middle_ref), custom_call_target="tpu_custom_call" | custom-call | flops 5905580032 | bytes 16777216 | tf_op jit(solution)/shard_map/pallas_call | solution.py:752
  283.9 24.5 %shard_map.301 = (f32[1024,1024]{1,0:T(8,128)}, bf16[1024,1024]{1,0:T(8,128)(2,1)}, bf16[1024,1024]{1,0:T(8,128)(2,1)}, f32[1,1024]{1,0:T(1,128)}) custom-call(bf16[2,1024,1408]{2,1,0:T(8,128)(2,1)} %get-tuple-element.260.refs_1_.dgate_ref, bf16[2,1024,1408]{2,1,0:T(8,128)(2,1)} %get-tuple-element.264.refs_1_.dup_ref, bf16[2,1024,4736]{2,1,0:T(8,128)(2,1)} %bitcast.169, ...), custom_call_target="tpu_custom_call" | custom-call | flops 11811160064 | bytes 16777216 | tf_op jit(solution)/shard_map/pallas_call | solution.py:771
  313.3 9.6 %shard_map.304 = (bf16[2,256,1408]{2,1,0:T(8,128)(2,1)}, bf16[2,256,1408]{2,1,0:T(8,128)(2,1)}) custom-call(s32[4]{0:T(128)} %pad_add_fusion.1.bits, bf16[2,2,256,1024]{3,2,1,0:T(8,128)(2,1)} %bitcast.210, bf16[2,1024,1408]{2,1,0:T(8,128)(2,1)} %get-tuple-element.264.refs_1_.dup_ref, bf16[2,2,256,1408]{3,2,1,0:T(8,128)(2,1)} %collective-permute-done.16.refs_2_), custom_call_target="tpu_custom_call" | custom-call | flops 2952790016 | bytes 16777216 | tf_op jit(solution)/shard_map/pallas_call | solution.py:539
  322.9 9.9 %shard_map.303 = (bf16[2,256,1408]{2,1,0:T(8,128)(2,1)}, bf16[2,256,1408]{2,1,0:T(8,128)(2,1)}) custom-call(s32[4]{0:T(128)} %pad_add_fusion.1.bits, bf16[2,2,256,1024]{3,2,1,0:T(8,128)(2,1)} %bitcast.211, bf16[2,1024,1408]{2,1,0:T(8,128)(2,1)} %get-tuple-element.260.refs_1_.dgate_ref, bf16[2,2,256,1408]{3,2,1,0:T(8,128)(2,1)} %collective-permute-done.15.refs_2_), custom_call_target="tpu_custom_call" | custom-call | flops 2952790016 | bytes 16777216 | tf_op jit(solution)/shard_map/pallas_call | solution.py:539
  334.3 11.2 %shard_map.305 = (bf16[1024,1024]{1,0:T(8,128)(2,1)}, bf16[2,1024,512]{2,1,0:T(8,128)(2,1)}, f32[1,256]{1,0:T(1,128)}, f32[4,128,256]{2,1,0:T(8,128)}) custom-call(s32[2,8]{1,0:T(2,128)} %pad_add_fusion.info, bf16[1024,1024]{1,0:T(8,128)(2,1)} %get-tuple-element.275.dm_ref, bf16[1024,1024]{1,0:T(8,128)(2,1)} %get-tuple-element.276.core_ref, ...), custom_call_target="tpu_custom_call" | custom-call | flops 536870912 | bytes 16777216 | tf_op jit(solution)/shard_map/pallas_call | solution.py:802
  360.0 12.5 %collective-permute-done.20 = bf16[4,128,256]{2,1,0:T(8,128)(2,1)S(1)} collective-permute-done((bf16[4,128,256]{2,1,0:T(8,128)(2,1)S(1)}, bf16[4,128,256]{2,1,0:T(8,128)(2,1)S(1)}, u32[]{:S(2)}, u32[]{:S(2)}) %collective-permute-start.20) | collective-permute-done | bytes 262176 | tf_op jit(solution)/shard_map/ppermute | solution.py:449
  373.3 21.4 %shard_map.306 = (bf16[2,1024,768]{2,1,0:T(8,128)(2,1)}, bf16[2,1024,768]{2,1,0:T(8,128)(2,1)}, f32[1024,16]{1,0:T(8,128)}, f32[16,512]{1,0:T(8,128)}, f32[1,512]{1,0:T(1,128)}) custom-call(s32[2,8]{1,0:T(2,128)} %pad_add_fusion.info, bf16[2,1024,768]{2,1,0:T(8,128)(2,1)} %convert_bitcast_fusion.k_ref.v0_ref.q_ref, ...), custom_call_target="tpu_custom_call" | custom-call | flops 3221225472 | bytes 16777216 | tf_op jit(solution)/shard_map/pallas_call | solution.py:814
  424.8 13.7 %shard_map.311 = (bf16[1024,1024]{1,0:T(8,128)(2,1)}, f32[1,1024]{1,0:T(1,128)}) custom-call(bf16[2,1024,768]{2,1,0:T(8,128)(2,1)} %get-tuple-element.340.refs_1_.da_ref, bf16[2,1024,768]{2,1,0:T(8,128)(2,1)} %get-tuple-element.346.refs_1_.db_ref, bf16[2,1024,768]{2,1,0:T(8,128)(2,1)} %bitcast.201, bf16[2,1024,768]{2,1,0:T(8,128)(2,1)} %bitcast.190, ...), custom_call_target="tpu_custom_call" | custom-call | flops 6442450944 | bytes 16777216 | tf_op jit(solution)/shard_map/pallas_call | solution.py:854
  443.4 9.5 %shard_map.313 = (bf16[2,256,1024]{2,1,0:T(8,128)(2,1)}, bf16[2,256,1024]{2,1,0:T(8,128)(2,1)}) custom-call(s32[4]{0:T(128)} %pad_add_fusion.1.bits, bf16[2,2,256,1024]{3,2,1,0:T(8,128)(2,1)} %bitcast.181, bf16[2,1024,768]{2,1,0:T(8,128)(2,1)} %get-tuple-element.346.refs_1_.db_ref, bf16[2,2,256,1024]{3,2,1,0:T(8,128)(2,1)} %bitcast.185, ...), custom_call_target="tpu_custom_call" | custom-call | flops 2147483648 | bytes 16777216 | tf_op jit(solution)/shard_map/pallas_call | solution.py:539
  453.0 9.8 %shard_map.312 = (bf16[2,256,1024]{2,1,0:T(8,128)(2,1)}, bf16[2,256,1024]{2,1,0:T(8,128)(2,1)}) custom-call(s32[4]{0:T(128)} %pad_add_fusion.1.bits, bf16[2,2,256,1024]{3,2,1,0:T(8,128)(2,1)} %bitcast.182, bf16[2,1024,768]{2,1,0:T(8,128)(2,1)} %get-tuple-element.340.refs_1_.da_ref, bf16[2,2,256,1024]{3,2,1,0:T(8,128)(2,1)} %bitcast.186, ...), custom_call_target="tpu_custom_call" | custom-call | flops 2147483648 | bytes 16777216 | tf_op jit(solution)/shard_map/pallas_call | solution.py:539
  466.2 23.6 %collective-permute-done.36 = f32[214,128]{1,0:T(8,128)S(1)} collective-permute-done((f32[214,128]{1,0:T(8,128)S(1)}, f32[214,128]{1,0:T(8,128)S(1)}, u32[]{:S(2)}, u32[]{:S(2)}) %collective-permute-start.36) | collective-permute-done | bytes 109600 | tf_op jit(solution)/shard_map/ppermute | solution.py:449
  506.7 9.0 %collective-permute-done.32 = bf16[256,1024]{1,0:T(8,128)(2,1)S(1)} collective-permute-done((bf16[256,1024]{1,0:T(8,128)(2,1)}, bf16[256,1024]{1,0:T(8,128)(2,1)S(1)}, u32[]{:S(2)}, u32[]{:S(2)}) %collective-permute-start.32) | collective-permute-done | bytes 524320 | tf_op jit(solution)/shard_map/ppermute | solution.py:449
  524.0 8.9 %collective-permute-done.34 = bf16[128,2048]{1,0:T(8,128)(2,1)S(1)} collective-permute-done((bf16[128,2048]{1,0:T(8,128)(2,1)}, bf16[128,2048]{1,0:T(8,128)(2,1)S(1)}, u32[]{:S(2)}, u32[]{:S(2)}) %collective-permute-start.34) | collective-permute-done | bytes 524320 | tf_op jit(solution)/shard_map/ppermute | solution.py:450
  536.8 8.0 %collective-permute-done.35 = bf16[64,2048]{1,0:T(8,128)(2,1)S(1)} collective-permute-done((bf16[64,2048]{1,0:T(8,128)(2,1)S(1)}, bf16[64,2048]{1,0:T(8,128)(2,1)S(1)}, u32[]{:S(2)}, u32[]{:S(2)}) %collective-permute-start.35) | collective-permute-done | bytes 262176 | tf_op jit(solution)/shard_map/ppermute | solution.py:450
  (277 shorter events, 221.8 us)
Async XLA Ops:
  7.2 162.8 %all-gather.2.cloned.1.call-start = ((), (), s32[]{:S(2)}) async-start(), calls=%async_computation | async-start | bytes 20004864 | tf_op jit(solution)/shard_map/all_gather | solution.py:444
  24.2 19.3 %collective-permute-start.1 = (bf16[2,64,768]{2,1,0:T(8,128)(2,1)S(1)}, bf16[2,64,768]{2,1,0:T(8,128)(2,1)S(1)}, u32[]{:S(2)}, u32[]{:S(2)}) collective-permute-start(bf16[2,64,768]{2,1,0:T(8,128)(2,1)S(1)} %maximum_select_fusion.15), channel_id=1, source_target_pairs={{0,8},{2,10},{4,12},{6,14},{8,0},{10,2},{12,4},{14,6},{16,24},{18,... | collective-permute-start | bytes 589832 | tf_op jit(solution)/shard_map/ppermute | solution.py:450
  47.7 38.4 %collective-permute-start.8 = (bf16[2,2,2,64,768]{4,3,2,1,0:T(8,128)(2,1)}, bf16[2,2,2,64,768]{4,3,2,1,0:T(8,128)(2,1)S(1)}, u32[]{:S(2)}, u32[]{:S(2)}) collective-permute-start(bf16[2,2,2,64,768]{4,3,2,1,0:T(8,128)(2,1)} %maximum_select_fusion.9), channel_id=1, source_target_pairs={{0,4},{2,6},{4,0},{6,2},{8,12},{10,14},{12,8},{14,10},{16,20},{18,... | collective-permute-start | bytes 2359304 | tf_op jit(solution)/shard_map/ppermute | solution.py:450
  59.1 28.6 %collective-permute-start.3 = (bf16[2,2,2,64,768]{4,3,2,1,0:T(8,128)(2,1)}, bf16[2,2,2,64,768]{4,3,2,1,0:T(8,128)(2,1)}, u32[]{:S(2)}, u32[]{:S(2)}) collective-permute-start(bf16[2,2,2,64,768]{4,3,2,1,0:T(8,128)(2,1)} %maximum_select_fusion.7), channel_id=1, source_target_pairs={{0,1},{1,0},{2,3},{3,2},{4,5},{5,4},{6,7},{7,6},{8,9},{9,8},{10,11... | collective-permute-start | bytes 2359304 | tf_op jit(solution)/shard_map/ppermute | solution.py:449
  90.6 18.4 %collective-permute-start.4 = (bf16[2,2,2,2,64,768]{5,4,3,2,1,0:T(8,128)(2,1)}, bf16[2,2,2,2,64,768]{5,4,3,2,1,0:T(8,128)(2,1)}, u32[]{:S(2)}, u32[]{:S(2)}) collective-permute-start(bf16[2,2,2,2,64,768]{5,4,3,2,1,0:T(8,128)(2,1)} %maximum_select_fusion.3), channel_id=1, source_target_pairs={{0,2},{2,0},{4,6},{6,4},{8,10},{10,8},{12,14},{14,12},{16,18},{18,... | collective-permute-start | bytes 4718600 | tf_op jit(solution)/shard_map/ppermute | solution.py:450
  208.6 24.4 %collective-permute-start.11 = (bf16[2,2,256,768]{3,2,1,0:T(8,128)(2,1)}, bf16[2,2,256,768]{3,2,1,0:T(8,128)(2,1)}, u32[]{:S(2)}, u32[]{:S(2)}) collective-permute-start(bf16[2,2,256,768]{3,2,1,0:T(8,128)(2,1)} %shard_map.292), channel_id=1, source_target_pairs={{0,2},{2,0},{4,6},{6,4},{8,10},{10,8},{12,14},{14,12},{16,18},{18,... | collective-permute-start | bytes 4718600 | tf_op jit(solution)/shard_map/ppermute | solution.py:450
  208.9 24.1 %collective-permute-start.12 = (bf16[2,2,256,640]{3,2,1,0:T(8,128)(2,1)}, bf16[2,2,256,640]{3,2,1,0:T(8,128)(2,1)S(1)}, u32[]{:S(2)}, u32[]{:S(2)}) collective-permute-start(bf16[2,2,256,640]{3,2,1,0:T(8,128)(2,1)} %shard_map.293), channel_id=1, source_target_pairs={{0,2},{2,0},{4,6},{6,4},{8,10},{10,8},{12,14},{14,12},{16,18},{18,... | collective-permute-start | bytes 3932168 | tf_op jit(solution)/shard_map/ppermute | solution.py:450
  247.9 28.2 %collective-permute-start.13 = (bf16[2,256,768]{2,1,0:T(8,128)(2,1)}, bf16[2,256,768]{2,1,0:T(8,128)(2,1)S(1)}, u32[]{:S(2)}, u32[]{:S(2)}) collective-permute-start(bf16[2,256,768]{2,1,0:T(8,128)(2,1)} %get-tuple-element.228), channel_id=1, source_target_pairs={{0,4},{2,6},{4,0},{6,2},{8,12},{10,14},{12,8},{14,10},{16,20},{18,... | collective-permute-start | bytes 2359304 | tf_op jit(solution)/shard_map/ppermute | solution.py:450
  249.5 26.7 %collective-permute-start.14 = (bf16[2,256,640]{2,1,0:T(8,128)(2,1)S(1)}, bf16[2,256,640]{2,1,0:T(8,128)(2,1)S(1)}, u32[]{:S(2)}, u32[]{:S(2)}) collective-permute-start(bf16[2,256,640]{2,1,0:T(8,128)(2,1)S(1)} %copy-done.41), channel_id=1, source_target_pairs={{0,1},{1,0},{2,3},{3,2},{4,5},{5,4},{6,7},{7,6},{8,9},{9,8},{10,11... | collective-permute-start | bytes 1966088 | tf_op jit(solution)/shard_map/ppermute | solution.py:449
  280.9 27.4 %collective-permute-start.15 = (bf16[2,2,256,1408]{3,2,1,0:T(8,128)(2,1)}, bf16[2,2,256,1408]{3,2,1,0:T(8,128)(2,1)}, u32[]{:S(2)}, u32[]{:S(2)}) collective-permute-start(bf16[2,2,256,1408]{3,2,1,0:T(8,128)(2,1)} %shard_map.298), channel_id=1, source_target_pairs={{0,2},{2,0},{4,6},{6,4},{8,10},{10,8},{12,14},{14,12},{16,18},{18,... | collective-permute-start | bytes 8650760 | tf_op jit(solution)/shard_map/ppermute | solution.py:450
  281.0 27.4 %collective-permute-start.16 = (bf16[2,2,256,1408]{3,2,1,0:T(8,128)(2,1)}, bf16[2,2,256,1408]{3,2,1,0:T(8,128)(2,1)}, u32[]{:S(2)}, u32[]{:S(2)}) collective-permute-start(bf16[2,2,256,1408]{3,2,1,0:T(8,128)(2,1)} %shard_map.299), channel_id=1, source_target_pairs={{0,2},{2,0},{4,6},{6,4},{8,10},{10,8},{12,14},{14,12},{16,18},{18,... | collective-permute-start | bytes 8650760 | tf_op jit(solution)/shard_map/ppermute | solution.py:450
  281.5 26.9 %collective-permute-start.17 = (bf16[256,768]{1,0:T(8,128)(2,1)}, bf16[256,768]{1,0:T(8,128)(2,1)S(1)}, u32[]{:S(2)}, u32[]{:S(2)}) collective-permute-start(bf16[256,768]{1,0:T(8,128)(2,1)} %get-tuple-element.251), channel_id=1, source_target_pairs={{0,1},{1,0},{2,3},{3,2},{4,5},{5,4},{6,7},{7,6},{8,9},{9,8},{10,11... | collective-permute-start | bytes 1179656 | tf_op jit(solution)/shard_map/ppermute | solution.py:449
  283.4 25.0 %collective-permute-start.18 = (bf16[256,640]{1,0:T(8,128)(2,1)}, bf16[256,640]{1,0:T(8,128)(2,1)S(1)}, u32[]{:S(2)}, u32[]{:S(2)}) collective-permute-start(bf16[256,640]{1,0:T(8,128)(2,1)} %get-tuple-element.252), channel_id=1, source_target_pairs={{0,4},{2,6},{4,0},{6,2},{8,12},{10,14},{12,8},{14,10},{16,20},{18,... | collective-permute-start | bytes 983048 | tf_op jit(solution)/shard_map/ppermute | solution.py:450
  312.2 20.6 %collective-permute-start.19 = (bf16[128,1408]{1,0:T(8,128)(2,1)}, bf16[128,1408]{1,0:T(8,128)(2,1)S(1)}, u32[]{:S(2)}, u32[]{:S(2)}) collective-permute-start(bf16[128,1408]{1,0:T(8,128)(2,1)} %get-tuple-element.268), channel_id=1, source_target_pairs={{0,8},{2,10},{4,12},{6,14},{8,0},{10,2},{12,4},{14,6},{16,24},{18,... | collective-permute-start | bytes 1081352 | tf_op jit(solution)/shard_map/ppermute | solution.py:450
  332.9 61.8 %collective-permute-start.21 = (bf16[2,256,1408]{2,1,0:T(8,128)(2,1)}, bf16[2,256,1408]{2,1,0:T(8,128)(2,1)}, u32[]{:S(2)}, u32[]{:S(2)}) collective-permute-start(bf16[2,256,1408]{2,1,0:T(8,128)(2,1)} %get-tuple-element.293), channel_id=1, source_target_pairs={{0,4},{2,6},{4,0},{6,2},{8,12},{10,14},{12,8},{14,10},{16,20},{18,... | collective-permute-start | bytes 4325384 | tf_op jit(solution)/shard_map/ppermute | solution.py:450
  334.3 60.3 %collective-permute-start.22 = (bf16[2,256,1408]{2,1,0:T(8,128)(2,1)}, bf16[2,256,1408]{2,1,0:T(8,128)(2,1)}, u32[]{:S(2)}, u32[]{:S(2)}) collective-permute-start(bf16[2,256,1408]{2,1,0:T(8,128)(2,1)} %get-tuple-element.294), channel_id=1, source_target_pairs={{0,1},{1,0},{2,3},{3,2},{4,5},{5,4},{6,7},{7,6},{8,9},{9,8},{10,11... | collective-permute-start | bytes 4325384 | tf_op jit(solution)/shard_map/ppermute | solution.py:449
  346.6 25.9 %collective-permute-start.20 = (bf16[4,128,256]{2,1,0:T(8,128)(2,1)S(1)}, bf16[4,128,256]{2,1,0:T(8,128)(2,1)S(1)}, u32[]{:S(2)}, u32[]{:S(2)}) collective-permute-start(bf16[4,128,256]{2,1,0:T(8,128)(2,1)S(1)} %convert_element_type.54), channel_id=1, source_target_pairs={{0,1},{1,0},{2,3},{3,2},{4,5},{5,4},{6,7},{7,6},{8,9},{9,8},{10,11... | collective-permute-start | bytes 786440 | tf_op jit(solution)/shard_map/ppermute | solution.py:449
  357.6 37.0 %collective-permute-start.23 = (bf16[64,1408]{1,0:T(8,128)(2,1)S(1)}, bf16[64,1408]{1,0:T(8,128)(2,1)S(1)}, u32[]{:S(2)}, u32[]{:S(2)}) collective-permute-start(bf16[64,1408]{1,0:T(8,128)(2,1)S(1)} %dynamic-slice_bitcast_fusion.2), channel_id=1, source_target_pairs={{0,16},{2,18},{4,20},{6,22},{8,24},{10,26},{12,28},{14,30},{16,0},... | collective-permute-start | bytes 540680 | tf_op jit(solution)/shard_map/ppermute | solution.py:450
  421.0 19.8 %collective-permute-start.26 = (bf16[2,2,256,1024]{3,2,1,0:T(8,128)(2,1)}, bf16[2,2,256,1024]{3,2,1,0:T(8,128)(2,1)}, u32[]{:S(2)}, u32[]{:S(2)}) collective-permute-start(bf16[2,2,256,1024]{3,2,1,0:T(8,128)(2,1)} %shard_map.308), channel_id=1, source_target_pairs={{0,2},{2,0},{4,6},{6,4},{8,10},{10,8},{12,14},{14,12},{16,18},{18,... | collective-permute-start | bytes 6291464 | tf_op jit(solution)/shard_map/ppermute | solution.py:450
  421.0 19.8 %collective-permute-start.27 = (bf16[2,2,256,1024]{3,2,1,0:T(8,128)(2,1)}, bf16[2,2,256,1024]{3,2,1,0:T(8,128)(2,1)}, u32[]{:S(2)}, u32[]{:S(2)}) collective-permute-start(bf16[2,2,256,1024]{3,2,1,0:T(8,128)(2,1)} %shard_map.309), channel_id=1, source_target_pairs={{0,2},{2,0},{4,6},{6,4},{8,10},{10,8},{12,14},{14,12},{16,18},{18,... | collective-permute-start | bytes 6291464 | tf_op jit(solution)/shard_map/ppermute | solution.py:450
  441.0 21.8 %collective-permute-start.29 = (bf16[64,2816]{1,0:T(8,128)(2,1)S(1)}, bf16[64,2816]{1,0:T(8,128)(2,1)S(1)}, u32[]{:S(2)}, u32[]{:S(2)}) collective-permute-start(bf16[64,2816]{1,0:T(8,128)(2,1)S(1)} %dynamic-slice_bitcast_fusion), channel_id=1, source_target_pairs={{0,16},{2,18},{4,20},{6,22},{8,24},{10,26},{12,28},{14,30},{16,0},... | collective-permute-start | bytes 1081352 | tf_op jit(solution)/shard_map/ppermute | solution.py:450
  462.8 34.2 %collective-permute-start.30 = (bf16[2,256,1024]{2,1,0:T(8,128)(2,1)}, bf16[2,256,1024]{2,1,0:T(8,128)(2,1)S(1)}, u32[]{:S(2)}, u32[]{:S(2)}) collective-permute-start(bf16[2,256,1024]{2,1,0:T(8,128)(2,1)} %get-tuple-element.353), channel_id=1, source_target_pairs={{0,4},{2,6},{4,0},{6,2},{8,12},{10,14},{12,8},{14,10},{16,20},{18,... | collective-permute-start | bytes 3145736 | tf_op jit(solution)/shard_map/ppermute | solution.py:450
  463.5 33.5 %collective-permute-start.31 = (bf16[2,256,1024]{2,1,0:T(8,128)(2,1)}, bf16[2,256,1024]{2,1,0:T(8,128)(2,1)}, u32[]{:S(2)}, u32[]{:S(2)}) collective-permute-start(bf16[2,256,1024]{2,1,0:T(8,128)(2,1)} %get-tuple-element.355), channel_id=1, source_target_pairs={{0,1},{1,0},{2,3},{3,2},{4,5},{5,4},{6,7},{7,6},{8,9},{9,8},{10,11... | collective-permute-start | bytes 3145736 | tf_op jit(solution)/shard_map/ppermute | solution.py:449
  465.5 24.3 %collective-permute-start.36 = (f32[214,128]{1,0:T(8,128)S(1)}, f32[214,128]{1,0:T(8,128)S(1)}, u32[]{:S(2)}, u32[]{:S(2)}) collective-permute-start(f32[214,128]{1,0:T(8,128)S(1)} %concatenate.247), channel_id=1, source_target_pairs={{0,1},{1,0},{2,3},{3,2},{4,5},{5,4},{6,7},{7,6},{8,9},{9,8},{10,11... | collective-permute-start | bytes 328712 | tf_op jit(solution)/shard_map/ppermute | solution.py:449
  (63 other events, 637.6 us)
Sparse Core Ops, SparseCore 0:
  10.9 159.0 all-gather.1

commit v5 on v4

--- a/solution.py
+++ b/solution.py
@@ -18,6 +18,7 @@
 ALL = ("tensor", "dp")
 VMEM_BYTES = 56 * 1024 * 1024
 TILE = 256
+WIDE = 512
 
 
 def nn(a, b):
@@ -264,12 +265,14 @@
     return jnp.concatenate([ref[p] for ref in w_refs], axis=1)
 
 
-def middle_kernel(mixed_ref, w0, w1, w2, w3, hidden_ref, gain_ref, middle_ref, normed_ref):
+def middle_kernel(mixed_ref, w0, w1, w2, w3, hidden_ref, gain_ref, middle_ref, normed_ref, cols_ref):
     middle = hidden_ref[...].astype(F32)
     for p in range(2):
         middle += nt(mixed_ref[:, p * 512 : (p + 1) * 512], output_rows((w0, w1, w2, w3), p))
     middle_ref[...] = middle
-    normed_ref[...] = (rms_rows(middle)[0] * gain_ref[...]).astype(BF16)
+    normed = (rms_rows(middle)[0] * gain_ref[...]).astype(BF16)
+    normed_ref[...] = normed
+    cols_ref[...] = normed.T
 
 
 def ff_kernel(normed_ref, wg_ref, wu_ref, gate_ref, up_ref, first_ref, second_ref):
@@ -291,32 +294,49 @@
     dup_ref[0] = (d_activ * (gate * sig)).astype(BF16)
 
 
-def feed_kernel(first_ref, second_ref, wd_ref, middle_ref, out_ref):
-    total = middle_ref[...]
+def feed_kernel(first_ref, second_ref, wd_ref, middle_ref, out_ref, total):
+    p, m = pl.program_id(0), pl.program_id(1)
     cut = first_ref.shape[-1]
-    for p in range(2):
-        total += nt(first_ref[p], wd_ref[p, :, :cut]) + nt(second_ref[p], wd_ref[p, :, cut:])
-    out_ref[...] = total.astype(BF16)
+    part = nt(first_ref[0], wd_ref[0, :, :cut]) + nt(second_ref[0], wd_ref[0, :, cut:])
+
+    @pl.when(p == 0)
+    def _():
+        total[m] = part
+
+    @pl.when(p == 1)
+    def _():
+        out_ref[...] = (middle_ref[...] + total[m] + part).astype(BF16)
 
 
 def middle_back_kernel(
     dgate_ref, dup_ref, wg_ref, wu_ref, w0, w1, w2, w3, middle_ref, dout_ref, gain_ref,
-    dmiddle_ref, dmix_ref, dmixed_ref, dgain_ref,
+    dmiddle_ref, dmix_ref, cols_ref, dmixed_ref, dgain_ref, total,
 ):
-    @pl.when(pl.program_id(0) == 0)
+    p, m = pl.program_id(0), pl.program_id(1)
+    part = nt(dgate_ref[0], wg_ref[0]) + nt(dup_ref[0], wu_ref[0])
+
+    @pl.when((p == 0) & (m == 0))
     def _():
         dgain_ref[...] = jnp.zeros_like(dgain_ref)
 
-    grad = nt(dgate_ref[0], wg_ref[0]) + nt(dup_ref[0], wu_ref[0])
-    grad += nt(dgate_ref[1], wg_ref[1]) + nt(dup_ref[1], wu_ref[1])
-    normed, scale = rms_rows(middle_ref[...])
-    dgain_ref[...] += jnp.sum(grad * normed, axis=0, keepdims=True)
-    dmiddle = dout_ref[...].astype(F32) + rms_rows_back(normed, scale, gain_ref[...], grad)
-    dmiddle_ref[...] = dmiddle
-    dmix = dmiddle.astype(BF16)
-    dmix_ref[...] = dmix
-    for p in range(2):
-        dmixed_ref[:, p * 512 : (p + 1) * 512] = nn(dmix, output_rows((w0, w1, w2, w3), p)).astype(BF16)
+    @pl.when(p == 0)
+    def _():
+        total[m] = part
+
+    @pl.when(p == 1)
+    def _():
+        grad = total[m] + part
+        normed, scale = rms_rows(middle_ref[...])
+        dgain_ref[...] += jnp.sum(grad * normed, axis=0, keepdims=True)
+        dmiddle = dout_ref[...].astype(F32) + rms_rows_back(normed, scale, gain_ref[...], grad)
+        dmiddle_ref[...] = dmiddle
+        dmix = dmiddle.astype(BF16)
+        dmix_ref[...] = dmix
+        cols_ref[...] = dmix.T
+        for q in range(2):
+            dmixed_ref[:, q * 512 : (q + 1) * 512] = nn(
+                dmix, output_rows((w0, w1, w2, w3), q)
+            ).astype(BF16)
 
 
 def input_back_kernel(
@@ -336,35 +356,62 @@
     out_ref[...] = (dmiddle_ref[...] + back).astype(BF16)
 
 
-def grad_other_kernel(pairs, bits, *refs):
-    out = refs[-1]
+def grad_other_kernel(counts, bits, *refs):
+    outs = refs[2 * sum(counts) :]
     rows = refs[0].shape[1] * refs[0].shape[2]
+    i = 0
+    for count, out in zip(counts, outs):
+        at = 0
+        for _ in range(count):
+            left, right = refs[2 * i], refs[2 * i + 1]
+            cols = right.shape[-1]
+            result = nn(left[0].reshape(rows, left.shape[-1]), right[0]).astype(BF16)
+            out[0, :, :, at : at + cols] = result.reshape(out.shape[1], out.shape[2], cols)
+            at += cols
+            i += 1
+
+
+def grad_mine_kernel(counts, bits, *refs):
+    got_a, got_b, send_a, keep_a, send_b, keep_b = refs[2 * sum(counts) :]
+    own = send_a.shape[1]
+    step, x = pl.program_id(0), bits[1]
     at = 0
-    for i in range(pairs):
-        left, right = refs[2 * i], refs[2 * i + 1]
-        cols = right.shape[-1]
-        result = nn(left[0].reshape(rows, left.shape[-1]), right[0]).astype(BF16)
-        out[0, :, :, at : at + cols] = result.reshape(out.shape[1], out.shape[2], cols)
-        at += cols
-
-
-def grad_mine_kernel(pairs, bits, *refs):
-    got, send, keep = refs[2 * pairs :]
-    first = pl.program_id(0) == 0
-    at = 0
-    for i in range(pairs):
+    for i in range(counts[0]):
         left, right = refs[2 * i], refs[2 * i + 1]
         cols = slice(at, at + right.shape[-1])
         at += right.shape[-1]
-        result = (nn(left[0, 0], right[0]) + got[0, 0, :, cols].astype(F32)).astype(BF16)
-
-        @pl.when(first)
-        def _(result=result, cols=cols):
-            send[0, :, cols] = result
-
-        @pl.when(jnp.logical_not(first))
-        def _(result=result, cols=cols):
-            keep[0, :, cols] = result
+        result = nn(left[0].reshape(2 * own, left.shape[-1]), right[0])
+        low = (result[:own] + got_a[0, 0, :, cols].astype(F32)).astype(BF16)
+        high = (result[own:] + got_a[0, 1, :, cols].astype(F32)).astype(BF16)
+
+        @pl.when(x == 0)
+        def _(low=low, high=high, cols=cols):
+            send_a[0, :, cols] = high
+            keep_a[0, :, cols] = low
+
+        @pl.when(x == 1)
+        def _(low=low, high=high, cols=cols):
+            send_a[0, :, cols] = low
+            keep_a[0, :, cols] = high
+
+    at = 0
+    for i in range(counts[0], sum(counts)):
+        left, right = refs[2 * i], refs[2 * i + 1]
+        cols = slice(at, at + right.shape[-1])
+        at += right.shape[-1]
+        result = nn(left[0].reshape(2 * own, left.shape[-1]), right[0])
+        low = (result[:own] + got_b[0, 0, :, cols].astype(F32)).astype(BF16)
+        high = (result[own:] + got_b[0, 1, :, cols].astype(F32)).astype(BF16)
+
+        @pl.when(step == 0)
+        def _(low=low, high=high, cols=cols):
+            send_b[0, :, cols] = low
+            send_b[1, :, cols] = high
+
+        @pl.when(step == 1)
+        def _(low=low, high=high, cols=cols):
+            keep_b[0, :, cols] = low
+            keep_b[1, :, cols] = high
 
 
 def add(x, y):
@@ -478,13 +525,42 @@
     return shard.transpose(order).reshape(2, -1, shard.shape[-1])
 
 
-def owner_rows(act):
-    rows = act.shape[0]
+def owner_rows(cols):
+    count, rows = cols.shape
     z = len(long_strides())
-    own = act.shape[1] // lax.axis_size("dp")
-    split = act.reshape((rows,) + (2,) * (z + 2) + (own,))
-    split = split.transpose([z + 2, z + 1] + list(range(1, z + 1))[::-1] + [z + 3, 0])
+    own = count // lax.axis_size("dp")
+    split = cols.reshape((2,) * (z + 2) + (own, rows))
+    split = split.transpose([z + 1, z] + list(range(z))[::-1] + [z + 2, z + 3])
     return split.reshape(2, 2, -1, rows)
+
+
+class HopSum:
+    def __init__(self, x):
+        self.x, self.strides = x, [0, 1, 2] + long_strides()
+
+    def sends(self):
+        return [(self.x, self.strides[0])] if self.strides else []
+
+    def receive(self, got):
+        if self.strides:
+            self.x = self.x + got[0]
+            self.strides = self.strides[1:]
+
+    def finish(self):
+        while self.strides:
+            self.receive([swap(array, stride) for array, stride in self.sends()])
+        return self.x
+
+
+def in_flight(movers, work, *inputs, also=()):
+    sends = [mover.sends() for mover in movers]
+    flat = [pair for group in sends for pair in group] + list(also)
+    result, got = during(flat, work, *inputs)
+    at = 0
+    for mover, group in zip(movers, sends):
+        mover.receive(got[at : at + len(group)])
+        at += len(group)
+    return result, got[at:]
 
 
 def fence(*values):
@@ -497,57 +573,55 @@
     return fence(work(*inputs), got)
 
 
-def grad_other(bits, pairs):
-    own, rows = pairs[0][0].shape[2:]
-    cols = sum(right.shape[-1] for _, right in pairs)
-    in_specs = []
-    for _, right in pairs:
-        in_specs.append(pl.BlockSpec((1, 2, own, rows), lambda p, b: (1 - b[0], 0, 0, 0)))
-        in_specs.append(pl.BlockSpec((1, rows, right.shape[-1]), lambda p, b: (p, 0, 0)))
+def grad_other(bits, first, second):
+    own, rows = first[0][0].shape[2:]
+    in_specs, dims = [], []
+    for half in (first, second):
+        dims.append((2, 2, own, sum(right.shape[-1] for _, right in half)))
+        for _, right in half:
+            in_specs.append(pl.BlockSpec((1, 2, own, rows), lambda p, b: (1 - b[0], 0, 0, 0)))
+            in_specs.append(pl.BlockSpec((1, rows, right.shape[-1]), lambda p, b: (p, 0, 0)))
     return call(
-        functools.partial(grad_other_kernel, len(pairs)),
+        functools.partial(grad_other_kernel, (len(first), len(second))),
         2,
         in_specs,
-        pl.BlockSpec((1, 2, own, cols), lambda p, b: (p, 0, 0, 0)),
-        shape((2, 2, own, cols), BF16),
+        [pl.BlockSpec((1,) + d[1:], lambda p, b: (p, 0, 0, 0)) for d in dims],
+        [shape(d, BF16) for d in dims],
         [],
-        8 * own * rows * cols,
-    )(bits, *[array for pair in pairs for array in pair])
-
-
-def grad_mine(bits, pairs, got, by_x):
-    own, rows = pairs[0][0].shape[2:]
-    cols = got.shape[-1]
-
-    def x_of(s, j, b):
-        return b[1] ^ 1 ^ s if by_x else j
-
-    def p_of(s, j, b):
-        return j if by_x else b[2] ^ 1 ^ s
-
+        8 * own * rows * (dims[0][3] + dims[1][3]),
+    )(bits, *[array for half in (first, second) for pair in half for array in pair])
+
+
+def grad_mine(bits, first, second, got):
+    own, rows = first[0][0].shape[2:]
+    cols_a, cols_b = got[0].shape[-1], got[1].shape[-1]
+
+    def other_first(s, b):
+        return b[2] ^ 1 ^ s
+
+    left = pl.BlockSpec((1, 2, own, rows), lambda s, b: (b[0], 0, 0, 0))
     in_specs = []
-    for _, right in pairs:
-        in_specs.append(
-            pl.BlockSpec((1, 1, own, rows), lambda s, j, b: (b[0], x_of(s, j, b), 0, 0))
-        )
-        in_specs.append(
-            pl.BlockSpec((1, rows, right.shape[-1]), lambda s, j, b: (p_of(s, j, b), 0, 0))
-        )
-    in_specs.append(
-        pl.BlockSpec((1, 1, own, cols), lambda s, j, b: (p_of(s, j, b), x_of(s, j, b), 0, 0))
-    )
-    return call(
-        functools.partial(grad_mine_kernel, len(pairs)),
-        (2, 2),
+    for _, right in first:
+        in_specs += [left, pl.BlockSpec((1, rows, right.shape[-1]), lambda s, b: (s, 0, 0))]
+    for _, right in second:
+        in_specs += [
+            left,
+            pl.BlockSpec((1, rows, right.shape[-1]), lambda s, b: (other_first(s, b), 0, 0)),
+        ]
+    in_specs.append(pl.BlockSpec((1, 2, own, cols_a), lambda s, b: (s, 0, 0, 0)))
+    in_specs.append(pl.BlockSpec((1, 2, own, cols_b), lambda s, b: (other_first(s, b), 0, 0, 0)))
+    by_p = pl.BlockSpec((1, own, cols_a), lambda s, b: (s, 0, 0))
+    fixed = pl.BlockSpec((2, own, cols_b), lambda s, b: (0, 0, 0))
+    send_a, keep_a, send_b, keep_b = call(
+        functools.partial(grad_mine_kernel, (len(first), len(second))),
+        2,
         in_specs,
-        [
-            pl.BlockSpec((1, own, cols), lambda s, j, b: (jnp.where(s == 0, j, 1), 0, 0)),
-            pl.BlockSpec((1, own, cols), lambda s, j, b: (jnp.where(s == 0, 0, j), 0, 0)),
-        ],
-        [shape((2, own, cols), BF16)] * 2,
+        [by_p, by_p, fixed, fixed],
+        [shape((2, own, cols_a), BF16)] * 2 + [shape((2, own, cols_b), BF16)] * 2,
         [],
-        8 * own * rows * cols,
-    )(bits, *[array for pair in pairs for array in pair], got)
+        8 * own * rows * (cols_a + cols_b),
+    )(bits, *[array for half in (first, second) for pair in half for array in pair], *got)
+    return (send_a, keep_a), (send_b, keep_b)
 
 
 def whole(kernel, bits, arrays, outs):
@@ -570,6 +644,8 @@
         return self.out
 
     def receive(self, got):
+        if not self.out:
+            return
         strides = long_strides()
         if self.stage == 0:
             (ka, kb), (ga, gb) = self.keep, got
@@ -600,17 +676,8 @@
 
     def finish(self):
         while self.out:
-            self.receive([swap(array, stride) for array, stride in self.out])
+            in_flight([self], lambda: ())
         return self.keep[:, : self.cut], self.keep[:, self.cut :]
-
-
-def total_sum(x):
-    x = x + swap(x, 0)
-    stride = 1
-    while stride < lax.axis_size("dp"):
-        x = x + swap(x, stride)
-        stride *= 2
-    return x
 
 
 def local(
@@ -639,10 +706,12 @@
         jnp.concatenate([gate_weight, up_weight, down_weight.T, output_weight.T], axis=1)
     )
     dp_at = lax.axis_index("dp")
+    dout_rows = owner_rows(cotangent.T)
     bits = jnp.stack([dp_at % 2, (dp_at // 2) % 2, place, (dp_at // 4) % 2]).astype(jnp.int32)
 
     resid = hidden_in.astype(F32)
     normed_a = (rms(resid, 1e-6) * mixer_gain).astype(BF16)
+    normed_a_rows = owner_rows(normed_a.T)
     proj_a = jnp.einsum("td,pdc->ptc", normed_a, w_in_a, preferred_element_type=F32).astype(BF16)
     proj_v = jnp.einsum(
         "td,pdc->ptc", normed_a, w_in_b[..., :256], preferred_element_type=F32
@@ -681,34 +750,36 @@
         1 << 30,
     )(info, proj_a, proj_a, proj_a, proj_v, proj_og, proj_og, cum, seg, seg_row, state_in, gain)
 
-    tiles = rows // TILE
+    tiles, wides = rows // TILE, rows // WIDE
     cut = 768
     place_out = 3 * half // 128
 
-    def tile(cols):
-        return pl.BlockSpec((TILE, cols), lambda m: (m, 0))
-
-    def tile_pair(cols):
-        return pl.BlockSpec((2, TILE, cols), lambda m: (0, m, 0))
+    def tile(cols, size=TILE):
+        return pl.BlockSpec((size, cols), lambda m: (m, 0))
+
+    def tile_pair(cols, size=TILE):
+        return pl.BlockSpec((2, size, cols), lambda m: (0, m, 0))
 
     def keep(*dims, at=None):
-        return pl.BlockSpec(dims, lambda m: at or (0,) * len(dims))
+        return pl.BlockSpec(dims, lambda *_: at or (0,) * len(dims))
 
     def part(cols):
-        return pl.BlockSpec((1, TILE, cols), lambda p, m: (p, m, 0))
+        return pl.BlockSpec((1, WIDE, cols), lambda p, m: (p, m, 0))
 
     def part_weight(at):
         return pl.BlockSpec((1, width, half), lambda p, m: (p, 0, at))
 
-    part_rows = pl.BlockSpec((TILE, width), lambda p, m: (m, 0))
+    part_rows = pl.BlockSpec((WIDE, width), lambda p, m: (m, 0))
+    late_rows = pl.BlockSpec((WIDE, width), lambda p, m: (p * m, 0))
+    late_cols = pl.BlockSpec((width, WIDE), lambda p, m: (0, p * m))
     w_out = [keep(2, width, 128, at=(0, 0, place_out + i)) for i in range(4)]
     gain_b, gain_a = feed_gain.reshape(1, width), mixer_gain.reshape(1, width)
-    middle, normed_b = call(
+    middle, normed_b, normed_b_cols = call(
         middle_kernel,
         tiles,
         [tile(1024), *w_out, tile(width), keep(1, width)],
-        [tile(width), tile(width)],
-        [shape((rows, width), F32), shape((rows, width), BF16)],
+        [tile(width), tile(width), pl.BlockSpec((width, TILE), lambda m: (0, m))],
+        [shape((rows, width), F32), shape((rows, width), BF16), shape((width, rows), BF16)],
         [],
         2 * rows * width * 1024,
         0,
@@ -716,7 +787,7 @@
     wide = shape((2, rows, half), BF16)
     gate_pre, up_pre, activ_a, activ_b = call(
         ff_kernel,
-        (2, tiles),
+        (2, wides),
         [part_rows, part_weight(0), part_weight(1)],
         [part(half), part(half), part(cut), part(half - cut)],
         [wide, wide, shape((2, rows, cut), BF16), shape((2, rows, half - cut), BF16)],
@@ -728,7 +799,7 @@
     def ff_back(dout, weight, gate_pre, up_pre):
         return call(
             ff_back_kernel,
-            (2, tiles),
+            (2, wides),
             [part_rows, part_weight(2), part(half), part(half)],
             [part(half), part(half)],
             [wide, wide],
@@ -737,80 +808,62 @@
             0,
         )(dout, weight, gate_pre, up_pre)
 
-    dout_rows = owner_rows(cotangent)
-    sent = [grad_other(bits, [(dout_rows, activ)]) for activ in (activ_a, activ_b)]
-    (d_gate, d_up), got = during(
-        [(array, 1) for array in sent], ff_back, cotangent, w_rest, gate_pre, up_pre
-    )
-    down = Halving(
-        bits,
-        grad_mine(bits, [(dout_rows, activ_a)], got[0], True),
-        grad_mine(bits, [(dout_rows, activ_b)], got[1], False),
-    )
-
-    def feed_and_other(activ_a, activ_b, weight, middle, normed_rows, d_gate, d_up):
-        block_out = call(
-            feed_kernel,
-            tiles,
-            [tile_pair(cut), tile_pair(half - cut), keep(2, width, half, at=(0, 0, 2)), tile(width)],
-            tile(width),
-            shape((rows, width), BF16),
-            [],
-            4 * rows * width * half,
-            0,
-        )(activ_a, activ_b, weight, middle)
-        return block_out, [grad_other(bits, [(normed_rows, grad)]) for grad in (d_gate, d_up)]
-
-    normed_rows = owner_rows(normed_b)
-    (block_out, sent), got = during(
-        down.sends(), feed_and_other, activ_a, activ_b, w_rest, middle, normed_rows, d_gate, d_up
-    )
-    down.receive(got)
+    down_pairs = [(dout_rows, activ_a)], [(dout_rows, activ_b)]
+    sent = grad_other(bits, *down_pairs)
+    (d_gate, d_up), got = in_flight(
+        [], ff_back, cotangent, w_rest, gate_pre, up_pre, also=[(array, 1) for array in sent]
+    )
+    down = Halving(bits, *grad_mine(bits, *down_pairs, got))
+
+    def other_gate_up(normed_cols, d_gate, d_up):
+        normed_rows = owner_rows(normed_cols)
+        return normed_rows, grad_other(bits, [(normed_rows, d_gate)], [(normed_rows, d_up)])
+
+    (normed_rows, sent), _ = in_flight([down], other_gate_up, normed_b_cols, d_gate, d_up)
 
     def middle_back(d_gate, d_up, weight, middle, dout):
         return call(
             middle_back_kernel,
-            tiles,
-            [tile_pair(half), tile_pair(half), keep(2, width, half), keep(2, width, half, at=(0, 0, 1)),
-             *w_out, tile(width), tile(width), keep(1, width)],
-            [tile(width), tile(width), tile(1024), keep(1, width)],
-            [shape((rows, width), F32), shape((rows, width), BF16), shape((rows, 1024), BF16),
-             shape((1, width), F32)],
-            [],
+            (2, wides),
+            [part(half), part(half), part_weight(0), part_weight(1), *w_out, late_rows, late_rows,
+             keep(1, width)],
+            [late_rows, late_rows, late_cols, late_rows, keep(1, width)],
+            [shape((rows, width), F32), shape((rows, width), BF16), shape((width, rows), BF16),
+             shape((rows, 1024), BF16), shape((1, width), F32)],
+            [pltpu.VMEM((wides, WIDE, width), F32)],
             8 * rows * width * half,
             0,
         )(d_gate, d_up, weight, weight, weight, weight, weight, weight, middle, dout, gain_b)
 
-    (d_middle, d_mix, d_mixed, feed_gain_grad), got = during(
-        [(array, 1) for array in sent] + down.sends(), middle_back, d_gate, d_up, w_rest, middle, cotangent
-    )
-    down.receive(got[2:])
-
-    def mine_grads(normed_rows, d_gate, d_up, got_gate, got_up):
-        return (
-            grad_mine(bits, [(normed_rows, d_gate)], got_gate, True),
-            grad_mine(bits, [(normed_rows, d_up)], got_up, False),
-        )
-
-    (first, second), got = during(down.sends(), mine_grads, normed_rows, d_gate, d_up, *got[:2])
-    down.receive(got)
-    gate_up = Halving(bits, first, second)
-
+    (d_middle, d_mix, d_mix_cols, d_mixed, feed_gain_grad), got = in_flight(
+        [down], middle_back, d_gate, d_up, w_rest, middle, cotangent,
+        also=[(array, 1) for array in sent],
+    )
+
+    d_core, d_og, head_gain_grad, d_state = call(
+        post_kernel,
+        blocks,
+        [r_spec(1024), r_spec(1024), p_spec(256, 0), p_spec(256, 1), p_spec(256, 0), r_spec(512),
+         r_spec(1), f_spec(1, VAL)],
+        [r_spec(1024), p_spec(512, 0), f_spec(1, VAL), f_spec(HEADS, KEY, VAL)],
+        [shape((rows, 1024), BF16), shape((2, rows, 512), BF16), shape((1, VAL), F32), state_f32],
+        [pltpu.VMEM((1, 512), F32)],
+        1 << 29,
+    )(info, d_mixed, core, proj_og, proj_og, proj_a, cum, seg, gain)
+
+    def mine_gate_up(normed_rows, d_gate, d_up, d_mix_cols, *got):
+        mix_rows = owner_rows(d_mix_cols)
+        return mix_rows, grad_mine(bits, [(normed_rows, d_gate)], [(normed_rows, d_up)], got)
+
+    (mix_rows, halves), (d_state_in,) = in_flight(
+        [down], mine_gate_up, normed_rows, d_gate, d_up, d_mix_cols, *got,
+        also=[(d_state.astype(BF16), 0)],
+    )
+    gate_up = Halving(bits, *halves)
+    d_state_in = jnp.where(place == 1, jnp.zeros_like(d_state_in), d_state_in)
     p_back, r_back, f_back, row_back, s_back = specs(blocks, True)
 
-    def mixer_back(d_mixed):
-        d_core, d_og, head_gain_grad, d_state = call(
-            post_kernel,
-            blocks,
-            [r_spec(1024), r_spec(1024), p_spec(256, 0), p_spec(256, 1), p_spec(256, 0), r_spec(512),
-             r_spec(1), f_spec(1, VAL)],
-            [r_spec(1024), p_spec(512, 0), f_spec(1, VAL), f_spec(HEADS, KEY, VAL)],
-            [shape((rows, 1024), BF16), shape((2, rows, 512), BF16), shape((1, VAL), F32), state_f32],
-            [pltpu.VMEM((1, 512), F32)],
-            1 << 29,
-        )(info, d_mixed, core, proj_og, proj_og, proj_a, cum, seg, gain)
-        mix_rows, (d_state_in,) = during([(d_state.astype(BF16), 0)], owner_rows, d_mix)
-        d_state_in = jnp.where(place == 1, jnp.zeros_like(d_state_in), d_state_in)
+    def mixer_back(d_core, d_og, d_state_in, normed_rows, mix_rows, mixed_a, mixed_b):
         d_a, d_b, d_rank, low_second_grad, bias_grad = call(
             back_kernel,
             blocks,
@@ -824,64 +877,73 @@
             3 << 30,
         )(info, proj_a, proj_a, proj_a, proj_v, d_og, cum, sig, states, d_core, seg, seg_row,
           d_state_in, low_second, lowrank)
-        return mix_rows, head_gain_grad, d_a, d_b, d_rank, low_second_grad, bias_grad
-
-    (mix_rows, head_gain_grad, d_a, d_b, d_rank, low_second_grad, bias_grad), got = during(
-        gate_up.sends() + down.sends(), mixer_back, d_mixed
-    )
-    gate_up.receive(got[:2])
-    down.receive(got[2:])
+        sent = grad_other(
+            bits, [(normed_rows, d_a), (mix_rows, mixed_a)], [(normed_rows, d_b), (mix_rows, mixed_b)]
+        )
+        low_first_grad = tn(normed_a, d_rank.astype(BF16))
+        return d_a, d_b, d_rank, low_first_grad, low_second_grad, bias_grad, sent
+
+    (d_a, d_b, d_rank, low_first_grad, low_second_grad, bias_grad, sent), _ = in_flight(
+        [gate_up, down], mixer_back, d_core, d_og, d_state_in, normed_a_rows, mix_rows, mixed_a, mixed_b
+    )
     own_down = down.finish()
-
-    def other_mix(normed_rows, mix_rows, d_a, d_b, mixed_a, mixed_b):
-        return (
-            grad_other(bits, [(normed_rows, d_a), (mix_rows, mixed_a)]),
-            grad_other(bits, [(normed_rows, d_b), (mix_rows, mixed_b)]),
-        )
-
-    def mine_mix(normed_rows, mix_rows, d_a, d_b, mixed_a, mixed_b, got_a, got_b):
-        return (
-            grad_mine(bits, [(normed_rows, d_a), (mix_rows, mixed_a)], got_a, True),
-            grad_mine(bits, [(normed_rows, d_b), (mix_rows, mixed_b)], got_b, False),
-        )
-
-    mix_operands = (owner_rows(normed_a), mix_rows, d_a, d_b, mixed_a, mixed_b)
-    sent, got = during(gate_up.sends(), other_mix, *mix_operands)
-    gate_up.receive(got)
+    parts = (feed_gain_grad, low_first_grad, low_second_grad, bias_grad, head_gain_grad)
+    small_sum = HopSum(jnp.concatenate([part.reshape(-1, 128) for part in parts]))
 
     def input_back(d_a, d_b, w_a, w_b, d_rank, d_middle):
-        low_first_grad = tn(normed_a, d_rank.astype(BF16))
-        input_grad, mixer_gain_grad = call(
+        return call(
             input_back_kernel,
-            tiles,
-            [tile_pair(768), tile_pair(768), keep(2, width, 768), keep(2, width, 768), tile(16),
-             keep(width, 16), tile(width), tile(width), keep(1, width)],
-            [tile(width), keep(1, width)],
+            wides,
+            [tile_pair(768, WIDE), tile_pair(768, WIDE), keep(2, width, 768), keep(2, width, 768),
+             tile(16, WIDE), keep(width, 16), tile(width, WIDE), tile(width, WIDE), keep(1, width)],
+            [tile(width, WIDE), keep(1, width)],
             [shape((rows, width), BF16), shape((1, width), F32)],
             [],
             4 * rows * width * 1536,
             0,
         )(d_a, d_b, w_a, w_b, d_rank, low_first, hidden_in, d_middle, gain_a)
-        return input_grad, mixer_gain_grad, low_first_grad
-
-    (input_grad, mixer_gain_grad, low_first_grad), got = during(
-        [(array, 1) for array in sent] + gate_up.sends(),
-        input_back, d_a, d_b, w_in_a, w_in_b, d_rank, d_middle,
-    )
-    gate_up.receive(got[2:])
-    (first, second), got = during(gate_up.sends(), mine_mix, *mix_operands, *got[:2])
-    gate_up.receive(got)
-    mix = Halving(bits, first, second)
+
+    (input_grad, mixer_gain_grad), got = in_flight(
+        [gate_up, small_sum], input_back, d_a, d_b, w_in_a, w_in_b, d_rank, d_middle,
+        also=[(array, 1) for array in sent],
+    )
+    gain_sum = HopSum(mixer_gain_grad.reshape(-1, 128))
+
+    def mine_mix(normed_rows, mix_rows, d_a, d_b, mixed_a, mixed_b, *got):
+        return grad_mine(
+            bits, [(normed_rows, d_a), (mix_rows, mixed_a)],
+            [(normed_rows, d_b), (mix_rows, mixed_b)], got,
+        )
+
+    halves, _ = in_flight(
+        [gate_up, small_sum, gain_sum], mine_mix, normed_a_rows, mix_rows, d_a, d_b, mixed_a, mixed_b, *got
+    )
+    mix = Halving(bits, *halves)
+
+    def feed_out(activ_a, activ_b, weight, middle):
+        return call(
+            feed_kernel,
+            (2, wides),
+            [part(cut), part(half - cut), part_weight(2), late_rows],
+            late_rows,
+            shape((rows, width), BF16),
+            [pltpu.VMEM((wides, WIDE, width), F32)],
+            4 * rows * width * half,
+            0,
+        )(activ_a, activ_b, weight, middle)
+
+    block_out, _ = in_flight(
+        [mix, gate_up, small_sum, gain_sum], feed_out, activ_a, activ_b, w_rest, middle
+    )
+    while mix.out:
+        in_flight([mix, gate_up, small_sum, gain_sum], lambda: ())
     own_gate, own_up = gate_up.finish()
     own_a, own_b = mix.finish()
     own_out = [own_a[:, 768:], own_b[:, 768:]]
 
-    parts = (mixer_gain_grad, feed_gain_grad, low_first_grad, low_second_grad, bias_grad, head_gain_grad)
-    flat = total_sum(jnp.concatenate([part.reshape(-1, 128) for part in parts]))
-    small, spot = [], 0
-    for part, dims in zip(
-        parts, ((width,), (width,), low_first.shape, low_second.shape, (512,), (VAL,))
-    ):
+    flat = small_sum.finish()
+    small, spot = [gain_sum.finish().reshape(width)], 0
+    for part, dims in zip(parts, ((width,), low_first.shape, low_second.shape, (512,), (VAL,))):
         size = part.size // 128
         small.append(flat[spot : spot + size].reshape(dims))
         spot += size

time: 565 us -> 509 us (0.901)
  waiting for transfers between devices: 146 us -> 104 us
  local copies, waits for them, and re-layouts: 42 us -> 32.4 us
  Pallas kernels: 266 us -> 257 us
    ppermute x11 -> x12, waiting for transfers between devices: 56.7 us -> 33.2 us  [swap(): return lax.ppermute(x, 'tensor', [(0, 1), (1, 0)])]
    ppermute x30 -> x34, waiting for transfers between devices: 80.2 us -> 66.4 us  [swap(): lax.ppermute(x, 'dp', [(i, i ^ stride) for i in range(lax.axis_size('dp'))])]
    pallas_call x18 -> x12, Pallas kernels: 189 us -> 180 us  [the longest x3 45.2 us: grad_mine(): call(functools.partial(grad_mine_kernel, (len(first), len(second))), 2, i...]
    transpose x4 -> x2, local copies, waits for them, and re-layouts: 11.2 us -> 4.78 us  [owner_rows(): split = split.transpose([z + 1, z] + list(range(z))[::-1] + [z + 2, z + 3])]
    ppermute x30 -> x34, starting transfers between devices: 28.9 us -> 31.7 us  [swap(): lax.ppermute(x, 'dp', [(i, i ^ stride) for i in range(lax.axis_size('dp'))])]
    unnamed x94 -> x100, local copies, waits for them, and re-layouts: 14.3 us -> 16.6 us
    ppermute x11 -> x12, starting transfers between devices: 12.9 us -> 13.4 us  [swap(): return lax.ppermute(x, 'tensor', [(0, 1), (1, 0)])]
  transfers between devices with their start and end apart: 42 -> 47, of which waited for: 19 -> 16; matrix products, arithmetic and copies ran while one was open for 13% -> 12% of each run, Pallas kernels for 36% -> 35%
where the time goes in v5:
time: 509 us; the launch traced here: 499 us
  Pallas kernels  257 us (50%)
  waiting for transfers between devices  104 us (20%)
  starting transfers between devices  45.1 us (9%)
  local copies, waits for them, and re-layouts  32.4 us (6%)
  other arithmetic  29.4 us (6%)
  between operations  15.5 us (3%)
  matrix products  15.1 us (3%)
    ppermute x34, waiting for transfers between devices, swap(): lax.ppermute(x, 'dp', [(i, i ^ stride) for i in range(lax.axis_size('dp'))])  66.4 us
    pallas_call x3, Pallas kernels, grad_mine(): call(functools.partial(grad_mine_kernel, (len(first), len(second))), 2, i...  45.2 us
    ppermute x12, waiting for transfers between devices, swap(): return lax.ppermute(x, 'tensor', [(0, 1), (1, 0)])  33.2 us
    pallas_call x3, Pallas kernels, grad_other(): call(functools.partial(grad_other_kernel, (len(first), len(second))), 2,...  33.1 us
    ppermute x34, starting transfers between devices, swap(): lax.ppermute(x, 'dp', [(i, i ^ stride) for i in range(lax.axis_size('dp'))])  31.7 us
    pallas_call x1, Pallas kernels, middle_back(): call(middle_back_kernel, (2, wides), [part(half), part(half), part_weight...  26.5 us
    pallas_call x6, Pallas kernels, whole(): call(kernel, 1, [spec(a.shape) for a in arrays], [spec(dims) for dims in...  23.5 us
    pallas_call x1, Pallas kernels, mixer_back(): call(back_kernel, blocks, [p_back(256, 0), p_back(256, 1), p_back(256, 2)...  21.4 us
  transfers between devices with their start and end apart: 47, of which 16 were waited for; matrix products, arithmetic and copies ran while one was open for 12% of the time, Pallas kernels for 35%

profile of v5, /device:TPU:0, one launch (start us, length us, event | category | flops | bytes accessed | tf_op | source)
XLA Modules:
  0.0 499.0 jit_solution(14378746395356892278)
XLA Ops:
  25.1 13.2 %collective-permute-done.1 = bf16[2,64,768]{2,1,0:T(8,128)(2,1)S(1)} collective-permute-done((bf16[2,64,768]{2,1,0:T(8,128)(2,1)S(1)}, bf16[2,64,768]{2,1,0:T(8,128)(2,1)S(1)}, u32[]{:S(2)}, u32[]{:S(2)}) %collective-permute-start.1) | collective-permute-done | bytes 196640 | tf_op jit(solution)/shard_map/ppermute | solution.py:497
  48.7 8.8 %collective-permute-done.7 = bf16[2,2,64,768]{3,2,1,0:T(8,128)(2,1)S(1)} collective-permute-done((bf16[2,2,64,768]{3,2,1,0:T(8,128)(2,1)S(1)}, bf16[2,2,64,768]{3,2,1,0:T(8,128)(2,1)S(1)}, u32[]{:S(2)}, u32[]{:S(2)}) %collective-permute-start.7) | collective-permute-done | bytes 393248 | tf_op jit(solution)/shard_map/ppermute | solution.py:496
  60.8 16.4 %collective-permute-done.3 = bf16[2,2,2,64,768]{4,3,2,1,0:T(8,128)(2,1)S(1)} collective-permute-done((bf16[2,2,2,64,768]{4,3,2,1,0:T(8,128)(2,1)}, bf16[2,2,2,64,768]{4,3,2,1,0:T(8,128)(2,1)S(1)}, u32[]{:S(2)}, u32[]{:S(2)}) %collective-permute-start.3) | collective-permute-done | bytes 786464 | tf_op jit(solution)/shard_map/ppermute | solution.py:496
  78.8 7.1 %collective-permute-done.8 = bf16[2,2,2,64,768]{4,3,2,1,0:T(8,128)(2,1)} collective-permute-done((bf16[2,2,2,64,768]{4,3,2,1,0:T(8,128)(2,1)}, bf16[2,2,2,64,768]{4,3,2,1,0:T(8,128)(2,1)}, u32[]{:S(2)}, u32[]{:S(2)}) %collective-permute-start.8) | collective-permute-done | bytes 786464 | tf_op jit(solution)/shard_map/ppermute | solution.py:497
  120.1 11.4 %shard_map.288 = (f32[1024,512]{1,0:T(8,128)}, bf16[1024,512]{1,0:T(8,128)(2,1)}, f32[4,128,256]{2,1,0:T(8,128)}) custom-call(s32[2,8]{1,0:T(2,128)} %pad_add_fusion.info, f32[1024,16]{1,0:T(8,128)} %fusion.30.low_ref, f32[16,512]{1,0:T(8,128)} %second_ref.3, f32[1,512]{1,0:T(1,128)} %bitcast.251, ...), custom_call_target="tpu_custom_call" | custom-call | flops 536870912 | bytes 16777216 | tf_op jit(solution)/shard_map/pallas_call | solution.py:723
  143.8 12.7 %shard_map.289 = (bf16[1024,1024]{1,0:T(8,128)(2,1)}, bf16[2,1024,256]{2,1,0:T(8,128)(2,1)}, bf16[2,1024,256]{2,1,0:T(8,128)(2,1)}, bf16[1024,1024]{1,0:T(8,128)(2,1)}, bf16[8,4,128,256]{3,2,1,0:T(8,128)(2,1)}) custom-call(s32[2,8]{1,0:T(2,128)} %pad_add_fusion.info, bf16[2,1024,768]{2,1,0:T(8,128)(2,1)} %convert_bitcast_fusion.k_ref.v0_ref.q_ref, ...), custom_call_target="tpu_custom_call" | custom-call | flops 1073741824 | bytes 16777216 | tf_op jit(solution)/shard_map/pallas_call | solution.py:740
  161.3 8.2 %shard_map.290 = (f32[1024,1024]{1,0:T(8,128)}, bf16[1024,1024]{1,0:T(8,128)(2,1)}, bf16[1024,1024]{1,0:T(8,128)(2,1)}) custom-call(bf16[1024,1024]{1,0:T(8,128)(2,1)} %get-tuple-element.238.mixed_ref, bf16[2,1024,4736]{2,1,0:T(8,128)(2,1)} %bitcast.165, bf16[2,1024,4736]{2,1,0:T(8,128)(2,1)} %bitcast.166, bf16[2,1024,4736]{2,1,0:T(8,128)(2,1)} %bitcast.167, ...), custom_call_target="tpu_custom_call" | custom-call | flops 2147483648 | bytes 16777216 | tf_op jit(solution)/shard_map/pallas_call | solution.py:777
  169.5 19.8 %shard_map.291 = (bf16[2,1024,1408]{2,1,0:T(8,128)(2,1)}, bf16[2,1024,1408]{2,1,0:T(8,128)(2,1)}, bf16[2,1024,768]{2,1,0:T(8,128)(2,1)}, bf16[2,1024,640]{2,1,0:T(8,128)(2,1)}) custom-call(bf16[1024,1024]{1,0:T(8,128)(2,1)} %get-tuple-element.239.normed_ref, bf16[2,1024,4736]{2,1,0:T(8,128)(2,1)} %bitcast.169, bf16[2,1024,4736]{2,1,0:T(8,128)(2,1)} %bitcast.170), custom_call_target="tpu_custom_call" | custom-call | flops 11811160064 | bytes 16777216 | tf_op jit(solution)/shard_map/pallas_call | solution.py:788
  189.3 8.5 %shard_map.292 = (bf16[2,2,256,768]{3,2,1,0:T(8,128)(2,1)}, bf16[2,2,256,640]{3,2,1,0:T(8,128)(2,1)}) custom-call(s32[4]{0:T(128)} %pad_add_fusion.1.bits, bf16[2,2,256,1024]{3,2,1,0:T(8,128)(2,1)} %bitcast.188, bf16[2,1024,768]{2,1,0:T(8,128)(2,1)} %get-tuple-element.403.refs_1_.first_ref, bf16[2,2,256,1024]{3,2,1,0:T(8,128)(2,1)} %bitcast.189, ...), custom_call_target="tpu_custom_call" | custom-call | flops 2952790016 | bytes 16777216 | tf_op jit(solution)/shard_map/pallas_call | solution.py:584
  198.3 16.9 %shard_map.293 = (bf16[2,1024,1408]{2,1,0:T(8,128)(2,1)}, bf16[2,1024,1408]{2,1,0:T(8,128)(2,1)}) custom-call(bf16[1024,1024]{1,0:T(8,128)(2,1)} %dout_ref.1, bf16[2,1024,4736]{2,1,0:T(8,128)(2,1)} %bitcast.171, bf16[2,1024,1408]{2,1,0:T(8,128)(2,1)} %get-tuple-element.248.gate_ref, bf16[2,1024,1408]{2,1,0:T(8,128)(2,1)} %get-tuple-element.249.up_ref), custom_call_target="tpu_custom_call" | custom-call | flops 5905580032 | bytes 16777216 | tf_op jit(solution)/shard_map/pallas_call | solution.py:800
  216.8 11.5 %shard_map.294 = (bf16[2,256,768]{2,1,0:T(8,128)(2,1)}, bf16[2,256,768]{2,1,0:T(8,128)(2,1)}, bf16[2,256,640]{2,1,0:T(8,128)(2,1)}, bf16[2,256,640]{2,1,0:T(8,128)(2,1)}) custom-call(s32[4]{0:T(128)} %pad_add_fusion.1.bits, bf16[2,2,256,1024]{3,2,1,0:T(8,128)(2,1)} %bitcast.190, bf16[2,1024,768]{2,1,0:T(8,128)(2,1)} %get-tuple-element.403.refs_1_.first_ref, ...), custom_call_target="tpu_custom_call" | custom-call | flops 2952790016 | bytes 16777216 | tf_op jit(solution)/shard_map/pallas_call | solution.py:615
  232.0 13.5 %shard_map.295 = (bf16[2,2,256,1408]{3,2,1,0:T(8,128)(2,1)}, bf16[2,2,256,1408]{3,2,1,0:T(8,128)(2,1)}) custom-call(s32[4]{0:T(128)} %pad_add_fusion.1.bits, bf16[2,2,256,1024]{3,2,1,0:T(8,128)(2,1)} %bitcast.210, bf16[2,1024,1408]{2,1,0:T(8,128)(2,1)} %get-tuple-element.304.refs_1_.dgate_ref, bf16[2,2,256,1024]{3,2,1,0:T(8,128)(2,1)} %bitcast.211, ...), custom_call_target="tpu_custom_call" | custom-call | flops 5905580032 | bytes 16777216 | tf_op jit(solution)/shard_map/pallas_call | solution.py:584
  257.0 26.5 %shard_map.297 = (f32[1024,1024]{1,0:T(8,128)}, bf16[1024,1024]{1,0:T(8,128)(2,1)}, bf16[1024,1024]{1,0:T(8,128)(2,1)}, bf16[1024,1024]{1,0:T(8,128)(2,1)}, f32[1,1024]{1,0:T(1,128)}) custom-call(bf16[2,1024,1408]{2,1,0:T(8,128)(2,1)} %get-tuple-element.304.refs_1_.dgate_ref, bf16[2,1024,1408]{2,1,0:T(8,128)(2,1)} %get-tuple-element.305.refs_3_.dup_ref, ...), custom_call_target="tpu_custom_call" | custom-call | flops 11811160064 | bytes 16777216 | tf_op jit(solution)/shard_map/pallas_call | solution.py:825
  283.6 11.4 %shard_map.299 = (bf16[1024,1024]{1,0:T(8,128)(2,1)}, bf16[2,1024,512]{2,1,0:T(8,128)(2,1)}, f32[1,256]{1,0:T(1,128)}, f32[4,128,256]{2,1,0:T(8,128)}) custom-call(s32[2,8]{1,0:T(2,128)} %pad_add_fusion.info, bf16[1024,1024]{1,0:T(8,128)(2,1)} %get-tuple-element.295.dm_ref, bf16[1024,1024]{1,0:T(8,128)(2,1)} %get-tuple-element.296.core_ref, ...), custom_call_target="tpu_custom_call" | custom-call | flops 536870912 | bytes 16777216 | tf_op jit(solution)/shard_map/pallas_call | solution.py:843
  301.2 17.2 %shard_map.300 = (bf16[2,256,1408]{2,1,0:T(8,128)(2,1)}, bf16[2,256,1408]{2,1,0:T(8,128)(2,1)}, bf16[2,256,1408]{2,1,0:T(8,128)(2,1)}, bf16[2,256,1408]{2,1,0:T(8,128)(2,1)}) custom-call(s32[4]{0:T(128)} %pad_add_fusion.1.bits, bf16[2,2,256,1024]{3,2,1,0:T(8,128)(2,1)} %bitcast.212, bf16[2,1024,1408]{2,1,0:T(8,128)(2,1)} %get-tuple-element.304.refs_1_.dgate_ref, ...), custom_call_target="tpu_custom_call" | custom-call | flops 5905580032 | bytes 16777216 | tf_op jit(solution)/shard_map/pallas_call | solution.py:615
  324.1 21.4 %shard_map.301 = (bf16[2,1024,768]{2,1,0:T(8,128)(2,1)}, bf16[2,1024,768]{2,1,0:T(8,128)(2,1)}, f32[1024,16]{1,0:T(8,128)}, f32[16,512]{1,0:T(8,128)}, f32[1,512]{1,0:T(1,128)}) custom-call(s32[2,8]{1,0:T(2,128)} %pad_add_fusion.info, bf16[2,1024,768]{2,1,0:T(8,128)(2,1)} %convert_bitcast_fusion.k_ref.v0_ref.q_ref, ...), custom_call_target="tpu_custom_call" | custom-call | flops 3221225472 | bytes 16777216 | tf_op jit(solution)/shard_map/pallas_call | solution.py:867
  345.5 11.1 %shard_map.302 = (bf16[2,2,256,1024]{3,2,1,0:T(8,128)(2,1)}, bf16[2,2,256,1024]{3,2,1,0:T(8,128)(2,1)}) custom-call(s32[4]{0:T(128)} %pad_add_fusion.1.bits, bf16[2,2,256,1024]{3,2,1,0:T(8,128)(2,1)} %bitcast.179, bf16[2,1024,768]{2,1,0:T(8,128)(2,1)} %get-tuple-element.383.refs_1_.da_ref, bf16[2,2,256,1024]{3,2,1,0:T(8,128)(2,1)} %bitcast.183, ...), custom_call_target="tpu_custom_call" | custom-call | flops 4294967296 | bytes 16777216 | tf_op jit(solution)/shard_map/pallas_call | solution.py:584
  369.5 14.5 %shard_map.304 = (bf16[1024,1024]{1,0:T(8,128)(2,1)}, f32[1,1024]{1,0:T(1,128)}) custom-call(bf16[2,1024,768]{2,1,0:T(8,128)(2,1)} %get-tuple-element.383.refs_1_.da_ref, bf16[2,1024,768]{2,1,0:T(8,128)(2,1)} %get-tuple-element.386.refs_5_.db_ref, bf16[2,1024,768]{2,1,0:T(8,128)(2,1)} %bitcast.203, bf16[2,1024,768]{2,1,0:T(8,128)(2,1)} %bitcast.194, ...), custom_call_target="tpu_custom_call" | custom-call | flops 6442450944 | bytes 16777216 | tf_op jit(solution)/shard_map/pallas_call | solution.py:894
  392.7 16.5 %shard_map.306 = (bf16[2,256,1024]{2,1,0:T(8,128)(2,1)}, bf16[2,256,1024]{2,1,0:T(8,128)(2,1)}, bf16[2,256,1024]{2,1,0:T(8,128)(2,1)}, bf16[2,256,1024]{2,1,0:T(8,128)(2,1)}) custom-call(s32[4]{0:T(128)} %pad_add_fusion.1.bits, bf16[2,2,256,1024]{3,2,1,0:T(8,128)(2,1)} %bitcast.181, bf16[2,1024,768]{2,1,0:T(8,128)(2,1)} %get-tuple-element.383.refs_1_.da_ref, ...), custom_call_target="tpu_custom_call" | custom-call | flops 4294967296 | bytes 16777216 | tf_op jit(solution)/shard_map/pallas_call | solution.py:615
  414.6 12.3 %shard_map.307 = bf16[1024,1024]{1,0:T(8,128)(2,1)} custom-call(bf16[2,1024,768]{2,1,0:T(8,128)(2,1)} %get-tuple-element.403.refs_1_.first_ref, bf16[2,1024,640]{2,1,0:T(8,128)(2,1)} %get-tuple-element.404.refs_3_.second_ref, bf16[2,1024,4736]{2,1,0:T(8,128)(2,1)} %bitcast.178, f32[1024,1024]{1,0:T(8,128)} %get-tuple-element.406.middle_ref), custom_call_target="tpu_custom_call" | custom-call | flops 5905580032 | bytes 16777216 | tf_op jit(solution)/shard_map/pallas_call | solution.py:924
  426.9 10.2 %collective-permute-done.35 = f32[206,128]{1,0:T(8,128)S(1)} collective-permute-done((f32[206,128]{1,0:T(8,128)S(1)}, f32[206,128]{1,0:T(8,128)S(1)}, u32[]{:S(2)}, u32[]{:S(2)}) %collective-permute-start.35) | collective-permute-done | bytes 105504 | tf_op jit(solution)/shard_map/ppermute | solution.py:497
  447.5 9.6 %collective-permute-done.40 = f32[8,128]{1,0:T(8,128)S(1)} collective-permute-done((f32[8,128]{1,0:T(8,128)S(1)}, f32[8,128]{1,0:T(8,128)S(1)}, u32[]{:S(2)}, u32[]{:S(2)}) %collective-permute-start.40) | collective-permute-done | bytes 4128 | tf_op jit(solution)/shard_map/ppermute | solution.py:497
  465.9 9.8 %collective-permute-done.43 = f32[8,128]{1,0:T(8,128)S(1)} collective-permute-done((f32[8,128]{1,0:T(8,128)S(1)}, f32[8,128]{1,0:T(8,128)S(1)}, u32[]{:S(2)}, u32[]{:S(2)}) %collective-permute-start.43) | collective-permute-done | bytes 4128 | tf_op jit(solution)/shard_map/ppermute | solution.py:497
  481.7 6.7 %collective-permute-done.45 = f32[8,128]{1,0:T(8,128)S(1)} collective-permute-done((f32[8,128]{1,0:T(8,128)S(1)}, f32[8,128]{1,0:T(8,128)S(1)}, u32[]{:S(2)}, u32[]{:S(2)}) %collective-permute-start.45) | collective-permute-done | bytes 4128 | tf_op jit(solution)/shard_map/ppermute | solution.py:497
  (289 shorter events, 168.3 us)
Async XLA Ops:
  7.2 154.1 %all-gather.2.cloned.1.call-start = ((), (), s32[]{:S(2)}) async-start(), calls=%async_computation | async-start | bytes 20004864 | tf_op jit(solution)/shard_map/all_gather | solution.py:491
  24.1 19.3 %collective-permute-start.6 = (bf16[2,64,768]{2,1,0:T(8,128)(2,1)S(1)}, bf16[2,64,768]{2,1,0:T(8,128)(2,1)S(1)}, u32[]{:S(2)}, u32[]{:S(2)}) collective-permute-start(bf16[2,64,768]{2,1,0:T(8,128)(2,1)S(1)} %maximum_select_fusion.17), channel_id=1, source_target_pairs={{0,8},{2,10},{4,12},{6,14},{8,0},{10,2},{12,4},{14,6},{16,24},{18,... | collective-permute-start | bytes 589832 | tf_op jit(solution)/shard_map/ppermute | solution.py:497
  47.3 29.9 %collective-permute-start.3 = (bf16[2,2,2,64,768]{4,3,2,1,0:T(8,128)(2,1)}, bf16[2,2,2,64,768]{4,3,2,1,0:T(8,128)(2,1)S(1)}, u32[]{:S(2)}, u32[]{:S(2)}) collective-permute-start(bf16[2,2,2,64,768]{4,3,2,1,0:T(8,128)(2,1)} %maximum_select_fusion.7), channel_id=1, source_target_pairs={{0,1},{1,0},{2,3},{3,2},{4,5},{5,4},{6,7},{7,6},{8,9},{9,8},{10,11... | collective-permute-start | bytes 2359304 | tf_op jit(solution)/shard_map/ppermute | solution.py:496
  58.5 27.4 %collective-permute-start.8 = (bf16[2,2,2,64,768]{4,3,2,1,0:T(8,128)(2,1)}, bf16[2,2,2,64,768]{4,3,2,1,0:T(8,128)(2,1)}, u32[]{:S(2)}, u32[]{:S(2)}) collective-permute-start(bf16[2,2,2,64,768]{4,3,2,1,0:T(8,128)(2,1)} %maximum_select_fusion.9), channel_id=1, source_target_pairs={{0,4},{2,6},{4,0},{6,2},{8,12},{10,14},{12,8},{14,10},{16,20},{18,... | collective-permute-start | bytes 2359304 | tf_op jit(solution)/shard_map/ppermute | solution.py:497
  78.7 25.9 %collective-permute-start.4 = (bf16[2,2,2,2,64,768]{5,4,3,2,1,0:T(8,128)(2,1)}, bf16[2,2,2,2,64,768]{5,4,3,2,1,0:T(8,128)(2,1)}, u32[]{:S(2)}, u32[]{:S(2)}) collective-permute-start(bf16[2,2,2,2,64,768]{5,4,3,2,1,0:T(8,128)(2,1)} %maximum_select_fusion.3), channel_id=1, source_target_pairs={{0,2},{2,0},{4,6},{6,4},{8,10},{10,8},{12,14},{14,12},{16,18},{18,... | collective-permute-start | bytes 4718600 | tf_op jit(solution)/shard_map/ppermute | solution.py:497
  228.3 20.0 %collective-permute-start.13 = (bf16[2,256,768]{2,1,0:T(8,128)(2,1)}, bf16[2,256,768]{2,1,0:T(8,128)(2,1)S(1)}, u32[]{:S(2)}, u32[]{:S(2)}) collective-permute-start(bf16[2,256,768]{2,1,0:T(8,128)(2,1)} %get-tuple-element.267), channel_id=1, source_target_pairs={{0,4},{2,6},{4,0},{6,2},{8,12},{10,14},{12,8},{14,10},{16,20},{18,... | collective-permute-start | bytes 2359304 | tf_op jit(solution)/shard_map/ppermute | solution.py:497
  252.8 30.7 %collective-permute-start.17 = (bf16[2,2,256,1408]{3,2,1,0:T(8,128)(2,1)}, bf16[2,2,256,1408]{3,2,1,0:T(8,128)(2,1)}, u32[]{:S(2)}, u32[]{:S(2)}) collective-permute-start(bf16[2,2,256,1408]{3,2,1,0:T(8,128)(2,1)} %get-tuple-element.289), channel_id=1, source_target_pairs={{0,2},{2,0},{4,6},{6,4},{8,10},{10,8},{12,14},{14,12},{16,18},{18,... | collective-permute-start | bytes 8650760 | tf_op jit(solution)/shard_map/ppermute | solution.py:497
  252.8 30.7 %collective-permute-start.18 = (bf16[2,2,256,1408]{3,2,1,0:T(8,128)(2,1)}, bf16[2,2,256,1408]{3,2,1,0:T(8,128)(2,1)}, u32[]{:S(2)}, u32[]{:S(2)}) collective-permute-start(bf16[2,2,256,1408]{3,2,1,0:T(8,128)(2,1)} %get-tuple-element.290), channel_id=1, source_target_pairs={{0,2},{2,0},{4,6},{6,4},{8,10},{10,8},{12,14},{14,12},{16,18},{18,... | collective-permute-start | bytes 8650760 | tf_op jit(solution)/shard_map/ppermute | solution.py:497
  255.0 28.6 %collective-permute-start.15 = (bf16[256,768]{1,0:T(8,128)(2,1)S(1)}, bf16[256,768]{1,0:T(8,128)(2,1)S(1)}, u32[]{:S(2)}, u32[]{:S(2)}) collective-permute-start(bf16[256,768]{1,0:T(8,128)(2,1)S(1)} %copy-done.43), channel_id=1, source_target_pairs={{0,1},{1,0},{2,3},{3,2},{4,5},{5,4},{6,7},{7,6},{8,9},{9,8},{10,11... | collective-permute-start | bytes 1179656 | tf_op jit(solution)/shard_map/ppermute | solution.py:496
  256.5 27.1 %collective-permute-start.16 = (bf16[256,640]{1,0:T(8,128)(2,1)S(1)}, bf16[256,640]{1,0:T(8,128)(2,1)S(1)}, u32[]{:S(2)}, u32[]{:S(2)}) collective-permute-start(bf16[256,640]{1,0:T(8,128)(2,1)S(1)} %copy-done.45), channel_id=1, source_target_pairs={{0,4},{2,6},{4,0},{6,2},{8,12},{10,14},{12,8},{14,10},{16,20},{18,... | collective-permute-start | bytes 983048 | tf_op jit(solution)/shard_map/ppermute | solution.py:497
  299.1 20.9 %collective-permute-start.19 = (bf16[128,1408]{1,0:T(8,128)(2,1)}, bf16[128,1408]{1,0:T(8,128)(2,1)S(1)}, u32[]{:S(2)}, u32[]{:S(2)}) collective-permute-start(bf16[128,1408]{1,0:T(8,128)(2,1)} %get-tuple-element.312), channel_id=1, source_target_pairs={{0,8},{2,10},{4,12},{6,14},{8,0},{10,2},{12,4},{14,6},{16,24},{18,... | collective-permute-start | bytes 1081352 | tf_op jit(solution)/shard_map/ppermute | solution.py:497
  299.2 20.8 %collective-permute-start.20 = (bf16[4,128,256]{2,1,0:T(8,128)(2,1)S(1)}, bf16[4,128,256]{2,1,0:T(8,128)(2,1)S(1)}, u32[]{:S(2)}, u32[]{:S(2)}) collective-permute-start(bf16[4,128,256]{2,1,0:T(8,128)(2,1)S(1)} %convert_element_type.54), channel_id=1, source_target_pairs={{0,1},{1,0},{2,3},{3,2},{4,5},{5,4},{6,7},{7,6},{8,9},{9,8},{10,11... | collective-permute-start | bytes 786440 | tf_op jit(solution)/shard_map/ppermute | solution.py:496
  320.8 36.5 %collective-permute-start.21 = (bf16[2,256,1408]{2,1,0:T(8,128)(2,1)}, bf16[2,256,1408]{2,1,0:T(8,128)(2,1)S(1)}, u32[]{:S(2)}, u32[]{:S(2)}) collective-permute-start(bf16[2,256,1408]{2,1,0:T(8,128)(2,1)} %get-tuple-element.341), channel_id=1, source_target_pairs={{0,4},{2,6},{4,0},{6,2},{8,12},{10,14},{12,8},{14,10},{16,20},{18,... | collective-permute-start | bytes 4325384 | tf_op jit(solution)/shard_map/ppermute | solution.py:497
  321.7 35.7 %collective-permute-start.22 = (bf16[2,256,1408]{2,1,0:T(8,128)(2,1)}, bf16[2,256,1408]{2,1,0:T(8,128)(2,1)S(1)}, u32[]{:S(2)}, u32[]{:S(2)}) collective-permute-start(bf16[2,256,1408]{2,1,0:T(8,128)(2,1)} %get-tuple-element.342), channel_id=1, source_target_pairs={{0,1},{1,0},{2,3},{3,2},{4,5},{5,4},{6,7},{7,6},{8,9},{9,8},{10,11... | collective-permute-start | bytes 4325384 | tf_op jit(solution)/shard_map/ppermute | solution.py:496
  322.3 35.0 %collective-permute-start.23 = (bf16[64,1408]{1,0:T(8,128)(2,1)S(1)}, bf16[64,1408]{1,0:T(8,128)(2,1)S(1)}, u32[]{:S(2)}, u32[]{:S(2)}) collective-permute-start(bf16[64,1408]{1,0:T(8,128)(2,1)S(1)} %dynamic-slice_bitcast_fusion.2), channel_id=1, source_target_pairs={{0,16},{2,18},{4,20},{6,22},{8,24},{10,26},{12,28},{14,30},{16,0},... | collective-permute-start | bytes 540680 | tf_op jit(solution)/shard_map/ppermute | solution.py:497
  364.8 21.2 %collective-permute-start.27 = (bf16[2,2,256,1024]{3,2,1,0:T(8,128)(2,1)}, bf16[2,2,256,1024]{3,2,1,0:T(8,128)(2,1)S(1)}, u32[]{:S(2)}, u32[]{:S(2)}) collective-permute-start(bf16[2,2,256,1024]{3,2,1,0:T(8,128)(2,1)} %get-tuple-element.372), channel_id=1, source_target_pairs={{0,2},{2,0},{4,6},{6,4},{8,10},{10,8},{12,14},{14,12},{16,18},{18,... | collective-permute-start | bytes 6291464 | tf_op jit(solution)/shard_map/ppermute | solution.py:497
  364.9 21.1 %collective-permute-start.28 = (bf16[2,2,256,1024]{3,2,1,0:T(8,128)(2,1)}, bf16[2,2,256,1024]{3,2,1,0:T(8,128)(2,1)}, u32[]{:S(2)}, u32[]{:S(2)}) collective-permute-start(bf16[2,2,256,1024]{3,2,1,0:T(8,128)(2,1)} %get-tuple-element.373), channel_id=1, source_target_pairs={{0,2},{2,0},{4,6},{6,4},{8,10},{10,8},{12,14},{14,12},{16,18},{18,... | collective-permute-start | bytes 6291464 | tf_op jit(solution)/shard_map/ppermute | solution.py:497
  365.4 20.6 %collective-permute-start.24 = (bf16[256,1408]{1,0:T(8,128)(2,1)}, bf16[256,1408]{1,0:T(8,128)(2,1)S(1)}, u32[]{:S(2)}, u32[]{:S(2)}) collective-permute-start(bf16[256,1408]{1,0:T(8,128)(2,1)} %get-tuple-element.369), channel_id=1, source_target_pairs={{0,1},{1,0},{2,3},{3,2},{4,5},{5,4},{6,7},{7,6},{8,9},{9,8},{10,11... | collective-permute-start | bytes 2162696 | tf_op jit(solution)/shard_map/ppermute | solution.py:496
  366.7 19.3 %collective-permute-start.25 = (bf16[256,1408]{1,0:T(8,128)(2,1)}, bf16[256,1408]{1,0:T(8,128)(2,1)}, u32[]{:S(2)}, u32[]{:S(2)}) collective-permute-start(bf16[256,1408]{1,0:T(8,128)(2,1)} %get-tuple-element.370), channel_id=1, source_target_pairs={{0,4},{2,6},{4,0},{6,2},{8,12},{10,14},{12,8},{14,10},{16,20},{18,... | collective-permute-start | bytes 2162696 | tf_op jit(solution)/shard_map/ppermute | solution.py:497
  390.6 18.6 %collective-permute-start.29 = (bf16[128,2816]{1,0:T(8,128)(2,1)}, bf16[128,2816]{1,0:T(8,128)(2,1)S(1)}, u32[]{:S(2)}, u32[]{:S(2)}) collective-permute-start(bf16[128,2816]{1,0:T(8,128)(2,1)} %get-tuple-element.394), channel_id=1, source_target_pairs={{0,8},{2,10},{4,12},{6,14},{8,0},{10,2},{12,4},{14,6},{16,24},{18,... | collective-permute-start | bytes 2162696 | tf_op jit(solution)/shard_map/ppermute | solution.py:497
  409.5 27.7 %collective-permute-start.32 = (bf16[2,256,1024]{2,1,0:T(8,128)(2,1)}, bf16[2,256,1024]{2,1,0:T(8,128)(2,1)S(1)}, u32[]{:S(2)}, u32[]{:S(2)}) collective-permute-start(bf16[2,256,1024]{2,1,0:T(8,128)(2,1)} %get-tuple-element.407), channel_id=1, source_target_pairs={{0,4},{2,6},{4,0},{6,2},{8,12},{10,14},{12,8},{14,10},{16,20},{18,... | collective-permute-start | bytes 3145736 | tf_op jit(solution)/shard_map/ppermute | solution.py:497
  411.1 26.0 %collective-permute-start.33 = (bf16[2,256,1024]{2,1,0:T(8,128)(2,1)}, bf16[2,256,1024]{2,1,0:T(8,128)(2,1)}, u32[]{:S(2)}, u32[]{:S(2)}) collective-permute-start(bf16[2,256,1024]{2,1,0:T(8,128)(2,1)} %get-tuple-element.408), channel_id=1, source_target_pairs={{0,1},{1,0},{2,3},{3,2},{4,5},{5,4},{6,7},{7,6},{8,9},{9,8},{10,11... | collective-permute-start | bytes 3145736 | tf_op jit(solution)/shard_map/ppermute | solution.py:496
  411.7 25.5 %collective-permute-start.34 = (bf16[64,2816]{1,0:T(8,128)(2,1)S(1)}, bf16[64,2816]{1,0:T(8,128)(2,1)S(1)}, u32[]{:S(2)}, u32[]{:S(2)}) collective-permute-start(bf16[64,2816]{1,0:T(8,128)(2,1)S(1)} %dynamic-slice_bitcast_fusion), channel_id=1, source_target_pairs={{0,16},{2,18},{4,20},{6,22},{8,24},{10,26},{12,28},{14,30},{16,0},... | collective-permute-start | bytes 1081352 | tf_op jit(solution)/shard_map/ppermute | solution.py:497
  413.1 24.0 %collective-permute-start.35 = (f32[206,128]{1,0:T(8,128)S(1)}, f32[206,128]{1,0:T(8,128)S(1)}, u32[]{:S(2)}, u32[]{:S(2)}) collective-permute-start(f32[206,128]{1,0:T(8,128)S(1)} %add.134), channel_id=1, source_target_pairs={{0,4},{2,6},{4,0},{6,2},{8,12},{10,14},{12,8},{14,10},{16,20},{18,... | collective-permute-start | bytes 316424 | tf_op jit(solution)/shard_map/ppermute | solution.py:497
  (71 other events, 733.1 us)
Sparse Core Ops, SparseCore 0:
  10.9 150.3 all-gather.1
